TPU v7x, 256 devices: a whole 4x4x8 slice. The times are simulated.
256 devices in a mesh: row: 4 (over z_hi), col: 64 (over x, y, z_lo, core).
Axes of the slice: x: 4, y: 4, z: 8 (z_hi: 4, z_lo: 2; z = z_hi * 2 + z_lo), core: 2. Of those that a mesh axis runs over, the one named last changes fastest.
Arguments:
- object_field: float32 [2, 2048, 32768], P(None, 'row', 'col'), may hold values from -6 to 6
- probe_modes: float32 [2, 2, 128, 128], replicated, may hold values from -5 to 5
- photons: bfloat16 [4, 64, 64, 128, 128], P('row', 'col'), may hold values from 0.099609375 to 10
- positions: int32 [4, 64, 64, 2], P('row', 'col'), may hold values from 0 to 511, as said below
- counts: int32 [4, 64], P('row', 'col'), may hold values from 8 to 64, as said below
Outputs:
- object_gradient: float32 [2, 2048, 32768], P(None, 'row', 'col')
- probe_gradient: float32 [2, 2, 128, 128], replicated
Inputs may be any that keep to these rules, and one draw needn't show every extreme that they name: `positions`: each tile's offsets lie inside that tile; slots at or beyond the tile's count hold offsets that are ignored. `counts`: some tile has all 64 slots valid and some has 8; most tiles have few.
All inputs are finite; a program needn't handle non-finite values.
Results may differ from a plain program's by a relative error of at most 0.0012.
The roundings to bfloat16 on the way count: a program that leaves them out, or rounds other values in their place, can miss the bound.
Values sent between devices are 32-bit elements; how exact they have to be, the bound alone decides.
No kernel may reach another device: no remote copies, remote signals or barrier semaphores. Data moves between devices by JAX's collectives and lax.ppermute only.
A program may use at most 64 MiB of HBM per device.

v0:
```python
import functools
import math

import jax
import jax.numpy as jnp
import numpy as np
from jax import lax
from jax.experimental import pallas as pl
from jax.experimental.pallas import tpu as pltpu
from jax.sharding import Mesh
from jax.sharding import PartitionSpec as P

F32 = jnp.float32
BF16 = jnp.bfloat16
PATCH = 128
BLOCK = 8
VMEM_LIMIT = 63 * 2**20
ROW = "z_hi"
COL = ("x", "y", "z_lo", "core")
BOTH = (ROW,) + COL
PLANE = ("x", "y", "core")
DEPTH = ("z_hi", "z_lo")


def waves_of(patch_len):
    index_range = np.arange(patch_len)
    product = (index_range[:, None] * index_range[None, :]) % patch_len
    angle = product.astype(np.float32) * np.float32(2.0 * math.pi / patch_len)
    pair = np.stack([np.cos(angle), np.sin(angle)]) / np.float32(math.sqrt(patch_len))
    return jnp.asarray(pair, F32)


def dot(a, b):
    return jnp.dot(a, b, preferred_element_type=F32)


def slot_block(at, slots, valids, pos, row_base, field, grad, photons, probe, probe_sum, plus_ref, minus_ref):
    n = len(slots)
    lane = lax.broadcasted_iota(jnp.int32, (PATCH, PATCH), 1)
    plus = plus_ref[...]
    minus = minus_ref[...]
    places, patches, waves = [], [], []
    for s in slots:
        top = pos[0, s] - row_base
        left = pos[1, s]
        tile = left // PATCH
        shift = left % PATCH
        back = (PATCH - shift) % PATCH
        keep = lane >= shift
        patch = []
        for k in range(2):
            a = field[tile, k, pl.ds(top, PATCH), :]
            b = field[tile + 1, k, pl.ds(top, PATCH), :]
            patch.append(pltpu.roll(jnp.where(keep, a, b), back, 1))
        places.append((top, tile, shift, keep))
        patches.append(patch)
        for m in range(2):
            pr = probe[0, m]
            pi = probe[1, m]
            wr = (pr * patch[0] - pi * patch[1]).astype(BF16)
            wi = (pr * patch[1] + pi * patch[0]).astype(BF16)
            waves.append(jnp.concatenate([wr, wi], axis=0))
    first = dot(plus, jnp.concatenate(waves, axis=1)).astype(BF16)
    cols = [slice(q * PATCH, (q + 1) * PATCH) for q in range(2 * n)]
    turned = [jnp.concatenate([first[:PATCH, q], first[PATCH:, q]], axis=1) for q in cols]
    far = dot(jnp.concatenate(turned, axis=0), minus)
    scaled = []
    for i in range(n):
        f0 = far[2 * i * PATCH:(2 * i + 1) * PATCH]
        f1 = far[(2 * i + 1) * PATCH:(2 * i + 2) * PATCH]
        power = f0 * f0 + f1 * f1
        intensity = power[:, :PATCH] + power[:, PATCH:]
        factor = (1.0 - photons[at[i]].astype(F32) / (intensity + 1.0)) * valids[i]
        for f in (f0, f1):
            re = (f[:, :PATCH] * factor).astype(BF16)
            im = (f[:, PATCH:] * factor).astype(BF16)
            scaled.append(jnp.concatenate([re, im], axis=1))
    back_pass = dot(jnp.concatenate(scaled, axis=0), plus).astype(BF16)
    unturned = [jnp.concatenate([back_pass[q, :PATCH], back_pass[q, PATCH:]], axis=0) for q in cols]
    exit_grad = dot(minus, jnp.concatenate(unturned, axis=1))
    for m in range(2):
        sum_re = sum_im = None
        for i in range(n):
            er = exit_grad[:PATCH, cols[2 * i + m]]
            ei = exit_grad[PATCH:, cols[2 * i + m]]
            o_re, o_im = patches[i]
            t_re = o_re * er + o_im * ei
            t_im = o_re * ei - o_im * er
            sum_re = t_re if sum_re is None else sum_re + t_re
            sum_im = t_im if sum_im is None else sum_im + t_im
        probe_sum[0, m] += sum_re
        probe_sum[1, m] += sum_im
    for i in range(n):
        g_re = g_im = None
        for m in range(2):
            er = exit_grad[:PATCH, cols[2 * i + m]]
            ei = exit_grad[PATCH:, cols[2 * i + m]]
            pr = probe[0, m]
            pi = probe[1, m]
            t_re = pr * er + pi * ei
            t_im = pr * ei - pi * er
            g_re = t_re if g_re is None else g_re + t_re
            g_im = t_im if g_im is None else g_im + t_im
        top, tile, shift, keep = places[i]
        for k, g in ((0, g_re), (1, g_im)):
            g = pltpu.roll(g, shift, 1)
            grad[tile, k, pl.ds(top, PATCH), :] += jnp.where(keep, g, 0.0)
            grad[tile + 1, k, pl.ds(top, PATCH), :] += jnp.where(keep, 0.0, g)


def fill_tables(waves, plus_ref, minus_ref):
    c = waves[0].astype(BF16)
    s = waves[1].astype(BF16)
    plus_ref[:PATCH, :PATCH] = c
    plus_ref[:PATCH, PATCH:] = s
    plus_ref[PATCH:, :PATCH] = -s
    plus_ref[PATCH:, PATCH:] = c
    minus_ref[:PATCH, :PATCH] = c
    minus_ref[:PATCH, PATCH:] = -s
    minus_ref[PATCH:, :PATCH] = s
    minus_ref[PATCH:, PATCH:] = c


def list_slots(wanted, pos, count, listed, photons, photon_buf, photon_sems):
    def list_step(s, found):
        chosen = wanted(pos[0, s])

        @pl.when(chosen)
        def _():
            listed[found] = s
            pltpu.make_async_copy(photons.at[s], photon_buf.at[found], photon_sems.at[found]).start()

        return found + chosen.astype(jnp.int32)

    return lax.fori_loop(0, count, list_step, jnp.int32(0))


def run_slots(found, pos, row_base, listed, field, grad, photons, photon_buf, photon_sems, probe, probe_sum,
              plus_ref, minus_ref):
    def step(k, carry, first=0, width=BLOCK):
        places = [first + k * width + i for i in range(width)]
        at = [jnp.minimum(p, found - 1) for p in places]
        slots = [listed[a] for a in at]
        valids = [jnp.where(p < found, 1.0, 0.0).astype(F32) for p in places]
        for p, a, s in zip(places, at, slots):
            @pl.when(p < found)
            def _(a=a, s=s):
                pltpu.make_async_copy(photons.at[s], photon_buf.at[a], photon_sems.at[a]).wait()

        slot_block(at, slots, valids, pos, row_base, field, grad, photon_buf, probe, probe_sum, plus_ref, minus_ref)
        return carry

    rest = found % BLOCK
    small = (rest > 0) & (rest <= BLOCK // 2)
    blocks = found // BLOCK + ((rest > 0) & jnp.logical_not(small)).astype(jnp.int32)
    lax.fori_loop(0, blocks, step, 0)

    @pl.when(small)
    def _():
        step(0, 0, blocks * BLOCK, BLOCK // 2)


def copies_of(pairs, sems):
    return [pltpu.make_async_copy(a, b, sems.at[i]) for i, (a, b) in enumerate(pairs)]


def start_all(copies):
    for c in copies:
        c.start()


def wait_all(copies):
    for c in copies:
        c.wait()


def by_tiles(array, tiles):
    return [array.at[:, :, pl.ds(t * PATCH, PATCH)] for t in range(tiles)]


def right_rim_kernel(own, right, right_buf, sems):
    load = pltpu.make_async_copy(own.at[:, :, pl.ds(0, PATCH)], right_buf, sems.at[0])
    load.start()
    load.wait()
    store = pltpu.make_async_copy(right_buf, right, sems.at[0])
    store.start()
    store.wait()


def below_rim_kernel(own, after, below, corner, below_buf, sems):
    rim = pl.ds(0, PATCH)
    load = pltpu.make_async_copy(own.at[:, rim, :], below_buf, sems.at[0])
    load.start()
    load.wait()
    stores = copies_of([(below_buf, below), (below_buf.at[:, :, rim], corner)], sems)
    start_all(stores)
    wait_all(stores)


def upper_kernel(pos, count, own, right, photons, probe_in, waves_in, g_own, g_right, probe_out,
                 field, grad, photon_buf, probe, waves, plus_ref, minus_ref, probe_sum, listed, sems, photon_sems):
    rows, cols = own.shape[1], own.shape[2]
    tiles = cols // PATCH
    loads = copies_of(
        [(waves_in, waves), (probe_in, probe)]
        + [(a, field.at[t]) for t, a in enumerate(by_tiles(own, tiles))]
        + [(right, field.at[tiles])],
        sems,
    )
    start_all(loads)
    found = list_slots(lambda top: top <= rows - PATCH, pos, count[0], listed, photons, photon_buf, photon_sems)
    grad[...] = jnp.zeros(grad.shape, F32)
    probe_sum[...] = jnp.zeros(probe_sum.shape, F32)
    loads[0].wait()
    fill_tables(waves, plus_ref, minus_ref)
    wait_all(loads[1:])
    run_slots(found, pos, 0, listed, field, grad, photons, photon_buf, photon_sems, probe, probe_sum,
              plus_ref, minus_ref)
    stores = copies_of(
        [(probe_sum, probe_out)]
        + [(grad.at[t], a) for t, a in enumerate(by_tiles(g_own, tiles))]
        + [(grad.at[tiles], g_right)],
        sems,
    )
    start_all(stores)
    wait_all(stores)


def lower_kernel(scale, pos, count, own, right, below, corner, photons, probe_in, waves_in, own_in, right_in, sum_in,
                 g_own, g_right, g_below, probe_out,
                 field, grad, photon_buf, probe, waves, plus_ref, minus_ref, probe_sum, listed, sems, photon_sems):
    rows, cols = own.shape[1], own.shape[2]
    tiles = cols // PATCH
    base = rows - PATCH
    last, upper, lower = pl.ds(base, PATCH), pl.ds(0, PATCH), pl.ds(PATCH, PATCH)

    def last_rows(array):
        return [array.at[:, last, pl.ds(t * PATCH, PATCH)] for t in range(tiles)]

    loads = copies_of(
        [(waves_in, waves), (probe_in, probe), (sum_in, probe_sum)]
        + [(a, field.at[t, :, upper, :]) for t, a in enumerate(last_rows(own) + [right.at[:, last, :]])]
        + [(a, field.at[t, :, lower, :]) for t, a in enumerate(by_tiles(below, tiles) + [corner])]
        + [(a, grad.at[t, :, upper, :]) for t, a in enumerate(last_rows(own_in) + [right_in.at[:, last, :]])],
        sems,
    )
    start_all(loads)
    found = list_slots(lambda top: top > base, pos, count[0], listed, photons, photon_buf, photon_sems)
    for t in range(tiles + 1):
        grad[t, :, lower, :] = jnp.zeros((2, PATCH, PATCH), F32)
    loads[0].wait()
    fill_tables(waves, plus_ref, minus_ref)
    wait_all(loads[1:])
    run_slots(found, pos, base, listed, field, grad, photons, photon_buf, photon_sems, probe, probe_sum,
              plus_ref, minus_ref)
    probe_sum[...] = probe_sum[...] * scale
    stores = copies_of(
        [(probe_sum, probe_out)]
        + [(grad.at[t, :, lower, :], a) for t, a in enumerate(by_tiles(g_below, tiles + 1))]
        + [(grad.at[t, :, upper, :], a) for t, a in enumerate(last_rows(g_own) + [g_right.at[:, last, :]])],
        sems,
    )
    start_all(stores)
    wait_all(stores)


def corner_kernel(right_in, above, right, rim_buf, corner_buf, sems):
    rows = right.at[:, pl.ds(0, PATCH), :]
    corner = above.at[:, :, pl.ds(above.shape[2] - PATCH, PATCH)]
    loads = copies_of([(rows, rim_buf), (corner, corner_buf)], sems)
    start_all(loads)
    wait_all(loads)
    rim_buf[...] += corner_buf[...]
    store = pltpu.make_async_copy(rim_buf, rows, sems.at[0])
    store.start()
    store.wait()


def seam_kernel(grad_in, above, left, parts, grad, probe,
                top_buf, left_buf, above_buf, beside_buf, probe_buf, sems):
    rows, cols = grad.shape[1], grad.shape[2]
    rest = rows - PATCH
    top_rim = grad.at[:, pl.ds(0, PATCH), :]
    left_rim = grad.at[:, pl.ds(PATCH, rest), pl.ds(0, PATCH)]
    loads = copies_of(
        [(top_rim, top_buf), (left_rim, left_buf), (above.at[:, :, pl.ds(0, cols)], above_buf), (left, beside_buf),
         (parts, probe_buf)],
        sems,
    )
    start_all(loads)
    wait_all(loads)
    join = pltpu.make_async_copy(probe_buf, probe, sems.at[2])
    join.start()
    top_buf[:, :, PATCH:] += above_buf[:, :, PATCH:]
    top_buf[:, :, :PATCH] += above_buf[:, :, :PATCH] + beside_buf[:, :PATCH, :]
    left_buf[...] += beside_buf[:, PATCH:, :]
    stores = copies_of([(top_buf, top_rim), (left_buf, left_rim)], sems)
    start_all(stores)
    wait_all(stores)
    join.wait()


def shape(*dims):
    return jax.ShapeDtypeStruct(dims, F32)


def everyone(value, axes, count):
    sent = jnp.broadcast_to(value[None], (count,) + value.shape)
    return lax.all_to_all(sent, axes, 0, 0, tiled=True)


def body(object_field, probe_modes, photons, positions, counts):
    rows, cols = object_field.shape[1], object_field.shape[2]
    slot_count = photons.shape[2]
    tiles = cols // PATCH
    n_row, n_col = lax.axis_size(ROW), lax.axis_size(COL)
    pos = positions[0, 0].T
    count = counts[0]
    photon_rows = photons[0, 0]
    waves = waves_of(PATCH)
    scale = 1.0 / math.sqrt(n_row * n_col * slot_count)
    down = [(i, i + 1) for i in range(n_row - 1)]
    along = [(i, i + 1) for i in range(n_col - 1)]
    up, back = ([(j, i) for i, j in pairs] for pairs in (down, along))
    diagonal = [
        (a * n_col + b, (a + 1) * n_col + b + 1) for a in range(n_row - 1) for b in range(n_col - 1)
    ]
    diagonal_back = [(j, i) for i, j in diagonal]
    smem = pl.BlockSpec(memory_space=pltpu.SMEM)
    hbm = pl.BlockSpec(memory_space=pl.ANY)
    params = pltpu.CompilerParams(vmem_limit_bytes=VMEM_LIMIT)
    small = pltpu.CompilerParams(vmem_limit_bytes=8 * 2**20)

    right = pl.pallas_call(
        right_rim_kernel,
        out_shape=shape(2, rows, PATCH),
        in_specs=[hbm],
        out_specs=hbm,
        scratch_shapes=[pltpu.VMEM((2, rows, PATCH), F32), pltpu.SemaphoreType.DMA((1,))],
        compiler_params=params,
        name="right_rim",
    )(object_field)
    below, corner = pl.pallas_call(
        below_rim_kernel,
        out_shape=(shape(2, PATCH, cols), shape(2, PATCH, PATCH)),
        in_specs=[hbm, hbm],
        out_specs=(hbm,) * 2,
        scratch_shapes=[pltpu.VMEM((2, PATCH, cols), F32), pltpu.SemaphoreType.DMA((2,))],
        compiler_params=params,
        name="below_rim",
    )(object_field, right)
    below = lax.ppermute(below, ROW, up)
    right = lax.ppermute(right, COL, back)
    corner = lax.ppermute(corner, BOTH, diagonal_back)

    def scratch(height):
        return [
            pltpu.VMEM((tiles + 1, 2, height, PATCH), F32),
            pltpu.VMEM((tiles + 1, 2, height, PATCH), F32),
            pltpu.VMEM(photon_rows.shape, BF16),
            pltpu.VMEM(probe_modes.shape, F32),
            pltpu.VMEM(waves.shape, F32),
            pltpu.VMEM((2 * PATCH, 2 * PATCH), BF16),
            pltpu.VMEM((2 * PATCH, 2 * PATCH), BF16),
            pltpu.VMEM(probe_modes.shape, F32),
            pltpu.SMEM((slot_count,), jnp.int32),
            pltpu.SemaphoreType.DMA((3 * tiles + 6,)),
            pltpu.SemaphoreType.DMA((slot_count,)),
        ]

    own_shape, right_shape, probe_shape = shape(2, rows, cols), shape(2, rows, PATCH), shape(*probe_modes.shape)
    g_own, g_right, probe_1 = pl.pallas_call(
        upper_kernel,
        out_shape=(own_shape, right_shape, probe_shape),
        in_specs=[smem, smem] + [hbm] * 5,
        out_specs=(hbm,) * 3,
        scratch_shapes=scratch(rows),
        compiler_params=params,
        cost_estimate=pl.CostEstimate(flops=10**9, bytes_accessed=2**20, transcendentals=0),
        name="upper_slots",
    )(pos, count, object_field, right, photon_rows, probe_modes, waves)
    g_own, g_right, g_below, probe_2 = pl.pallas_call(
        functools.partial(lower_kernel, scale),
        out_shape=(own_shape, right_shape, shape(2, PATCH, cols + PATCH), probe_shape),
        in_specs=[smem] * 2 + [hbm] * 10,
        out_specs=(hbm,) * 4,
        scratch_shapes=scratch(2 * PATCH),
        input_output_aliases={9: 0, 10: 1},
        compiler_params=params,
        cost_estimate=pl.CostEstimate(flops=10**9, bytes_accessed=2**20, transcendentals=0),
        name="lower_slots",
    )(pos, count, object_field, right, below, corner, photon_rows, probe_modes, waves, g_own, g_right, probe_1)

    plane, depth = lax.axis_size(PLANE), lax.axis_size(DEPTH)
    above = lax.ppermute(g_below, ROW, down)
    shares = lax.all_to_all(probe_2.reshape(plane, -1, PATCH), PLANE, 0, 0, tiled=True)
    share = jnp.sum(shares, axis=0)
    share = jnp.sum(everyone(share, DEPTH, depth), axis=0)
    g_right = pl.pallas_call(
        corner_kernel,
        out_shape=right_shape,
        in_specs=[hbm, hbm],
        out_specs=hbm,
        scratch_shapes=[
            pltpu.VMEM((2, PATCH, PATCH), F32),
            pltpu.VMEM((2, PATCH, PATCH), F32),
            pltpu.SemaphoreType.DMA((2,)),
        ],
        input_output_aliases={0: 0},
        compiler_params=small,
        name="corner",
    )(g_right, above)
    share, g_right = lax.optimization_barrier((share, g_right))
    left = lax.ppermute(g_right, COL, along)
    parts = everyone(share, PLANE, plane)

    object_gradient, probe_gradient = pl.pallas_call(
        seam_kernel,
        out_shape=(own_shape, shape(*parts.shape)),
        in_specs=[hbm] * 4,
        out_specs=(hbm, hbm),
        scratch_shapes=[
            pltpu.VMEM((2, PATCH, cols), F32),
            pltpu.VMEM((2, rows - PATCH, PATCH), F32),
            pltpu.VMEM((2, PATCH, cols), F32),
            pltpu.VMEM((2, rows, PATCH), F32),
            pltpu.VMEM(parts.shape, F32),
            pltpu.SemaphoreType.DMA((5,)),
        ],
        input_output_aliases={0: 0},
        compiler_params=small,
        name="seams",
    )(g_own, above, left, parts)
    return (object_gradient, probe_gradient.reshape(probe_modes.shape))


def solution(mesh):
    fine = Mesh(mesh.devices.reshape(4, 4, 4, 2, 2), BOTH)
    in_specs = (
        P(None, ROW, COL),
        P(),
        P(ROW, COL, None, None, None),
        P(ROW, COL, None, None),
        P(ROW, COL),
    )
    out_specs = (P(None, ROW, COL), P())
    return jax.shard_map(body, mesh=fine, in_specs=in_specs, out_specs=out_specs, check_vma=False)
```

profile of v0, /device:TPU:1, one launch (start us, length us, event | category | flops | bytes accessed | tf_op | source)
XLA Modules:
  0.0 111.1 jit_solution(9940453148227583308)
XLA Ops:
  0.6 1.8 %right_rim.1.after = f32[2,512,128]{2,1,0:T(8,128)} custom-call(f32[2,512,512]{2,1,0:T(8,128)} %own.7), custom_call_target="tpu_custom_call" | custom-call | tf_op jit(solution)/shard_map/right_rim/pallas_call | solution.py:334
  2.5 5.1 %collective-permute-start = (f32[2,512,128]{2,1,0:T(8,128)}, f32[2,512,128]{2,1,0:T(8,128)S(1)}, u32[]{:S(2)}, u32[]{:S(2)}) collective-permute-start(f32[2,512,128]{2,1,0:T(8,128)} %right_rim.1.after), channel_id=1, source_target_pairs={{1,0},{2,1},{3,2},{4,3},{5,4},{6,5},{7,6},{8,7},{9,8},{10,9},{11,1... | collective-permute-start | bytes 1572872 | tf_op jit(solution)/shard_map/ppermute | solution.py:353
  7.6 1.9 %below_rim.1 = (f32[2,128,512]{2,1,0:T(8,128)}, f32[2,128,128]{2,1,0:T(8,128)}) custom-call(f32[2,512,512]{2,1,0:T(8,128)} %own.7, f32[2,512,128]{2,1,0:T(8,128)} %right_rim.1.after), custom_call_target="tpu_custom_call" | custom-call | tf_op jit(solution)/shard_map/below_rim/pallas_call | solution.py:343
  9.5 1.3 %collective-permute-start.1 = (f32[2,128,512]{2,1,0:T(8,128)}, f32[2,128,512]{2,1,0:T(8,128)}, u32[]{:S(2)}, u32[]{:S(2)}) collective-permute-start(f32[2,128,512]{2,1,0:T(8,128)} %get-tuple-element.15), channel_id=1, source_target_pairs={{64,0},{128,64},{192,128},{65,1},{129,65},{193,129},{66,2},{130,66... | collective-permute-start | bytes 1572872 | tf_op jit(solution)/shard_map/ppermute | solution.py:352
  10.8 1.3 %collective-permute-start.2 = (f32[2,128,128]{2,1,0:T(8,128)}, f32[2,128,128]{2,1,0:T(8,128)S(1)}, u32[]{:S(2)}, u32[]{:S(2)}) collective-permute-start(f32[2,128,128]{2,1,0:T(8,128)} %get-tuple-element.16), channel_id=1, source_target_pairs={{65,0},{66,1},{67,2},{68,3},{69,4},{70,5},{71,6},{72,7},{73,8},{74... | collective-permute-start | bytes 393224 | tf_op jit(solution)/shard_map/ppermute | solution.py:354
  12.8 1.7 %collective-permute-done.right = f32[2,512,128]{2,1,0:T(8,128)S(1)} collective-permute-done((f32[2,512,128]{2,1,0:T(8,128)}, f32[2,512,128]{2,1,0:T(8,128)S(1)}, u32[]{:S(2)}, u32[]{:S(2)}) %collective-permute-start) | collective-permute-done | bytes 524320 | tf_op jit(solution)/shard_map/ppermute | solution.py:353
  14.5 0.0 copy-start
  14.5 0.8 copy-done
  15.3 7.3 %upper_slots.1 = (f32[2,512,512]{2,1,0:T(8,128)}, f32[2,512,128]{2,1,0:T(8,128)}, f32[2,2,128,128]{3,2,1,0:T(8,128)}) custom-call(s32[2,64]{1,0:T(2,128)} %bitcast.12, s32[1]{0:T(128)} %bitcast.7.count, f32[2,512,512]{2,1,0:T(8,128)} %own.7, f32[2,512,128]{2,1,0:T(8,128)} %copy-done, bf16[64,128,128]{2,1,0:T(8,128)(2,1)} %bitcast.9, ...), custom_call_target="tpu_custom_call" | custom-call | flops 1000000000 | bytes 1048576 | tf_op jit(solution)/shard_map/upper_slots/pallas_call | solution.py:372
  22.5 21.3 %collective-permute-done.2.corner = f32[2,128,128]{2,1,0:T(8,128)S(1)} collective-permute-done((f32[2,128,128]{2,1,0:T(8,128)}, f32[2,128,128]{2,1,0:T(8,128)S(1)}, u32[]{:S(2)}, u32[]{:S(2)}) %collective-permute-start.2) | collective-permute-done | bytes 131104 | tf_op jit(solution)/shard_map/ppermute | solution.py:354
  43.9 0.0 copy-start.1
  43.9 0.0 collective-permute-done.1.below
  43.9 0.6 copy-done.1
  44.5 5.6 %lower_slots.1 = (f32[2,512,512]{2,1,0:T(8,128)}, f32[2,512,128]{2,1,0:T(8,128)}, f32[2,128,640]{2,1,0:T(8,128)}, f32[2,2,128,128]{3,2,1,0:T(8,128)}) custom-call(s32[2,64]{1,0:T(2,128)} %bitcast.13, s32[1]{0:T(128)} %bitcast.8.count, f32[2,512,512]{2,1,0:T(8,128)} %own.7, f32[2,512,128]{2,1,0:T(8,128)} %copy-done, ...), custom_call_target="tpu_custom_call", output_to_operand_aliasing={{0}: (9, {}), {1}: (10, {})} | custom-call | flops 1000000000 | bytes 1048576 | tf_op jit(solution)/shard_map/lower_slots/pallas_call | solution.py:382
  50.1 8.2 %collective-permute-start.3 = (f32[2,128,640]{2,1,0:T(8,128)}, f32[2,128,640]{2,1,0:T(8,128)S(1)}, u32[]{:S(2)}, u32[]{:S(2)}) collective-permute-start(f32[2,128,640]{2,1,0:T(8,128)} %get-tuple-element.21), channel_id=1, source_target_pairs={{0,64},{64,128},{128,192},{1,65},{65,129},{129,193},{2,66},{66,130... | collective-permute-start | bytes 1966088 | tf_op jit(solution)/shard_map/ppermute | solution.py:395
  58.3 16.2 %all_to_all.15 = f32[32,16,128]{2,1,0:T(8,128)S(1)} all-to-all(f32[32,16,128]{2,1,0:T(8,128)} %bitcast.11), channel_id=1, replica_groups=mesh['z_hi'=4,'x'=4,'y'=4,'z_lo'=2,'core'=2] {'x','y','core'}, dimensions={0} | all-to-all | bytes 524288 | tf_op jit(solution)/shard_map/all_to_all | solution.py:396
  74.5 10.6 %all_to_all.16 = f32[8,16,128]{2,1,0:T(8,128)S(1)} all-to-all(f32[8,16,128]{2,1,0:T(8,128)S(1)} %broadcast_in_dim.4), channel_id=1, replica_groups=mesh['z_hi'=4,'x'=4,'y'=4,'z_lo'=2,'core'=2] {'z_hi','z_lo'}, dimensions={0} | all-to-all | bytes 131072 | tf_op jit(solution)/shard_map/all_to_all | solution.py:309
  85.1 0.0 collective-permute-done.3.above
  85.1 1.6 %corner.1 = f32[2,512,128]{2,1,0:T(8,128)} custom-call(f32[2,512,128]{2,1,0:T(8,128)} %get-tuple-element.23.right_in, f32[2,128,640]{2,1,0:T(8,128)S(1)} %collective-permute-done.3.above), custom_call_target="tpu_custom_call", output_to_operand_aliasing={{}: (0, {})} | custom-call | tf_op jit(solution)/shard_map/corner/pallas_call | solution.py:399
  86.7 3.9 %collective-permute-start.4 = (f32[2,512,128]{2,1,0:T(8,128)}, f32[2,512,128]{2,1,0:T(8,128)S(1)}, u32[]{:S(2)}, u32[]{:S(2)}) collective-permute-start(f32[2,512,128]{2,1,0:T(8,128)} %corner.1), channel_id=1, source_target_pairs={{0,1},{1,2},{2,3},{3,4},{4,5},{5,6},{6,7},{7,8},{8,9},{9,10},{10,1... | collective-permute-start | bytes 1572872 | tf_op jit(solution)/shard_map/ppermute | solution.py:414
  90.6 18.3 %all_to_all.17.parts = f32[32,16,128]{2,1,0:T(8,128)S(1)} all-to-all(f32[32,16,128]{2,1,0:T(8,128)S(1)} %broadcast_in_dim.5), channel_id=1, replica_groups=mesh['z_hi'=4,'x'=4,'y'=4,'z_lo'=2,'core'=2] {'x','y','core'}, dimensions={0} | all-to-all | bytes 524288 | tf_op jit(solution)/shard_map/all_to_all | solution.py:309
  108.9 0.0 collective-permute-done.4.left
  108.9 2.2 %seams.1 = (f32[2,512,512]{2,1,0:T(8,128)}, f32[32,16,128]{2,1,0:T(8,128)}) custom-call(f32[2,512,512]{2,1,0:T(8,128)} %get-tuple-element.20.grad_in, f32[2,128,640]{2,1,0:T(8,128)S(1)} %collective-permute-done.3.above, f32[2,512,128]{2,1,0:T(8,128)S(1)} %collective-permute-done.4.left, ...), custom_call_target="tpu_custom_call", output_to_operand_aliasing={{0}: (0, {})} | custom-call | tf_op jit(solution)/shard_map/seams/pallas_call | solution.py:417
  (4 shorter events, 0.1 us)
Async XLA Ops:
  2.5 12.0 %collective-permute-start = (f32[2,512,128]{2,1,0:T(8,128)}, f32[2,512,128]{2,1,0:T(8,128)S(1)}, u32[]{:S(2)}, u32[]{:S(2)}) collective-permute-start(f32[2,512,128]{2,1,0:T(8,128)} %right_rim.1.after), channel_id=1, source_target_pairs={{1,0},{2,1},{3,2},{4,3},{5,4},{6,5},{7,6},{8,7},{9,8},{10,9},{11,1... | collective-permute-start | bytes 1572872 | tf_op jit(solution)/shard_map/ppermute | solution.py:353
  9.5 34.3 %collective-permute-start.1 = (f32[2,128,512]{2,1,0:T(8,128)}, f32[2,128,512]{2,1,0:T(8,128)}, u32[]{:S(2)}, u32[]{:S(2)}) collective-permute-start(f32[2,128,512]{2,1,0:T(8,128)} %get-tuple-element.15), channel_id=1, source_target_pairs={{64,0},{128,64},{192,128},{65,1},{129,65},{193,129},{66,2},{130,66... | collective-permute-start | bytes 1572872 | tf_op jit(solution)/shard_map/ppermute | solution.py:352
  10.8 33.0 %collective-permute-start.2 = (f32[2,128,128]{2,1,0:T(8,128)}, f32[2,128,128]{2,1,0:T(8,128)S(1)}, u32[]{:S(2)}, u32[]{:S(2)}) collective-permute-start(f32[2,128,128]{2,1,0:T(8,128)} %get-tuple-element.16), channel_id=1, source_target_pairs={{65,0},{66,1},{67,2},{68,3},{69,4},{70,5},{71,6},{72,7},{73,8},{74... | collective-permute-start | bytes 393224 | tf_op jit(solution)/shard_map/ppermute | solution.py:354
  14.5 0.8 copy-start
  43.9 0.6 copy-start.1
  50.1 35.0 %collective-permute-start.3 = (f32[2,128,640]{2,1,0:T(8,128)}, f32[2,128,640]{2,1,0:T(8,128)S(1)}, u32[]{:S(2)}, u32[]{:S(2)}) collective-permute-start(f32[2,128,640]{2,1,0:T(8,128)} %get-tuple-element.21), channel_id=1, source_target_pairs={{0,64},{64,128},{128,192},{1,65},{65,129},{129,193},{2,66},{66,130... | collective-permute-start | bytes 1966088 | tf_op jit(solution)/shard_map/ppermute | solution.py:395
  86.7 22.2 %collective-permute-start.4 = (f32[2,512,128]{2,1,0:T(8,128)}, f32[2,512,128]{2,1,0:T(8,128)S(1)}, u32[]{:S(2)}, u32[]{:S(2)}) collective-permute-start(f32[2,512,128]{2,1,0:T(8,128)} %corner.1), channel_id=1, source_target_pairs={{0,1},{1,2},{2,3},{3,4},{4,5},{5,6},{6,7},{7,8},{8,9},{9,10},{10,1... | collective-permute-start | bytes 1572872 | tf_op jit(solution)/shard_map/ppermute | solution.py:414
where the time goes:
time: 112 us; the launch traced here: 111 us
  blocking collectives  45.1 us (40%)
  waiting for transfers between devices  23 us (21%)
  Pallas kernels  20.4 us (18%)
  starting transfers between devices  19.8 us (18%)
  local copies, waits for them, and re-layouts  1.45 us (1%)
  between operations  1.39 us (1%)
    all_to_all x2, blocking collectives, everyone(): return lax.all_to_all(sent, axes, 0, 0, tiled=True)  28.9 us
    ppermute x1, waiting for transfers between devices, body(): corner = lax.ppermute(corner, BOTH, diagonal_back)  21.3 us
    all_to_all x1, blocking collectives, body(): lax.all_to_all(probe_2.reshape(plane, -1, PATCH), PLANE, 0, 0, tiled=True)  16.2 us
    ppermute x1, starting transfers between devices, body(): above = lax.ppermute(g_below, ROW, down)  8.16 us
    pallas_call x1, Pallas kernels, body(): pl.pallas_call(upper_kernel, out_shape=(own_shape, right_shape, probe_sha...  7.25 us
    pallas_call x1, Pallas kernels, body(): pl.pallas_call(functools.partial(lower_kernel, scale), out_shape=(own_sha...  5.58 us
    ppermute x1, starting transfers between devices, body(): right = lax.ppermute(right, COL, back)  5.15 us
    ppermute x1, starting transfers between devices, body(): left = lax.ppermute(g_right, COL, along)  3.86 us
  transfers between devices with their start and end apart: 5, of which 2 were waited for; matrix products, arithmetic and copies ran while one was open for 0% of the time, Pallas kernels for 8%

commit v1 on v0

--- a/solution.py
+++ b/solution.py
@@ -15,6 +15,7 @@
 PATCH = 128
 BLOCK = 8
 VMEM_LIMIT = 63 * 2**20
+SPLIT = 2 * PATCH
 ROW = "z_hi"
 COL = ("x", "y", "z_lo", "core")
 BOTH = (ROW,) + COL
@@ -34,7 +35,7 @@
     return jnp.dot(a, b, preferred_element_type=F32)
 
 
-def slot_block(at, slots, valids, pos, row_base, field, grad, photons, probe, probe_sum, plus_ref, minus_ref):
+def slot_block(at, slots, valids, pos, row_base, first_tile, field, grad, photons, probe, probe_sum, plus_ref, minus_ref):
     n = len(slots)
     lane = lax.broadcasted_iota(jnp.int32, (PATCH, PATCH), 1)
     plus = plus_ref[...]
@@ -43,7 +44,7 @@
     for s in slots:
         top = pos[0, s] - row_base
         left = pos[1, s]
-        tile = left // PATCH
+        tile = left // PATCH - first_tile
         shift = left % PATCH
         back = (PATCH - shift) % PATCH
         keep = lane >= shift
@@ -123,7 +124,7 @@
 
 def list_slots(wanted, pos, count, listed, photons, photon_buf, photon_sems):
     def list_step(s, found):
-        chosen = wanted(pos[0, s])
+        chosen = wanted(pos[0, s], pos[1, s])
 
         @pl.when(chosen)
         def _():
@@ -135,7 +136,7 @@
     return lax.fori_loop(0, count, list_step, jnp.int32(0))
 
 
-def run_slots(found, pos, row_base, listed, field, grad, photons, photon_buf, photon_sems, probe, probe_sum,
+def run_slots(found, pos, row_base, first_tile, listed, field, grad, photons, photon_buf, photon_sems, probe, probe_sum,
               plus_ref, minus_ref):
     def step(k, carry, first=0, width=BLOCK):
         places = [first + k * width + i for i in range(width)]
@@ -147,7 +148,7 @@
             def _(a=a, s=s):
                 pltpu.make_async_copy(photons.at[s], photon_buf.at[a], photon_sems.at[a]).wait()
 
-        slot_block(at, slots, valids, pos, row_base, field, grad, photon_buf, probe, probe_sum, plus_ref, minus_ref)
+        slot_block(at, slots, valids, pos, row_base, first_tile, field, grad, photon_buf, probe, probe_sum, plus_ref, minus_ref)
         return carry
 
     rest = found % BLOCK
@@ -187,12 +188,18 @@
     store.wait()
 
 
-def below_rim_kernel(own, after, below, corner, below_buf, sems):
+def below_rim_kernel(own, after, below_left, below_right, corner, below_buf, sems):
     rim = pl.ds(0, PATCH)
+    left_cols = below_left.shape[2]
     load = pltpu.make_async_copy(own.at[:, rim, :], below_buf, sems.at[0])
     load.start()
     load.wait()
-    stores = copies_of([(below_buf, below), (below_buf.at[:, :, rim], corner)], sems)
+    stores = copies_of(
+        [(below_buf.at[:, :, pl.ds(0, left_cols)], below_left),
+         (below_buf.at[:, :, pl.ds(left_cols, below_right.shape[2])], below_right),
+         (below_buf.at[:, :, rim], corner)],
+        sems,
+    )
     start_all(stores)
     wait_all(stores)
 
@@ -208,13 +215,13 @@
         sems,
     )
     start_all(loads)
-    found = list_slots(lambda top: top <= rows - PATCH, pos, count[0], listed, photons, photon_buf, photon_sems)
+    found = list_slots(lambda top, left: top <= rows - PATCH, pos, count[0], listed, photons, photon_buf, photon_sems)
     grad[...] = jnp.zeros(grad.shape, F32)
     probe_sum[...] = jnp.zeros(probe_sum.shape, F32)
     loads[0].wait()
     fill_tables(waves, plus_ref, minus_ref)
     wait_all(loads[1:])
-    run_slots(found, pos, 0, listed, field, grad, photons, photon_buf, photon_sems, probe, probe_sum,
+    run_slots(found, pos, 0, 0, listed, field, grad, photons, photon_buf, photon_sems, probe, probe_sum,
               plus_ref, minus_ref)
     stores = copies_of(
         [(probe_sum, probe_out)]
@@ -226,42 +233,71 @@
     wait_all(stores)
 
 
-def lower_kernel(scale, pos, count, own, right, below, corner, photons, probe_in, waves_in, own_in, right_in, sum_in,
-                 g_own, g_right, g_below, probe_out,
-                 field, grad, photon_buf, probe, waves, plus_ref, minus_ref, probe_sum, listed, sems, photon_sems):
-    rows, cols = own.shape[1], own.shape[2]
-    tiles = cols // PATCH
-    base = rows - PATCH
-    last, upper, lower = pl.ds(base, PATCH), pl.ds(0, PATCH), pl.ds(PATCH, PATCH)
-
-    def last_rows(array):
-        return [array.at[:, last, pl.ds(t * PATCH, PATCH)] for t in range(tiles)]
-
-    loads = copies_of(
-        [(waves_in, waves), (probe_in, probe), (sum_in, probe_sum)]
-        + [(a, field.at[t, :, upper, :]) for t, a in enumerate(last_rows(own) + [right.at[:, last, :]])]
-        + [(a, field.at[t, :, lower, :]) for t, a in enumerate(by_tiles(below, tiles) + [corner])]
-        + [(a, grad.at[t, :, upper, :]) for t, a in enumerate(last_rows(own_in) + [right_in.at[:, last, :]])],
-        sems,
-    )
+def lower_kernel(wanted, first_tile, scale, pos, count, photons, probe_in, waves_in, sum_in, fields, grads, sends,
+                 probe_out, field, grad, photon_buf, probe, waves, plus_ref, minus_ref, probe_sum, listed, sems,
+                 photon_sems):
+    upper, lower = pl.ds(0, PATCH), pl.ds(PATCH, PATCH)
+    pairs = [(waves_in, waves), (probe_in, probe), (sum_in, probe_sum)]
+    for t, (last, rim) in enumerate(fields):
+        pairs += [(last, field.at[t, :, upper, :]), (rim, field.at[t, :, lower, :])]
+    for t, (last_in, _, rim_in) in enumerate(grads):
+        pairs.append((last_in, grad.at[t, :, upper, :]))
+        if rim_in is not None:
+            pairs.append((rim_in, grad.at[t, :, lower, :]))
+    loads = copies_of(pairs, sems)
     start_all(loads)
-    found = list_slots(lambda top: top > base, pos, count[0], listed, photons, photon_buf, photon_sems)
-    for t in range(tiles + 1):
-        grad[t, :, lower, :] = jnp.zeros((2, PATCH, PATCH), F32)
+    found = list_slots(wanted, pos, count[0], listed, photons, photon_buf, photon_sems)
+    for t, (_, _, rim_in) in enumerate(grads):
+        if rim_in is None:
+            grad[t, :, lower, :] = jnp.zeros((2, PATCH, PATCH), F32)
     loads[0].wait()
     fill_tables(waves, plus_ref, minus_ref)
     wait_all(loads[1:])
-    run_slots(found, pos, base, listed, field, grad, photons, photon_buf, photon_sems, probe, probe_sum,
+    base = 3 * PATCH
+    run_slots(found, pos, base, first_tile, listed, field, grad, photons, photon_buf, photon_sems, probe, probe_sum,
               plus_ref, minus_ref)
-    probe_sum[...] = probe_sum[...] * scale
-    stores = copies_of(
-        [(probe_sum, probe_out)]
-        + [(grad.at[t, :, lower, :], a) for t, a in enumerate(by_tiles(g_below, tiles + 1))]
-        + [(grad.at[t, :, upper, :], a) for t, a in enumerate(last_rows(g_own) + [g_right.at[:, last, :]])],
-        sems,
-    )
+    if scale is not None:
+        probe_sum[...] = probe_sum[...] * scale
+    pairs = [(probe_sum, probe_out)]
+    for t, (_, last_out, _) in enumerate(grads):
+        pairs.append((grad.at[t, :, upper, :], last_out))
+    for t, send in enumerate(sends):
+        pairs.append((grad.at[t, :, lower, :], send))
+    stores = copies_of(pairs, sems)
     start_all(stores)
     wait_all(stores)
+
+
+def block_of(array, row, tile):
+    return array.at[:, pl.ds(row, PATCH), pl.ds(tile * PATCH, PATCH)]
+
+
+def lower_left_kernel(pos, count, own, below, photons, probe_in, waves_in, own_in, sum_in,
+                      g_own, g_below, carried, probe_out, *scratch):
+    base = own.shape[1] - PATCH
+    lower_kernel(
+        lambda top, left: (top > base) & (left < SPLIT), 0, None, pos, count, photons, probe_in, waves_in, sum_in,
+        [(block_of(own, base, t), block_of(below, 0, t)) for t in range(3)],
+        [(block_of(own_in, base, t), block_of(g_own, base, t), None) for t in range(3)],
+        [block_of(g_below, 0, 0), block_of(g_below, 0, 1), carried],
+        probe_out, *scratch,
+    )
+
+
+def lower_right_kernel(scale, pos, count, own, right, below_left, below_right, corner, photons, probe_in, waves_in,
+                       own_in, right_in, carried, sum_in, g_own, g_right, g_below, probe_out, *scratch):
+    base = own.shape[1] - PATCH
+    last = pl.ds(base, PATCH)
+    lower_kernel(
+        lambda top, left: (top > base) & (left >= SPLIT), 2, scale, pos, count, photons, probe_in, waves_in, sum_in,
+        [(block_of(own, base, 2), block_of(below_left, 0, 2)), (block_of(own, base, 3), below_right),
+         (right.at[:, last, :], corner)],
+        [(block_of(own_in, base, 2), block_of(g_own, base, 2), carried),
+         (block_of(own_in, base, 3), block_of(g_own, base, 3), None),
+         (right_in.at[:, last, :], g_right.at[:, last, :], None)],
+        [block_of(g_below, 0, t) for t in range(3)],
+        probe_out, *scratch,
+    )
 
 
 def corner_kernel(right_in, above, right, rim_buf, corner_buf, sems):
@@ -276,14 +312,16 @@
     store.wait()
 
 
-def seam_kernel(grad_in, above, left, parts, grad, probe,
+def seam_kernel(grad_in, above_left, above_right, left, parts, grad, probe,
                 top_buf, left_buf, above_buf, beside_buf, probe_buf, sems):
     rows, cols = grad.shape[1], grad.shape[2]
     rest = rows - PATCH
     top_rim = grad.at[:, pl.ds(0, PATCH), :]
     left_rim = grad.at[:, pl.ds(PATCH, rest), pl.ds(0, PATCH)]
     loads = copies_of(
-        [(top_rim, top_buf), (left_rim, left_buf), (above.at[:, :, pl.ds(0, cols)], above_buf), (left, beside_buf),
+        [(top_rim, top_buf), (left_rim, left_buf), (left, beside_buf),
+         (above_left, above_buf.at[:, :, pl.ds(0, SPLIT)]),
+         (above_right.at[:, :, pl.ds(0, cols - SPLIT)], above_buf.at[:, :, pl.ds(SPLIT, cols - SPLIT)]),
          (parts, probe_buf)],
         sems,
     )
@@ -340,23 +378,26 @@
         compiler_params=params,
         name="right_rim",
     )(object_field)
-    below, corner = pl.pallas_call(
+    rim_shape = shape(2, PATCH, PATCH)
+    below_left, below_right, corner = pl.pallas_call(
         below_rim_kernel,
-        out_shape=(shape(2, PATCH, cols), shape(2, PATCH, PATCH)),
+        out_shape=(shape(2, PATCH, SPLIT + PATCH), rim_shape, rim_shape),
         in_specs=[hbm, hbm],
-        out_specs=(hbm,) * 2,
-        scratch_shapes=[pltpu.VMEM((2, PATCH, cols), F32), pltpu.SemaphoreType.DMA((2,))],
+        out_specs=(hbm,) * 3,
+        scratch_shapes=[pltpu.VMEM((2, PATCH, cols), F32), pltpu.SemaphoreType.DMA((3,))],
         compiler_params=params,
         name="below_rim",
     )(object_field, right)
-    below = lax.ppermute(below, ROW, up)
+    below_left = lax.ppermute(below_left, ROW, up)
     right = lax.ppermute(right, COL, back)
+    below_right, corner, right = lax.optimization_barrier((below_right, corner, right))
+    below_right = lax.ppermute(below_right, ROW, up)
     corner = lax.ppermute(corner, BOTH, diagonal_back)
 
-    def scratch(height):
+    def scratch(wide, height):
         return [
-            pltpu.VMEM((tiles + 1, 2, height, PATCH), F32),
-            pltpu.VMEM((tiles + 1, 2, height, PATCH), F32),
+            pltpu.VMEM((wide, 2, height, PATCH), F32),
+            pltpu.VMEM((wide, 2, height, PATCH), F32),
             pltpu.VMEM(photon_rows.shape, BF16),
             pltpu.VMEM(probe_modes.shape, F32),
             pltpu.VMEM(waves.shape, F32),
@@ -364,7 +405,7 @@
             pltpu.VMEM((2 * PATCH, 2 * PATCH), BF16),
             pltpu.VMEM(probe_modes.shape, F32),
             pltpu.SMEM((slot_count,), jnp.int32),
-            pltpu.SemaphoreType.DMA((3 * tiles + 6,)),
+            pltpu.SemaphoreType.DMA((tiles + 9,)),
             pltpu.SemaphoreType.DMA((slot_count,)),
         ]
 
@@ -374,25 +415,39 @@
         out_shape=(own_shape, right_shape, probe_shape),
         in_specs=[smem, smem] + [hbm] * 5,
         out_specs=(hbm,) * 3,
-        scratch_shapes=scratch(rows),
+        scratch_shapes=scratch(tiles + 1, rows),
         compiler_params=params,
         cost_estimate=pl.CostEstimate(flops=10**9, bytes_accessed=2**20, transcendentals=0),
         name="upper_slots",
     )(pos, count, object_field, right, photon_rows, probe_modes, waves)
-    g_own, g_right, g_below, probe_2 = pl.pallas_call(
-        functools.partial(lower_kernel, scale),
-        out_shape=(own_shape, right_shape, shape(2, PATCH, cols + PATCH), probe_shape),
-        in_specs=[smem] * 2 + [hbm] * 10,
+    g_own, g_below_left, carried, probe_1 = pl.pallas_call(
+        lower_left_kernel,
+        out_shape=(own_shape, shape(2, PATCH, SPLIT), rim_shape, probe_shape),
+        in_specs=[smem] * 2 + [hbm] * 7,
         out_specs=(hbm,) * 4,
-        scratch_shapes=scratch(2 * PATCH),
-        input_output_aliases={9: 0, 10: 1},
+        scratch_shapes=scratch(3, 2 * PATCH),
+        input_output_aliases={7: 0},
         compiler_params=params,
         cost_estimate=pl.CostEstimate(flops=10**9, bytes_accessed=2**20, transcendentals=0),
-        name="lower_slots",
-    )(pos, count, object_field, right, below, corner, photon_rows, probe_modes, waves, g_own, g_right, probe_1)
+        name="lower_left_slots",
+    )(pos, count, object_field, below_left, photon_rows, probe_modes, waves, g_own, probe_1)
+    above_left = lax.ppermute(g_below_left, ROW, down)
+    g_own, g_right, g_below_right, probe_2 = pl.pallas_call(
+        functools.partial(lower_right_kernel, scale),
+        out_shape=(own_shape, right_shape, shape(2, PATCH, cols + PATCH - SPLIT), probe_shape),
+        in_specs=[smem] * 2 + [hbm] * 12,
+        out_specs=(hbm,) * 4,
+        scratch_shapes=scratch(3, 2 * PATCH),
+        input_output_aliases={10: 0, 11: 1},
+        compiler_params=params,
+        cost_estimate=pl.CostEstimate(flops=10**10, bytes_accessed=2**20, transcendentals=0),
+        name="lower_right_slots",
+    )(pos, count, object_field, right, below_left, below_right, corner, photon_rows, probe_modes, waves,
+      g_own, g_right, carried, probe_1)
 
     plane, depth = lax.axis_size(PLANE), lax.axis_size(DEPTH)
-    above = lax.ppermute(g_below, ROW, down)
+    above_right = lax.ppermute(g_below_right, ROW, down)
+    probe_2, above_left = lax.optimization_barrier((probe_2, above_left))
     shares = lax.all_to_all(probe_2.reshape(plane, -1, PATCH), PLANE, 0, 0, tiled=True)
     share = jnp.sum(shares, axis=0)
     share = jnp.sum(everyone(share, DEPTH, depth), axis=0)
@@ -409,7 +464,7 @@
         input_output_aliases={0: 0},
         compiler_params=small,
         name="corner",
-    )(g_right, above)
+    )(g_right, above_right)
     share, g_right = lax.optimization_barrier((share, g_right))
     left = lax.ppermute(g_right, COL, along)
     parts = everyone(share, PLANE, plane)
@@ -417,7 +472,7 @@
     object_gradient, probe_gradient = pl.pallas_call(
         seam_kernel,
         out_shape=(own_shape, shape(*parts.shape)),
-        in_specs=[hbm] * 4,
+        in_specs=[hbm] * 5,
         out_specs=(hbm, hbm),
         scratch_shapes=[
             pltpu.VMEM((2, PATCH, cols), F32),
@@ -425,12 +480,12 @@
             pltpu.VMEM((2, PATCH, cols), F32),
             pltpu.VMEM((2, rows, PATCH), F32),
             pltpu.VMEM(parts.shape, F32),
-            pltpu.SemaphoreType.DMA((5,)),
+            pltpu.SemaphoreType.DMA((6,)),
         ],
         input_output_aliases={0: 0},
         compiler_params=small,
         name="seams",
-    )(g_own, above, left, parts)
+    )(g_own, above_left, above_right, left, parts)
     return (object_gradient, probe_gradient.reshape(probe_modes.shape))
 
 

time: 112 us -> 122 us (1.089)
  starting transfers between devices: 19.8 us -> 37.6 us
  waiting for transfers between devices: 23 us -> 12 us
  Pallas kernels: 20.4 us -> 29.9 us
  blocking collectives: 45.1 us -> 36 us
  local copies, waits for them, and re-layouts: 1.45 us -> 3.16 us
    ppermute x1, waiting for transfers between devices: 21.3 us -> 0.01 us  [body(): corner = lax.ppermute(corner, BOTH, diagonal_back)]
    all_to_all x2 -> x1, blocking collectives: 28.9 us -> 14.1 us  [everyone(): return lax.all_to_all(sent, axes, 0, 0, tiled=True)]
    all_to_all x0 -> x1, starting transfers between devices: none -> 9.81 us  [everyone(): return lax.all_to_all(sent, axes, 0, 0, tiled=True)]
    ppermute x2 -> x4, starting transfers between devices: 9.45 us -> 17.6 us  [the longest x1 11.9 us: body(): above_left = lax.ppermute(g_below_left, ROW, down)]
    pallas_call x1, Pallas kernels: 7.25 us -> 13.3 us  [body(): pl.pallas_call(upper_kernel, out_shape=(own_shape, right_shape, probe_sha...]
    all_to_all x1, blocking collectives: 16.2 us -> 21.9 us  [body(): lax.all_to_all(probe_2.reshape(plane, -1, PATCH), PLANE, 0, 0, tiled=True)]
    all_to_all x0 -> x1, waiting for transfers between devices: none -> 5.13 us  [everyone(): return lax.all_to_all(sent, axes, 0, 0, tiled=True)]
    pallas_call x2 -> x3, Pallas kernels: 7.49 us -> 12.3 us  [the longest x1 5.24 us: body(): pl.pallas_call(functools.partial(lower_right_kernel, scale), out_shape=(o...]
  transfers between devices with their start and end apart: 5 -> 8, of which waited for: 2 -> 3; matrix products, arithmetic and copies ran while one was open for 0% -> 1% of each run, Pallas kernels for 8% -> 21%
where the time goes in v1:
time: 122 us; the launch traced here: 120 us
  starting transfers between devices  37.6 us (31%)
  blocking collectives  36 us (30%)
  Pallas kernels  29.9 us (25%)
  waiting for transfers between devices  12 us (10%)
  local copies, waits for them, and re-layouts  3.16 us (3%)
  between operations  1.63 us (1%)
    all_to_all x1, blocking collectives, body(): lax.all_to_all(probe_2.reshape(plane, -1, PATCH), PLANE, 0, 0, tiled=True)  21.9 us
    all_to_all x1, blocking collectives, everyone(): return lax.all_to_all(sent, axes, 0, 0, tiled=True)  14.1 us
    pallas_call x1, Pallas kernels, body(): pl.pallas_call(upper_kernel, out_shape=(own_shape, right_shape, probe_sha...  13.3 us
    ppermute x1, starting transfers between devices, body(): above_left = lax.ppermute(g_below_left, ROW, down)  11.9 us
    all_to_all x1, starting transfers between devices, everyone(): return lax.all_to_all(sent, axes, 0, 0, tiled=True)  9.81 us
    pallas_call x1, Pallas kernels, body(): pl.pallas_call(functools.partial(lower_right_kernel, scale), out_shape=(o...  5.24 us
    ppermute x1, starting transfers between devices, body(): right = lax.ppermute(right, COL, back)  5.15 us
    pallas_call x1, Pallas kernels, body(): pl.pallas_call(lower_left_kernel, out_shape=(own_shape, shape(2, PATCH, S...  5.14 us
  transfers between devices with their start and end apart: 8, of which 3 were waited for; matrix products, arithmetic and copies ran while one was open for 1% of the time, Pallas kernels for 21%

profile of v1, /device:TPU:1, one launch (start us, length us, event | category | flops | bytes accessed | tf_op | source)
XLA Modules:
  0.0 120.3 jit_solution(3241030363820104163)
XLA Ops:
  0.6 1.8 %right_rim.1.after = f32[2,512,128]{2,1,0:T(8,128)} custom-call(f32[2,512,512]{2,1,0:T(8,128)} %own.9), custom_call_target="tpu_custom_call" | custom-call | tf_op jit(solution)/shard_map/right_rim/pallas_call | solution.py:372
  2.5 5.1 %collective-permute-start = (f32[2,512,128]{2,1,0:T(8,128)}, f32[2,512,128]{2,1,0:T(8,128)S(1)}, u32[]{:S(2)}, u32[]{:S(2)}) collective-permute-start(f32[2,512,128]{2,1,0:T(8,128)} %right_rim.1.after), channel_id=1, source_target_pairs={{1,0},{2,1},{3,2},{4,3},{5,4},{6,5},{7,6},{8,7},{9,8},{10,9},{11,1... | collective-permute-start | bytes 1572872 | tf_op jit(solution)/shard_map/ppermute | solution.py:392
  7.6 1.9 %below_rim.1 = (f32[2,128,384]{2,1,0:T(8,128)}, f32[2,128,128]{2,1,0:T(8,128)}, f32[2,128,128]{2,1,0:T(8,128)}) custom-call(f32[2,512,512]{2,1,0:T(8,128)} %own.9, f32[2,512,128]{2,1,0:T(8,128)} %right_rim.1.after), custom_call_target="tpu_custom_call" | custom-call | tf_op jit(solution)/shard_map/below_rim/pallas_call | solution.py:382
  9.6 1.3 %collective-permute-start.1 = (f32[2,128,384]{2,1,0:T(8,128)}, f32[2,128,384]{2,1,0:T(8,128)}, u32[]{:S(2)}, u32[]{:S(2)}) collective-permute-start(f32[2,128,384]{2,1,0:T(8,128)} %get-tuple-element.28), channel_id=1, source_target_pairs={{64,0},{128,64},{192,128},{65,1},{129,65},{193,129},{66,2},{130,66... | collective-permute-start | bytes 1179656 | tf_op jit(solution)/shard_map/ppermute | solution.py:391
  11.5 3.0 %collective-permute-done.right = f32[2,512,128]{2,1,0:T(8,128)S(1)} collective-permute-done((f32[2,512,128]{2,1,0:T(8,128)}, f32[2,512,128]{2,1,0:T(8,128)S(1)}, u32[]{:S(2)}, u32[]{:S(2)}) %collective-permute-start) | collective-permute-done | bytes 524320 | tf_op jit(solution)/shard_map/ppermute | solution.py:392
  14.5 1.3 %collective-permute-start.2 = (f32[2,128,128]{2,1,0:T(8,128)}, f32[2,128,128]{2,1,0:T(8,128)S(1)}, u32[]{:S(2)}, u32[]{:S(2)}) collective-permute-start(f32[2,128,128]{2,1,0:T(8,128)} %get-tuple-element.29), channel_id=1, source_target_pairs={{64,0},{128,64},{192,128},{65,1},{129,65},{193,129},{66,2},{130,66... | collective-permute-start | bytes 393224 | tf_op jit(solution)/shard_map/ppermute | solution.py:394
  15.8 1.3 %collective-permute-start.3 = (f32[2,128,128]{2,1,0:T(8,128)}, f32[2,128,128]{2,1,0:T(8,128)S(1)}, u32[]{:S(2)}, u32[]{:S(2)}) collective-permute-start(f32[2,128,128]{2,1,0:T(8,128)} %get-tuple-element.30), channel_id=1, source_target_pairs={{65,0},{66,1},{67,2},{68,3},{69,4},{70,5},{71,6},{72,7},{73,8},{74... | collective-permute-start | bytes 393224 | tf_op jit(solution)/shard_map/ppermute | solution.py:395
  17.1 0.0 copy-done.2
  17.1 13.3 %upper_slots.1 = (f32[2,512,512]{2,1,0:T(8,128)}, f32[2,512,128]{2,1,0:T(8,128)}, f32[2,2,128,128]{3,2,1,0:T(8,128)}) custom-call(s32[2,64]{1,0:T(2,128)} %bitcast.14, s32[1]{0:T(128)} %bitcast.7.count, f32[2,512,512]{2,1,0:T(8,128)} %own.9, f32[2,512,128]{2,1,0:T(8,128)} %copy-done.2, bf16[64,128,128]{2,1,0:T(8,128)(2,1)} %bitcast.10, ...), custom_call_target="tpu_custom_call" | custom-call | flops 1000000000 | bytes 1048576 | tf_op jit(solution)/shard_map/upper_slots/pallas_call | solution.py:413
  30.4 3.9 %collective-permute-done.1.below.below_left = f32[2,128,384]{2,1,0:T(8,128)} collective-permute-done((f32[2,128,384]{2,1,0:T(8,128)}, f32[2,128,384]{2,1,0:T(8,128)}, u32[]{:S(2)}, u32[]{:S(2)}) %collective-permute-start.1) | collective-permute-done | bytes 393248 | tf_op jit(solution)/shard_map/ppermute | solution.py:391
  34.3 5.1 %lower_left_slots.1 = (f32[2,512,512]{2,1,0:T(8,128)}, f32[2,128,256]{2,1,0:T(8,128)}, f32[2,128,128]{2,1,0:T(8,128)}, f32[2,2,128,128]{3,2,1,0:T(8,128)}) custom-call(s32[2,64]{1,0:T(2,128)} %bitcast.15, s32[1]{0:T(128)} %bitcast.8.count, f32[2,512,512]{2,1,0:T(8,128)} %own.9, ...), custom_call_target="tpu_custom_call", output_to_operand_aliasing={{0}: (7, {})} | custom-call | flops 1000000000 | bytes 1048576 | tf_op jit(solution)/shard_map/lower_left_slots/pallas_call | solution.py:423
  39.5 11.9 %collective-permute-start.4 = (f32[2,128,256]{2,1,0:T(8,128)}, f32[2,128,256]{2,1,0:T(8,128)S(1)}, u32[]{:S(2)}, u32[]{:S(2)}) collective-permute-start(f32[2,128,256]{2,1,0:T(8,128)} %get-tuple-element.39), channel_id=1, source_target_pairs={{0,64},{64,128},{128,192},{1,65},{65,129},{129,193},{2,66},{66,130... | collective-permute-start | bytes 786440 | tf_op jit(solution)/shard_map/ppermute | solution.py:434
  51.4 0.0 collective-permute-done.2.below_right
  51.4 0.0 collective-permute-done.3.corner
  51.4 0.6 copy-done.3
  52.0 0.1 copy-done.4
  52.1 5.2 %lower_right_slots.1 = (f32[2,512,512]{2,1,0:T(8,128)}, f32[2,512,128]{2,1,0:T(8,128)}, f32[2,128,384]{2,1,0:T(8,128)}, f32[2,2,128,128]{3,2,1,0:T(8,128)}) custom-call(s32[2,64]{1,0:T(2,128)} %bitcast.16, s32[1]{0:T(128)} %bitcast.9.count, f32[2,512,512]{2,1,0:T(8,128)} %own.9, ...), custom_call_target="tpu_custom_call", output_to_operand_aliasing={{0}: (10, {}), {1}: (11, {})} | custom-call | flops 10000000000 | bytes 1048576 | tf_op jit(solution)/shard_map/lower_right_slots/pallas_call | solution.py:435
  57.3 3.1 %collective-permute-start.5 = (f32[2,128,384]{2,1,0:T(8,128)}, f32[2,128,384]{2,1,0:T(8,128)S(1)}, u32[]{:S(2)}, u32[]{:S(2)}) collective-permute-start(f32[2,128,384]{2,1,0:T(8,128)} %get-tuple-element.41), channel_id=1, source_target_pairs={{0,64},{64,128},{128,192},{1,65},{65,129},{129,193},{2,66},{66,130... | collective-permute-start | bytes 1179656 | tf_op jit(solution)/shard_map/ppermute | solution.py:449
  60.4 0.0 collective-permute-done.4.above_left
  60.4 21.9 %all_to_all.15 = f32[32,16,128]{2,1,0:T(8,128)S(1)} all-to-all(f32[32,16,128]{2,1,0:T(8,128)} %bitcast.13), channel_id=1, replica_groups=mesh['z_hi'=4,'x'=4,'y'=4,'z_lo'=2,'core'=2] {'x','y','core'}, dimensions={0} | all-to-all | bytes 524288 | tf_op jit(solution)/shard_map/all_to_all | solution.py:451
  82.4 0.6 broadcast_in_dim.4
  83.0 9.8 %all-to-all-start.1 = ((f32[8,16,128]{2,1,0:T(8,128)}), f32[8,16,128]{2,1,0:T(8,128)S(1)}, u32[]{:S(2)}, u32[]{:S(2)}) async-start(f32[8,16,128]{2,1,0:T(8,128)} %broadcast_in_dim.4), calls=%async_computation.1 | async-start | bytes 131072 | tf_op jit(solution)/shard_map/all_to_all | solution.py:347
  92.8 0.0 collective-permute-done.5.above.above_right
  92.8 0.0 copy-start
  92.8 1.0 copy-done
  93.9 0.2 corner.1
  94.1 0.8 copy-done.1
  94.9 5.1 %all-to-all-done.1 = f32[8,16,128]{2,1,0:T(8,128)S(1)} async-done(((f32[8,16,128]{2,1,0:T(8,128)}), f32[8,16,128]{2,1,0:T(8,128)S(1)}, u32[]{:S(2)}, u32[]{:S(2)}) %all-to-all-start.1) | async-done | bytes 65568 | tf_op jit(solution)/shard_map/all_to_all | solution.py:347
  100.0 3.7 %collective-permute-start.6 = (f32[2,512,128]{2,1,0:T(8,128)}, f32[2,512,128]{2,1,0:T(8,128)S(1)}, u32[]{:S(2)}, u32[]{:S(2)}) collective-permute-start(f32[2,512,128]{2,1,0:T(8,128)} %copy-done.1), channel_id=1, source_target_pairs={{0,1},{1,2},{2,3},{3,4},{4,5},{5,6},{6,7},{7,8},{8,9},{9,10},{10,1... | collective-permute-start | bytes 1572872 | tf_op jit(solution)/shard_map/ppermute | solution.py:469
  103.8 14.1 %all_to_all.16.parts = f32[32,16,128]{2,1,0:T(8,128)S(1)} all-to-all(f32[32,16,128]{2,1,0:T(8,128)S(1)} %broadcast_in_dim.5), channel_id=1, replica_groups=mesh['z_hi'=4,'x'=4,'y'=4,'z_lo'=2,'core'=2] {'x','y','core'}, dimensions={0} | all-to-all | bytes 524288 | tf_op jit(solution)/shard_map/all_to_all | solution.py:347
  117.9 0.0 collective-permute-done.6.left
  117.9 2.2 %seams.1 = (f32[2,512,512]{2,1,0:T(8,128)}, f32[32,16,128]{2,1,0:T(8,128)}) custom-call(f32[2,512,512]{2,1,0:T(8,128)} %get-tuple-element.37.grad_in, f32[2,128,256]{2,1,0:T(8,128)S(1)} %collective-permute-done.4.above_left, f32[2,128,384]{2,1,0:T(8,128)S(1)} %collective-permute-done.5.above.above_right, ...), custom_call_target="tpu_custom_call", output_to_operand_aliasing={{0}: (0, {})} | custom-call | tf_op jit(solution)/shard_map/seams/pallas_call | solution.py:472
  (7 shorter events, 0.1 us)
Async XLA Ops:
  2.5 12.0 %collective-permute-start = (f32[2,512,128]{2,1,0:T(8,128)}, f32[2,512,128]{2,1,0:T(8,128)S(1)}, u32[]{:S(2)}, u32[]{:S(2)}) collective-permute-start(f32[2,512,128]{2,1,0:T(8,128)} %right_rim.1.after), channel_id=1, source_target_pairs={{1,0},{2,1},{3,2},{4,3},{5,4},{6,5},{7,6},{8,7},{9,8},{10,9},{11,1... | collective-permute-start | bytes 1572872 | tf_op jit(solution)/shard_map/ppermute | solution.py:392
  9.6 24.8 %collective-permute-start.1 = (f32[2,128,384]{2,1,0:T(8,128)}, f32[2,128,384]{2,1,0:T(8,128)}, u32[]{:S(2)}, u32[]{:S(2)}) collective-permute-start(f32[2,128,384]{2,1,0:T(8,128)} %get-tuple-element.28), channel_id=1, source_target_pairs={{64,0},{128,64},{192,128},{65,1},{129,65},{193,129},{66,2},{130,66... | collective-permute-start | bytes 1179656 | tf_op jit(solution)/shard_map/ppermute | solution.py:391
  14.5 2.6 %copy-start.2 = (f32[2,512,128]{2,1,0:T(8,128)}, f32[2,512,128]{2,1,0:T(8,128)S(1)}, u32[]{:S(2)}) copy-start(f32[2,512,128]{2,1,0:T(8,128)S(1)} %collective-permute-done.right) | copy-start | bytes 1572868
  14.5 36.9 %collective-permute-start.2 = (f32[2,128,128]{2,1,0:T(8,128)}, f32[2,128,128]{2,1,0:T(8,128)S(1)}, u32[]{:S(2)}, u32[]{:S(2)}) collective-permute-start(f32[2,128,128]{2,1,0:T(8,128)} %get-tuple-element.29), channel_id=1, source_target_pairs={{64,0},{128,64},{192,128},{65,1},{129,65},{193,129},{66,2},{130,66... | collective-permute-start | bytes 393224 | tf_op jit(solution)/shard_map/ppermute | solution.py:394
  15.8 35.6 %collective-permute-start.3 = (f32[2,128,128]{2,1,0:T(8,128)}, f32[2,128,128]{2,1,0:T(8,128)S(1)}, u32[]{:S(2)}, u32[]{:S(2)}) collective-permute-start(f32[2,128,128]{2,1,0:T(8,128)} %get-tuple-element.30), channel_id=1, source_target_pairs={{65,0},{66,1},{67,2},{68,3},{69,4},{70,5},{71,6},{72,7},{73,8},{74... | collective-permute-start | bytes 393224 | tf_op jit(solution)/shard_map/ppermute | solution.py:395
  39.5 21.0 %collective-permute-start.4 = (f32[2,128,256]{2,1,0:T(8,128)}, f32[2,128,256]{2,1,0:T(8,128)S(1)}, u32[]{:S(2)}, u32[]{:S(2)}) collective-permute-start(f32[2,128,256]{2,1,0:T(8,128)} %get-tuple-element.39), channel_id=1, source_target_pairs={{0,64},{64,128},{128,192},{1,65},{65,129},{129,193},{2,66},{66,130... | collective-permute-start | bytes 786440 | tf_op jit(solution)/shard_map/ppermute | solution.py:434
  51.4 0.6 copy-start.3
  51.4 0.7 copy-start.4
  57.3 35.5 %collective-permute-start.5 = (f32[2,128,384]{2,1,0:T(8,128)}, f32[2,128,384]{2,1,0:T(8,128)S(1)}, u32[]{:S(2)}, u32[]{:S(2)}) collective-permute-start(f32[2,128,384]{2,1,0:T(8,128)} %get-tuple-element.41), channel_id=1, source_target_pairs={{0,64},{64,128},{128,192},{1,65},{65,129},{129,193},{2,66},{66,130... | collective-permute-start | bytes 1179656 | tf_op jit(solution)/shard_map/ppermute | solution.py:449
  83.0 17.0 %all-to-all-start.1 = ((f32[8,16,128]{2,1,0:T(8,128)}), f32[8,16,128]{2,1,0:T(8,128)S(1)}, u32[]{:S(2)}, u32[]{:S(2)}) async-start(f32[8,16,128]{2,1,0:T(8,128)} %broadcast_in_dim.4), calls=%async_computation.1 | async-start | bytes 131072 | tf_op jit(solution)/shard_map/all_to_all | solution.py:347
  92.8 1.0 copy-start
  94.1 0.8 copy-start.1
  100.0 17.9 %collective-permute-start.6 = (f32[2,512,128]{2,1,0:T(8,128)}, f32[2,512,128]{2,1,0:T(8,128)S(1)}, u32[]{:S(2)}, u32[]{:S(2)}) collective-permute-start(f32[2,512,128]{2,1,0:T(8,128)} %copy-done.1), channel_id=1, source_target_pairs={{0,1},{1,2},{2,3},{3,4},{4,5},{5,6},{6,7},{7,8},{8,9},{9,10},{10,1... | collective-permute-start | bytes 1572872 | tf_op jit(solution)/shard_map/ppermute | solution.py:469

commit v2 on v0

--- a/solution.py
+++ b/solution.py
@@ -219,7 +219,7 @@
     stores = copies_of(
         [(probe_sum, probe_out)]
         + [(grad.at[t], a) for t, a in enumerate(by_tiles(g_own, tiles))]
-        + [(grad.at[tiles], g_right)],
+        + [(grad.at[tiles], g_right.at[:, pl.ds(0, rows), :])],
         sems,
     )
     start_all(stores)
@@ -227,7 +227,7 @@
 
 
 def lower_kernel(scale, pos, count, own, right, below, corner, photons, probe_in, waves_in, own_in, right_in, sum_in,
-                 g_own, g_right, g_below, probe_out,
+                 g_own, g_right, g_first, g_rest, probe_out,
                  field, grad, photon_buf, probe, waves, plus_ref, minus_ref, probe_sum, listed, sems, photon_sems):
     rows, cols = own.shape[1], own.shape[2]
     tiles = cols // PATCH
@@ -256,34 +256,36 @@
     probe_sum[...] = probe_sum[...] * scale
     stores = copies_of(
         [(probe_sum, probe_out)]
-        + [(grad.at[t, :, lower, :], a) for t, a in enumerate(by_tiles(g_below, tiles + 1))]
-        + [(grad.at[t, :, upper, :], a) for t, a in enumerate(last_rows(g_own) + [g_right.at[:, last, :]])],
+        + [(grad.at[t, :, lower, :], a) for t, a in enumerate([g_first] + by_tiles(g_rest, tiles - 1))]
+        + [(grad.at[t, :, upper, :], a) for t, a in enumerate(last_rows(g_own))]
+        + [(grad.at[tiles], g_right.at[:, pl.ds(base, 2 * PATCH), :])],
         sems,
     )
     start_all(stores)
     wait_all(stores)
 
 
-def corner_kernel(right_in, above, right, rim_buf, corner_buf, sems):
-    rows = right.at[:, pl.ds(0, PATCH), :]
-    corner = above.at[:, :, pl.ds(above.shape[2] - PATCH, PATCH)]
-    loads = copies_of([(rows, rim_buf), (corner, corner_buf)], sems)
+def corner_kernel(first, left, total, rim_buf, corner_buf, sems):
+    corner = left.at[:, pl.ds(left.shape[1] - PATCH, PATCH), :]
+    loads = copies_of([(first, rim_buf), (corner, corner_buf)], sems)
     start_all(loads)
     wait_all(loads)
     rim_buf[...] += corner_buf[...]
-    store = pltpu.make_async_copy(rim_buf, rows, sems.at[0])
+    store = pltpu.make_async_copy(rim_buf, total, sems.at[0])
     store.start()
     store.wait()
 
 
-def seam_kernel(grad_in, above, left, parts, grad, probe,
+def seam_kernel(grad_in, above_first, above_rest, left, parts, grad, probe,
                 top_buf, left_buf, above_buf, beside_buf, probe_buf, sems):
     rows, cols = grad.shape[1], grad.shape[2]
     rest = rows - PATCH
     top_rim = grad.at[:, pl.ds(0, PATCH), :]
     left_rim = grad.at[:, pl.ds(PATCH, rest), pl.ds(0, PATCH)]
     loads = copies_of(
-        [(top_rim, top_buf), (left_rim, left_buf), (above.at[:, :, pl.ds(0, cols)], above_buf), (left, beside_buf),
+        [(top_rim, top_buf), (left_rim, left_buf), (left.at[:, pl.ds(0, rows), :], beside_buf),
+         (above_first, above_buf.at[:, :, pl.ds(0, PATCH)]),
+         (above_rest, above_buf.at[:, :, pl.ds(PATCH, cols - PATCH)]),
          (parts, probe_buf)],
         sems,
     )
@@ -368,7 +370,7 @@
             pltpu.SemaphoreType.DMA((slot_count,)),
         ]
 
-    own_shape, right_shape, probe_shape = shape(2, rows, cols), shape(2, rows, PATCH), shape(*probe_modes.shape)
+    own_shape, right_shape, probe_shape = shape(2, rows, cols), shape(2, rows + PATCH, PATCH), shape(*probe_modes.shape)
     g_own, g_right, probe_1 = pl.pallas_call(
         upper_kernel,
         out_shape=(own_shape, right_shape, probe_shape),
@@ -379,11 +381,12 @@
         cost_estimate=pl.CostEstimate(flops=10**9, bytes_accessed=2**20, transcendentals=0),
         name="upper_slots",
     )(pos, count, object_field, right, photon_rows, probe_modes, waves)
-    g_own, g_right, g_below, probe_2 = pl.pallas_call(
+    rim_shape = shape(2, PATCH, PATCH)
+    g_own, g_right, g_first, g_rest, probe_2 = pl.pallas_call(
         functools.partial(lower_kernel, scale),
-        out_shape=(own_shape, right_shape, shape(2, PATCH, cols + PATCH), probe_shape),
+        out_shape=(own_shape, right_shape, rim_shape, shape(2, PATCH, cols - PATCH), probe_shape),
         in_specs=[smem] * 2 + [hbm] * 10,
-        out_specs=(hbm,) * 4,
+        out_specs=(hbm,) * 5,
         scratch_shapes=scratch(2 * PATCH),
         input_output_aliases={9: 0, 10: 1},
         compiler_params=params,
@@ -392,13 +395,14 @@
     )(pos, count, object_field, right, below, corner, photon_rows, probe_modes, waves, g_own, g_right, probe_1)
 
     plane, depth = lax.axis_size(PLANE), lax.axis_size(DEPTH)
-    above = lax.ppermute(g_below, ROW, down)
+    left = lax.ppermute(g_right, COL, along)
+    above_rest = lax.ppermute(g_rest, ROW, down)
     shares = lax.all_to_all(probe_2.reshape(plane, -1, PATCH), PLANE, 0, 0, tiled=True)
     share = jnp.sum(shares, axis=0)
-    share = jnp.sum(everyone(share, DEPTH, depth), axis=0)
-    g_right = pl.pallas_call(
+    share, left = lax.optimization_barrier((share, left))
+    g_first = pl.pallas_call(
         corner_kernel,
-        out_shape=right_shape,
+        out_shape=rim_shape,
         in_specs=[hbm, hbm],
         out_specs=hbm,
         scratch_shapes=[
@@ -406,18 +410,19 @@
             pltpu.VMEM((2, PATCH, PATCH), F32),
             pltpu.SemaphoreType.DMA((2,)),
         ],
-        input_output_aliases={0: 0},
         compiler_params=small,
         name="corner",
-    )(g_right, above)
-    share, g_right = lax.optimization_barrier((share, g_right))
-    left = lax.ppermute(g_right, COL, along)
+    )(g_first, left)
+    share, g_first = lax.optimization_barrier((share, g_first))
+    above_first = lax.ppermute(g_first, ROW, down)
+    share = jnp.sum(everyone(share, DEPTH, depth), axis=0)
+    share, above_first, above_rest = lax.optimization_barrier((share, above_first, above_rest))
     parts = everyone(share, PLANE, plane)
 
     object_gradient, probe_gradient = pl.pallas_call(
         seam_kernel,
         out_shape=(own_shape, shape(*parts.shape)),
-        in_specs=[hbm] * 4,
+        in_specs=[hbm] * 5,
         out_specs=(hbm, hbm),
         scratch_shapes=[
             pltpu.VMEM((2, PATCH, cols), F32),
@@ -425,12 +430,12 @@
             pltpu.VMEM((2, PATCH, cols), F32),
             pltpu.VMEM((2, rows, PATCH), F32),
             pltpu.VMEM(parts.shape, F32),
-            pltpu.SemaphoreType.DMA((5,)),
+            pltpu.SemaphoreType.DMA((6,)),
         ],
         input_output_aliases={0: 0},
         compiler_params=small,
         name="seams",
-    )(g_own, above, left, parts)
+    )(g_own, above_first, above_rest, left, parts)
     return (object_gradient, probe_gradient.reshape(probe_modes.shape))
 
 

time: 112 us -> 114 us (1.018)
  starting transfers between devices: 19.8 us -> 21.8 us
  waiting for transfers between devices: 23 us -> 21.6 us
    ppermute x1 -> x2, starting transfers between devices: 8.16 us -> 10.9 us  [the longest x1 8.03 us: body(): above_rest = lax.ppermute(g_rest, ROW, down)]
    ppermute x1, waiting for transfers between devices: 21.3 us -> 20 us  [body(): corner = lax.ppermute(corner, BOTH, diagonal_back)]
    pallas_call x1, Pallas kernels: 7.25 us -> 8.63 us  [body(): pl.pallas_call(upper_kernel, out_shape=(own_shape, right_shape, probe_sha...]
    pallas_call x1, Pallas kernels: 1.58 us -> 0.42 us  [body(): pl.pallas_call(corner_kernel, out_shape=rim_shape, in_specs=[hbm, hbm], o...]
    unnamed x4 -> x6, local copies, waits for them, and re-layouts: 1.43 us -> 2.34 us
  transfers between devices with their start and end apart: 5 -> 6, of which waited for: 2 -> 2; matrix products, arithmetic and copies ran while one was open for 0% -> 0% of each run, Pallas kernels for 8% -> 10%
where the time goes in v2:
time: 114 us; the launch traced here: 113 us
  blocking collectives  44.7 us (39%)
  starting transfers between devices  21.8 us (19%)
  waiting for transfers between devices  21.6 us (19%)
  Pallas kernels  20.7 us (18%)
  local copies, waits for them, and re-layouts  2.37 us (2%)
  between operations  1.42 us (1%)
    all_to_all x2, blocking collectives, everyone(): return lax.all_to_all(sent, axes, 0, 0, tiled=True)  28.9 us
    ppermute x1, waiting for transfers between devices, body(): corner = lax.ppermute(corner, BOTH, diagonal_back)  20 us
    all_to_all x1, blocking collectives, body(): lax.all_to_all(probe_2.reshape(plane, -1, PATCH), PLANE, 0, 0, tiled=True)  15.8 us
    pallas_call x1, Pallas kernels, body(): pl.pallas_call(upper_kernel, out_shape=(own_shape, right_shape, probe_sha...  8.63 us
    ppermute x1, starting transfers between devices, body(): above_rest = lax.ppermute(g_rest, ROW, down)  8.03 us
    pallas_call x1, Pallas kernels, body(): pl.pallas_call(functools.partial(lower_kernel, scale), out_shape=(own_sha...  5.64 us
    ppermute x1, starting transfers between devices, body(): right = lax.ppermute(right, COL, back)  5.15 us
    ppermute x1, starting transfers between devices, body(): left = lax.ppermute(g_right, COL, along)  3.24 us
  transfers between devices with their start and end apart: 6, of which 2 were waited for; matrix products, arithmetic and copies ran while one was open for 0% of the time, Pallas kernels for 10%

profile of v2, /device:TPU:1, one launch (start us, length us, event | category | flops | bytes accessed | tf_op | source)
XLA Modules:
  0.0 112.7 jit_solution(3033556838997322442)
XLA Ops:
  0.6 1.8 %right_rim.1.after = f32[2,512,128]{2,1,0:T(8,128)} custom-call(f32[2,512,512]{2,1,0:T(8,128)} %own.7), custom_call_target="tpu_custom_call" | custom-call | tf_op jit(solution)/shard_map/right_rim/pallas_call | solution.py:336
  2.5 5.1 %collective-permute-start = (f32[2,512,128]{2,1,0:T(8,128)}, f32[2,512,128]{2,1,0:T(8,128)S(1)}, u32[]{:S(2)}, u32[]{:S(2)}) collective-permute-start(f32[2,512,128]{2,1,0:T(8,128)} %right_rim.1.after), channel_id=1, source_target_pairs={{1,0},{2,1},{3,2},{4,3},{5,4},{6,5},{7,6},{8,7},{9,8},{10,9},{11,1... | collective-permute-start | bytes 1572872 | tf_op jit(solution)/shard_map/ppermute | solution.py:355
  7.6 1.9 %below_rim.1 = (f32[2,128,512]{2,1,0:T(8,128)}, f32[2,128,128]{2,1,0:T(8,128)}) custom-call(f32[2,512,512]{2,1,0:T(8,128)} %own.7, f32[2,512,128]{2,1,0:T(8,128)} %right_rim.1.after), custom_call_target="tpu_custom_call" | custom-call | tf_op jit(solution)/shard_map/below_rim/pallas_call | solution.py:345
  9.6 1.3 %collective-permute-start.1 = (f32[2,128,512]{2,1,0:T(8,128)}, f32[2,128,512]{2,1,0:T(8,128)}, u32[]{:S(2)}, u32[]{:S(2)}) collective-permute-start(f32[2,128,512]{2,1,0:T(8,128)} %get-tuple-element.21), channel_id=1, source_target_pairs={{64,0},{128,64},{192,128},{65,1},{129,65},{193,129},{66,2},{130,66... | collective-permute-start | bytes 1572872 | tf_op jit(solution)/shard_map/ppermute | solution.py:354
  10.9 1.3 %collective-permute-start.2 = (f32[2,128,128]{2,1,0:T(8,128)}, f32[2,128,128]{2,1,0:T(8,128)S(1)}, u32[]{:S(2)}, u32[]{:S(2)}) collective-permute-start(f32[2,128,128]{2,1,0:T(8,128)} %get-tuple-element.22), channel_id=1, source_target_pairs={{65,0},{66,1},{67,2},{68,3},{69,4},{70,5},{71,6},{72,7},{73,8},{74... | collective-permute-start | bytes 393224 | tf_op jit(solution)/shard_map/ppermute | solution.py:356
  12.8 1.7 %collective-permute-done.right = f32[2,512,128]{2,1,0:T(8,128)S(1)} collective-permute-done((f32[2,512,128]{2,1,0:T(8,128)}, f32[2,512,128]{2,1,0:T(8,128)S(1)}, u32[]{:S(2)}, u32[]{:S(2)}) %collective-permute-start) | collective-permute-done | bytes 524320 | tf_op jit(solution)/shard_map/ppermute | solution.py:355
  14.5 0.0 copy-start.1
  14.5 0.8 copy-done.1
  15.3 8.6 %upper_slots.1 = (f32[2,512,512]{2,1,0:T(8,128)}, f32[2,640,128]{2,1,0:T(8,128)}, f32[2,2,128,128]{3,2,1,0:T(8,128)}) custom-call(s32[2,64]{1,0:T(2,128)} %bitcast.12, s32[1]{0:T(128)} %bitcast.7.count, f32[2,512,512]{2,1,0:T(8,128)} %own.7, f32[2,512,128]{2,1,0:T(8,128)} %copy-done.1, bf16[64,128,128]{2,1,0:T(8,128)(2,1)} %bitcast.9, ...), custom_call_target="tpu_custom_call" | custom-call | flops 1000000000 | bytes 1048576 | tf_op jit(solution)/shard_map/upper_slots/pallas_call | solution.py:374
  23.9 20.0 %collective-permute-done.2.corner = f32[2,128,128]{2,1,0:T(8,128)S(1)} collective-permute-done((f32[2,128,128]{2,1,0:T(8,128)}, f32[2,128,128]{2,1,0:T(8,128)S(1)}, u32[]{:S(2)}, u32[]{:S(2)}) %collective-permute-start.2) | collective-permute-done | bytes 131104 | tf_op jit(solution)/shard_map/ppermute | solution.py:356
  43.9 0.0 copy-start.2
  43.9 0.0 collective-permute-done.1.below
  43.9 0.6 copy-done.2
  44.5 5.6 %lower_slots.1 = (f32[2,512,512]{2,1,0:T(8,128)}, f32[2,640,128]{2,1,0:T(8,128)}, f32[2,128,128]{2,1,0:T(8,128)}, f32[2,128,384]{2,1,0:T(8,128)}, f32[2,2,128,128]{3,2,1,0:T(8,128)}) custom-call(s32[2,64]{1,0:T(2,128)} %bitcast.13, s32[1]{0:T(128)} %bitcast.8.count, f32[2,512,512]{2,1,0:T(8,128)} %own.7, ...), custom_call_target="tpu_custom_call", output_to_operand_aliasing={{0}: (9, {}), {1}: (10, {})} | custom-call | flops 1000000000 | bytes 1048576 | tf_op jit(solution)/shard_map/lower_slots/pallas_call | solution.py:385
  50.2 3.2 %collective-permute-start.3 = (f32[2,640,128]{2,1,0:T(8,128)}, f32[2,640,128]{2,1,0:T(8,128)S(1)}, u32[]{:S(2)}, u32[]{:S(2)}) collective-permute-start(f32[2,640,128]{2,1,0:T(8,128)} %get-tuple-element.28), channel_id=1, source_target_pairs={{0,1},{1,2},{2,3},{3,4},{4,5},{5,6},{6,7},{7,8},{8,9},{9,10},{10,1... | collective-permute-start | bytes 1966088 | tf_op jit(solution)/shard_map/ppermute | solution.py:398
  53.4 8.0 %collective-permute-start.5 = (f32[2,128,384]{2,1,0:T(8,128)}, f32[2,128,384]{2,1,0:T(8,128)S(1)}, u32[]{:S(2)}, u32[]{:S(2)}) collective-permute-start(f32[2,128,384]{2,1,0:T(8,128)} %get-tuple-element.34), channel_id=1, source_target_pairs={{0,64},{64,128},{128,192},{1,65},{65,129},{129,193},{2,66},{66,130... | collective-permute-start | bytes 1179656 | tf_op jit(solution)/shard_map/ppermute | solution.py:399
  61.5 15.8 %all_to_all.15 = f32[32,16,128]{2,1,0:T(8,128)S(1)} all-to-all(f32[32,16,128]{2,1,0:T(8,128)} %bitcast.11), channel_id=1, replica_groups=mesh['z_hi'=4,'x'=4,'y'=4,'z_lo'=2,'core'=2] {'x','y','core'}, dimensions={0} | all-to-all | bytes 524288 | tf_op jit(solution)/shard_map/all_to_all | solution.py:400
  77.3 0.0 collective-permute-done.3.left
  77.3 0.0 copy-start
  77.3 0.9 copy-done
  78.2 0.4 corner.1
  78.7 2.8 %collective-permute-start.4 = (f32[2,128,128]{2,1,0:T(8,128)S(1)}, f32[2,128,128]{2,1,0:T(8,128)S(1)}, u32[]{:S(2)}, u32[]{:S(2)}) collective-permute-start(f32[2,128,128]{2,1,0:T(8,128)S(1)} %corner.1), channel_id=1, source_target_pairs={{0,64},{64,128},{128,192},{1,65},{65,129},{129,193},{2,66},{66,130... | collective-permute-start | bytes 393224 | tf_op jit(solution)/shard_map/ppermute | solution.py:417
  81.5 11.3 %all_to_all.16 = f32[8,16,128]{2,1,0:T(8,128)S(1)} all-to-all(f32[8,16,128]{2,1,0:T(8,128)S(1)} %broadcast_in_dim.4), channel_id=1, replica_groups=mesh['z_hi'=4,'x'=4,'y'=4,'z_lo'=2,'core'=2] {'z_hi','z_lo'}, dimensions={0} | all-to-all | bytes 131072 | tf_op jit(solution)/shard_map/all_to_all | solution.py:311
  92.8 0.0 collective-permute-done.5.above_rest
  92.9 0.0 collective-permute-done.4.above_first
  92.9 17.6 %all_to_all.17.parts = f32[32,16,128]{2,1,0:T(8,128)S(1)} all-to-all(f32[32,16,128]{2,1,0:T(8,128)S(1)} %broadcast_in_dim.5), channel_id=1, replica_groups=mesh['z_hi'=4,'x'=4,'y'=4,'z_lo'=2,'core'=2] {'x','y','core'}, dimensions={0} | all-to-all | bytes 524288 | tf_op jit(solution)/shard_map/all_to_all | solution.py:311
  110.5 2.2 %seams.1 = (f32[2,512,512]{2,1,0:T(8,128)}, f32[32,16,128]{2,1,0:T(8,128)}) custom-call(f32[2,512,512]{2,1,0:T(8,128)} %get-tuple-element.26.grad_in, f32[2,128,128]{2,1,0:T(8,128)S(1)} %collective-permute-done.4.above_first, f32[2,128,384]{2,1,0:T(8,128)S(1)} %collective-permute-done.5.above_rest, ...), custom_call_target="tpu_custom_call", output_to_operand_aliasing={{0}: (0, {})} | custom-call | tf_op jit(solution)/shard_map/seams/pallas_call | solution.py:422
  (4 shorter events, 0.1 us)
Async XLA Ops:
  2.5 12.0 %collective-permute-start = (f32[2,512,128]{2,1,0:T(8,128)}, f32[2,512,128]{2,1,0:T(8,128)S(1)}, u32[]{:S(2)}, u32[]{:S(2)}) collective-permute-start(f32[2,512,128]{2,1,0:T(8,128)} %right_rim.1.after), channel_id=1, source_target_pairs={{1,0},{2,1},{3,2},{4,3},{5,4},{6,5},{7,6},{8,7},{9,8},{10,9},{11,1... | collective-permute-start | bytes 1572872 | tf_op jit(solution)/shard_map/ppermute | solution.py:355
  9.6 34.3 %collective-permute-start.1 = (f32[2,128,512]{2,1,0:T(8,128)}, f32[2,128,512]{2,1,0:T(8,128)}, u32[]{:S(2)}, u32[]{:S(2)}) collective-permute-start(f32[2,128,512]{2,1,0:T(8,128)} %get-tuple-element.21), channel_id=1, source_target_pairs={{64,0},{128,64},{192,128},{65,1},{129,65},{193,129},{66,2},{130,66... | collective-permute-start | bytes 1572872 | tf_op jit(solution)/shard_map/ppermute | solution.py:354
  10.9 33.0 %collective-permute-start.2 = (f32[2,128,128]{2,1,0:T(8,128)}, f32[2,128,128]{2,1,0:T(8,128)S(1)}, u32[]{:S(2)}, u32[]{:S(2)}) collective-permute-start(f32[2,128,128]{2,1,0:T(8,128)} %get-tuple-element.22), channel_id=1, source_target_pairs={{65,0},{66,1},{67,2},{68,3},{69,4},{70,5},{71,6},{72,7},{73,8},{74... | collective-permute-start | bytes 393224 | tf_op jit(solution)/shard_map/ppermute | solution.py:356
  14.5 0.8 copy-start.1
  43.9 0.7 copy-start.2
  50.2 27.1 %collective-permute-start.3 = (f32[2,640,128]{2,1,0:T(8,128)}, f32[2,640,128]{2,1,0:T(8,128)S(1)}, u32[]{:S(2)}, u32[]{:S(2)}) collective-permute-start(f32[2,640,128]{2,1,0:T(8,128)} %get-tuple-element.28), channel_id=1, source_target_pairs={{0,1},{1,2},{2,3},{3,4},{4,5},{5,6},{6,7},{7,8},{8,9},{9,10},{10,1... | collective-permute-start | bytes 1966088 | tf_op jit(solution)/shard_map/ppermute | solution.py:398
  53.4 39.4 %collective-permute-start.5 = (f32[2,128,384]{2,1,0:T(8,128)}, f32[2,128,384]{2,1,0:T(8,128)S(1)}, u32[]{:S(2)}, u32[]{:S(2)}) collective-permute-start(f32[2,128,384]{2,1,0:T(8,128)} %get-tuple-element.34), channel_id=1, source_target_pairs={{0,64},{64,128},{128,192},{1,65},{65,129},{129,193},{2,66},{66,130... | collective-permute-start | bytes 1179656 | tf_op jit(solution)/shard_map/ppermute | solution.py:399
  77.3 0.9 copy-start
  78.7 14.2 %collective-permute-start.4 = (f32[2,128,128]{2,1,0:T(8,128)S(1)}, f32[2,128,128]{2,1,0:T(8,128)S(1)}, u32[]{:S(2)}, u32[]{:S(2)}) collective-permute-start(f32[2,128,128]{2,1,0:T(8,128)S(1)} %corner.1), channel_id=1, source_target_pairs={{0,64},{64,128},{128,192},{1,65},{65,129},{129,193},{2,66},{66,130... | collective-permute-start | bytes 393224 | tf_op jit(solution)/shard_map/ppermute | solution.py:417

commit v3 on v2

--- a/solution.py
+++ b/solution.py
@@ -276,8 +276,7 @@
     store.wait()
 
 
-def seam_kernel(grad_in, above_first, above_rest, left, parts, grad, probe,
-                top_buf, left_buf, above_buf, beside_buf, probe_buf, sems):
+def seam_kernel(grad_in, above_first, above_rest, left, grad, top_buf, left_buf, above_buf, beside_buf, sems):
     rows, cols = grad.shape[1], grad.shape[2]
     rest = rows - PATCH
     top_rim = grad.at[:, pl.ds(0, PATCH), :]
@@ -285,21 +284,17 @@
     loads = copies_of(
         [(top_rim, top_buf), (left_rim, left_buf), (left.at[:, pl.ds(0, rows), :], beside_buf),
          (above_first, above_buf.at[:, :, pl.ds(0, PATCH)]),
-         (above_rest, above_buf.at[:, :, pl.ds(PATCH, cols - PATCH)]),
-         (parts, probe_buf)],
+         (above_rest, above_buf.at[:, :, pl.ds(PATCH, cols - PATCH)])],
         sems,
     )
     start_all(loads)
     wait_all(loads)
-    join = pltpu.make_async_copy(probe_buf, probe, sems.at[2])
-    join.start()
     top_buf[:, :, PATCH:] += above_buf[:, :, PATCH:]
     top_buf[:, :, :PATCH] += above_buf[:, :, :PATCH] + beside_buf[:, :PATCH, :]
     left_buf[...] += beside_buf[:, PATCH:, :]
     stores = copies_of([(top_buf, top_rim), (left_buf, left_rim)], sems)
     start_all(stores)
     wait_all(stores)
-    join.wait()
 
 
 def shape(*dims):
@@ -399,7 +394,6 @@
     above_rest = lax.ppermute(g_rest, ROW, down)
     shares = lax.all_to_all(probe_2.reshape(plane, -1, PATCH), PLANE, 0, 0, tiled=True)
     share = jnp.sum(shares, axis=0)
-    share, left = lax.optimization_barrier((share, left))
     g_first = pl.pallas_call(
         corner_kernel,
         out_shape=rim_shape,
@@ -419,24 +413,24 @@
     share, above_first, above_rest = lax.optimization_barrier((share, above_first, above_rest))
     parts = everyone(share, PLANE, plane)
 
-    object_gradient, probe_gradient = pl.pallas_call(
+    object_gradient = pl.pallas_call(
         seam_kernel,
-        out_shape=(own_shape, shape(*parts.shape)),
-        in_specs=[hbm] * 5,
-        out_specs=(hbm, hbm),
+        out_shape=own_shape,
+        in_specs=[hbm] * 4,
+        out_specs=hbm,
         scratch_shapes=[
             pltpu.VMEM((2, PATCH, cols), F32),
             pltpu.VMEM((2, rows - PATCH, PATCH), F32),
             pltpu.VMEM((2, PATCH, cols), F32),
             pltpu.VMEM((2, rows, PATCH), F32),
-            pltpu.VMEM(parts.shape, F32),
-            pltpu.SemaphoreType.DMA((6,)),
+            pltpu.SemaphoreType.DMA((5,)),
         ],
         input_output_aliases={0: 0},
         compiler_params=small,
+        cost_estimate=pl.CostEstimate(flops=10**9, bytes_accessed=2**20, transcendentals=0),
         name="seams",
-    )(g_own, above_first, above_rest, left, parts)
-    return (object_gradient, probe_gradient.reshape(probe_modes.shape))
+    )(g_own, above_first, above_rest, left)
+    return (object_gradient, parts.reshape(probe_modes.shape))
 
 
 def solution(mesh):

time: 114 us -> 114 us (level)
  blocking collectives: 44.7 us -> 29.8 us
  waiting for transfers between devices: 21.6 us -> 29.9 us
  starting transfers between devices: 21.8 us -> 28.5 us
  Pallas kernels: 20.7 us -> 19.2 us
  local copies, waits for them, and re-layouts: 2.37 us -> 3.79 us
    all_to_all x2 -> x1, blocking collectives: 28.9 us -> 9.75 us  [everyone(): return lax.all_to_all(sent, axes, 0, 0, tiled=True)]
    all_to_all x0 -> x1, starting transfers between devices: none -> 10.1 us  [everyone(): return lax.all_to_all(sent, axes, 0, 0, tiled=True)]
    all_to_all x0 -> x1, waiting for transfers between devices: none -> 6.76 us  [everyone(): return lax.all_to_all(sent, axes, 0, 0, tiled=True)]
    all_to_all x1, blocking collectives: 15.8 us -> 20 us  [body(): lax.all_to_all(probe_2.reshape(plane, -1, PATCH), PLANE, 0, 0, tiled=True)]
    ppermute x1, starting transfers between devices: 8.03 us -> 5.82 us  [body(): above_rest = lax.ppermute(g_rest, ROW, down)]
    pallas_call x1, Pallas kernels: 8.63 us -> 7.18 us  [body(): pl.pallas_call(upper_kernel, out_shape=(own_shape, right_shape, probe_sha...]
    ppermute x1, waiting for transfers between devices: 20 us -> 21.4 us  [body(): corner = lax.ppermute(corner, BOTH, diagonal_back)]
    ppermute x1, starting transfers between devices: 2.82 us -> 1.62 us  [body(): above_first = lax.ppermute(g_first, ROW, down)]
  transfers between devices with their start and end apart: 6 -> 7, of which waited for: 2 -> 3; matrix products, arithmetic and copies ran while one was open for 0% -> 0% of each run, Pallas kernels for 10% -> 10%
where the time goes in v3:
time: 114 us; the launch traced here: 113 us
  waiting for transfers between devices  29.9 us (26%)
  blocking collectives  29.8 us (26%)
  starting transfers between devices  28.5 us (25%)
  Pallas kernels  19.2 us (17%)
  local copies, waits for them, and re-layouts  3.79 us (3%)
  between operations  1.43 us (1%)
    ppermute x1, waiting for transfers between devices, body(): corner = lax.ppermute(corner, BOTH, diagonal_back)  21.4 us
    all_to_all x1, blocking collectives, body(): lax.all_to_all(probe_2.reshape(plane, -1, PATCH), PLANE, 0, 0, tiled=True)  20 us
    all_to_all x1, starting transfers between devices, everyone(): return lax.all_to_all(sent, axes, 0, 0, tiled=True)  10.1 us
    all_to_all x1, blocking collectives, everyone(): return lax.all_to_all(sent, axes, 0, 0, tiled=True)  9.75 us
    pallas_call x1, Pallas kernels, body(): pl.pallas_call(upper_kernel, out_shape=(own_shape, right_shape, probe_sha...  7.18 us
    all_to_all x1, waiting for transfers between devices, everyone(): return lax.all_to_all(sent, axes, 0, 0, tiled=True)  6.76 us
    ppermute x1, starting transfers between devices, body(): above_rest = lax.ppermute(g_rest, ROW, down)  5.82 us
    pallas_call x1, Pallas kernels, body(): pl.pallas_call(functools.partial(lower_kernel, scale), out_shape=(own_sha...  5.66 us
  transfers between devices with their start and end apart: 7, of which 3 were waited for; matrix products, arithmetic and copies ran while one was open for 0% of the time, Pallas kernels for 10%

profile of v3, /device:TPU:1, one launch (start us, length us, event | category | flops | bytes accessed | tf_op | source)
XLA Modules:
  0.0 112.6 jit_solution(16836375395861758111)
XLA Ops:
  0.6 1.8 %right_rim.1.after = f32[2,512,128]{2,1,0:T(8,128)} custom-call(f32[2,512,512]{2,1,0:T(8,128)} %own.7), custom_call_target="tpu_custom_call" | custom-call | tf_op jit(solution)/shard_map/right_rim/pallas_call | solution.py:331
  2.5 5.1 %collective-permute-start = (f32[2,512,128]{2,1,0:T(8,128)}, f32[2,512,128]{2,1,0:T(8,128)S(1)}, u32[]{:S(2)}, u32[]{:S(2)}) collective-permute-start(f32[2,512,128]{2,1,0:T(8,128)} %right_rim.1.after), channel_id=1, source_target_pairs={{1,0},{2,1},{3,2},{4,3},{5,4},{6,5},{7,6},{8,7},{9,8},{10,9},{11,1... | collective-permute-start | bytes 1572872 | tf_op jit(solution)/shard_map/ppermute | solution.py:350
  7.6 1.9 %below_rim.1 = (f32[2,128,512]{2,1,0:T(8,128)}, f32[2,128,128]{2,1,0:T(8,128)}) custom-call(f32[2,512,512]{2,1,0:T(8,128)} %own.7, f32[2,512,128]{2,1,0:T(8,128)} %right_rim.1.after), custom_call_target="tpu_custom_call" | custom-call | tf_op jit(solution)/shard_map/below_rim/pallas_call | solution.py:340
  9.5 1.3 %collective-permute-start.1 = (f32[2,128,512]{2,1,0:T(8,128)}, f32[2,128,512]{2,1,0:T(8,128)}, u32[]{:S(2)}, u32[]{:S(2)}) collective-permute-start(f32[2,128,512]{2,1,0:T(8,128)} %get-tuple-element.17), channel_id=1, source_target_pairs={{64,0},{128,64},{192,128},{65,1},{129,65},{193,129},{66,2},{130,66... | collective-permute-start | bytes 1572872 | tf_op jit(solution)/shard_map/ppermute | solution.py:349
  10.8 1.3 %collective-permute-start.2 = (f32[2,128,128]{2,1,0:T(8,128)}, f32[2,128,128]{2,1,0:T(8,128)S(1)}, u32[]{:S(2)}, u32[]{:S(2)}) collective-permute-start(f32[2,128,128]{2,1,0:T(8,128)} %get-tuple-element.18), channel_id=1, source_target_pairs={{65,0},{66,1},{67,2},{68,3},{69,4},{70,5},{71,6},{72,7},{73,8},{74... | collective-permute-start | bytes 393224 | tf_op jit(solution)/shard_map/ppermute | solution.py:351
  12.8 1.7 %collective-permute-done.right = f32[2,512,128]{2,1,0:T(8,128)S(1)} collective-permute-done((f32[2,512,128]{2,1,0:T(8,128)}, f32[2,512,128]{2,1,0:T(8,128)S(1)}, u32[]{:S(2)}, u32[]{:S(2)}) %collective-permute-start) | collective-permute-done | bytes 524320 | tf_op jit(solution)/shard_map/ppermute | solution.py:350
  14.5 0.0 copy-start.1
  14.5 0.8 copy-done.1
  15.3 7.2 %upper_slots.1 = (f32[2,512,512]{2,1,0:T(8,128)}, f32[2,640,128]{2,1,0:T(8,128)}, f32[2,2,128,128]{3,2,1,0:T(8,128)}) custom-call(s32[2,64]{1,0:T(2,128)} %bitcast.13, s32[1]{0:T(128)} %bitcast.7.count, f32[2,512,512]{2,1,0:T(8,128)} %own.7, f32[2,512,128]{2,1,0:T(8,128)} %copy-done.1, bf16[64,128,128]{2,1,0:T(8,128)(2,1)} %bitcast.9, ...), custom_call_target="tpu_custom_call" | custom-call | flops 1000000000 | bytes 1048576 | tf_op jit(solution)/shard_map/upper_slots/pallas_call | solution.py:369
  22.5 21.4 %collective-permute-done.2.corner = f32[2,128,128]{2,1,0:T(8,128)S(1)} collective-permute-done((f32[2,128,128]{2,1,0:T(8,128)}, f32[2,128,128]{2,1,0:T(8,128)S(1)}, u32[]{:S(2)}, u32[]{:S(2)}) %collective-permute-start.2) | collective-permute-done | bytes 131104 | tf_op jit(solution)/shard_map/ppermute | solution.py:351
  43.9 0.0 copy-start.2
  43.9 0.0 collective-permute-done.1.below
  43.9 0.7 copy-done.2
  44.5 5.7 %lower_slots.1 = (f32[2,512,512]{2,1,0:T(8,128)}, f32[2,640,128]{2,1,0:T(8,128)}, f32[2,128,128]{2,1,0:T(8,128)}, f32[2,128,384]{2,1,0:T(8,128)}, f32[2,2,128,128]{3,2,1,0:T(8,128)}) custom-call(s32[2,64]{1,0:T(2,128)} %bitcast.14, s32[1]{0:T(128)} %bitcast.8.count, f32[2,512,512]{2,1,0:T(8,128)} %own.7, ...), custom_call_target="tpu_custom_call", output_to_operand_aliasing={{0}: (9, {}), {1}: (10, {})} | custom-call | flops 1000000000 | bytes 1048576 | tf_op jit(solution)/shard_map/lower_slots/pallas_call | solution.py:380
  50.2 3.2 %collective-permute-start.3 = (f32[2,640,128]{2,1,0:T(8,128)}, f32[2,640,128]{2,1,0:T(8,128)S(1)}, u32[]{:S(2)}, u32[]{:S(2)}) collective-permute-start(f32[2,640,128]{2,1,0:T(8,128)} %get-tuple-element.25), channel_id=1, source_target_pairs={{0,1},{1,2},{2,3},{3,4},{4,5},{5,6},{6,7},{7,8},{8,9},{9,10},{10,1... | collective-permute-start | bytes 1966088 | tf_op jit(solution)/shard_map/ppermute | solution.py:393
  53.4 5.8 %collective-permute-start.5 = (f32[2,128,384]{2,1,0:T(8,128)}, f32[2,128,384]{2,1,0:T(8,128)S(1)}, u32[]{:S(2)}, u32[]{:S(2)}) collective-permute-start(f32[2,128,384]{2,1,0:T(8,128)} %get-tuple-element.28), channel_id=1, source_target_pairs={{0,64},{64,128},{128,192},{1,65},{65,129},{129,193},{2,66},{66,130... | collective-permute-start | bytes 1179656 | tf_op jit(solution)/shard_map/ppermute | solution.py:394
  59.3 20.0 %all_to_all.15 = f32[32,16,128]{2,1,0:T(8,128)S(1)} all-to-all(f32[32,16,128]{2,1,0:T(8,128)} %bitcast.12), channel_id=1, replica_groups=mesh['z_hi'=4,'x'=4,'y'=4,'z_lo'=2,'core'=2] {'x','y','core'}, dimensions={0} | all-to-all | bytes 524288 | tf_op jit(solution)/shard_map/all_to_all | solution.py:395
  79.3 0.0 collective-permute-done.3.left
  79.4 0.0 copy-start
  79.4 0.9 copy-done
  80.3 0.4 corner.1
  80.7 1.6 %collective-permute-start.4 = (f32[2,128,128]{2,1,0:T(8,128)S(1)}, f32[2,128,128]{2,1,0:T(8,128)S(1)}, u32[]{:S(2)}, u32[]{:S(2)}) collective-permute-start(f32[2,128,128]{2,1,0:T(8,128)S(1)} %corner.1), channel_id=1, source_target_pairs={{0,64},{64,128},{128,192},{1,65},{65,129},{129,193},{2,66},{66,130... | collective-permute-start | bytes 393224 | tf_op jit(solution)/shard_map/ppermute | solution.py:411
  82.3 9.8 %all_to_all.16 = f32[8,16,128]{2,1,0:T(8,128)S(1)} all-to-all(f32[8,16,128]{2,1,0:T(8,128)S(1)} %broadcast_in_dim.4), channel_id=1, replica_groups=mesh['z_hi'=4,'x'=4,'y'=4,'z_lo'=2,'core'=2] {'z_hi','z_lo'}, dimensions={0} | all-to-all | bytes 131072 | tf_op jit(solution)/shard_map/all_to_all | solution.py:306
  92.1 0.0 collective-permute-done.5.above_rest
  92.1 0.0 collective-permute-done.4.above_first
  92.1 0.7 broadcast_in_dim.5
  92.8 10.1 %all-to-all-start.2 = ((f32[32,16,128]{2,1,0:T(8,128)}), f32[32,16,128]{2,1,0:T(8,128)S(1)}, u32[]{:S(2)}, u32[]{:S(2)}) async-start(f32[32,16,128]{2,1,0:T(8,128)} %broadcast_in_dim.5), calls=%async_computation.2 | async-start | bytes 524288 | tf_op jit(solution)/shard_map/all_to_all | solution.py:306
  102.9 2.2 %seams.1 = f32[2,512,512]{2,1,0:T(8,128)} custom-call(f32[2,512,512]{2,1,0:T(8,128)} %get-tuple-element.22.grad_in, f32[2,128,128]{2,1,0:T(8,128)S(1)} %collective-permute-done.4.above_first, f32[2,128,384]{2,1,0:T(8,128)S(1)} %collective-permute-done.5.above_rest, f32[2,640,128]{2,1,0:T(8,128)S(1)} %collective-permute-done.3.left), custom_call_target="tpu_custom_call", output_to_operand_aliasing={{}: (0, {})} | custom-call | flops 1000000000 | bytes 1048576 | tf_op jit(solution)/shard_map/seams/pallas_call | solution.py:416
  105.2 6.8 %all-to-all-done.2 = f32[32,16,128]{2,1,0:T(8,128)S(1)} async-done(((f32[32,16,128]{2,1,0:T(8,128)}), f32[32,16,128]{2,1,0:T(8,128)S(1)}, u32[]{:S(2)}, u32[]{:S(2)}) %all-to-all-start.2) | async-done | bytes 262176 | tf_op jit(solution)/shard_map/all_to_all | solution.py:306
  111.9 0.7 copy.16
  (3 shorter events, 0.1 us)
Async XLA Ops:
  2.5 12.0 %collective-permute-start = (f32[2,512,128]{2,1,0:T(8,128)}, f32[2,512,128]{2,1,0:T(8,128)S(1)}, u32[]{:S(2)}, u32[]{:S(2)}) collective-permute-start(f32[2,512,128]{2,1,0:T(8,128)} %right_rim.1.after), channel_id=1, source_target_pairs={{1,0},{2,1},{3,2},{4,3},{5,4},{6,5},{7,6},{8,7},{9,8},{10,9},{11,1... | collective-permute-start | bytes 1572872 | tf_op jit(solution)/shard_map/ppermute | solution.py:350
  9.5 34.3 %collective-permute-start.1 = (f32[2,128,512]{2,1,0:T(8,128)}, f32[2,128,512]{2,1,0:T(8,128)}, u32[]{:S(2)}, u32[]{:S(2)}) collective-permute-start(f32[2,128,512]{2,1,0:T(8,128)} %get-tuple-element.17), channel_id=1, source_target_pairs={{64,0},{128,64},{192,128},{65,1},{129,65},{193,129},{66,2},{130,66... | collective-permute-start | bytes 1572872 | tf_op jit(solution)/shard_map/ppermute | solution.py:349
  10.8 33.0 %collective-permute-start.2 = (f32[2,128,128]{2,1,0:T(8,128)}, f32[2,128,128]{2,1,0:T(8,128)S(1)}, u32[]{:S(2)}, u32[]{:S(2)}) collective-permute-start(f32[2,128,128]{2,1,0:T(8,128)} %get-tuple-element.18), channel_id=1, source_target_pairs={{65,0},{66,1},{67,2},{68,3},{69,4},{70,5},{71,6},{72,7},{73,8},{74... | collective-permute-start | bytes 393224 | tf_op jit(solution)/shard_map/ppermute | solution.py:351
  14.5 0.8 copy-start.1
  43.9 0.7 copy-start.2
  50.2 29.1 %collective-permute-start.3 = (f32[2,640,128]{2,1,0:T(8,128)}, f32[2,640,128]{2,1,0:T(8,128)S(1)}, u32[]{:S(2)}, u32[]{:S(2)}) collective-permute-start(f32[2,640,128]{2,1,0:T(8,128)} %get-tuple-element.25), channel_id=1, source_target_pairs={{0,1},{1,2},{2,3},{3,4},{4,5},{5,6},{6,7},{7,8},{8,9},{9,10},{10,1... | collective-permute-start | bytes 1966088 | tf_op jit(solution)/shard_map/ppermute | solution.py:393
  53.4 38.7 %collective-permute-start.5 = (f32[2,128,384]{2,1,0:T(8,128)}, f32[2,128,384]{2,1,0:T(8,128)S(1)}, u32[]{:S(2)}, u32[]{:S(2)}) collective-permute-start(f32[2,128,384]{2,1,0:T(8,128)} %get-tuple-element.28), channel_id=1, source_target_pairs={{0,64},{64,128},{128,192},{1,65},{65,129},{129,193},{2,66},{66,130... | collective-permute-start | bytes 1179656 | tf_op jit(solution)/shard_map/ppermute | solution.py:394
  79.4 0.9 copy-start
  80.7 11.4 %collective-permute-start.4 = (f32[2,128,128]{2,1,0:T(8,128)S(1)}, f32[2,128,128]{2,1,0:T(8,128)S(1)}, u32[]{:S(2)}, u32[]{:S(2)}) collective-permute-start(f32[2,128,128]{2,1,0:T(8,128)S(1)} %corner.1), channel_id=1, source_target_pairs={{0,64},{64,128},{128,192},{1,65},{65,129},{129,193},{2,66},{66,130... | collective-permute-start | bytes 393224 | tf_op jit(solution)/shard_map/ppermute | solution.py:411
  92.8 19.1 %all-to-all-start.2 = ((f32[32,16,128]{2,1,0:T(8,128)}), f32[32,16,128]{2,1,0:T(8,128)S(1)}, u32[]{:S(2)}, u32[]{:S(2)}) async-start(f32[32,16,128]{2,1,0:T(8,128)} %broadcast_in_dim.5), calls=%async_computation.2 | async-start | bytes 524288 | tf_op jit(solution)/shard_map/all_to_all | solution.py:306

commit v4 on v3

--- a/solution.py
+++ b/solution.py
@@ -219,7 +219,7 @@
     stores = copies_of(
         [(probe_sum, probe_out)]
         + [(grad.at[t], a) for t, a in enumerate(by_tiles(g_own, tiles))]
-        + [(grad.at[tiles], g_right.at[:, pl.ds(0, rows), :])],
+        + [(grad.at[tiles], g_right)],
         sems,
     )
     start_all(stores)
@@ -227,7 +227,7 @@
 
 
 def lower_kernel(scale, pos, count, own, right, below, corner, photons, probe_in, waves_in, own_in, right_in, sum_in,
-                 g_own, g_right, g_first, g_rest, probe_out,
+                 g_own, g_right, g_below, g_corner, probe_out,
                  field, grad, photon_buf, probe, waves, plus_ref, minus_ref, probe_sum, listed, sems, photon_sems):
     rows, cols = own.shape[1], own.shape[2]
     tiles = cols // PATCH
@@ -256,41 +256,27 @@
     probe_sum[...] = probe_sum[...] * scale
     stores = copies_of(
         [(probe_sum, probe_out)]
-        + [(grad.at[t, :, lower, :], a) for t, a in enumerate([g_first] + by_tiles(g_rest, tiles - 1))]
-        + [(grad.at[t, :, upper, :], a) for t, a in enumerate(last_rows(g_own))]
-        + [(grad.at[tiles], g_right.at[:, pl.ds(base, 2 * PATCH), :])],
+        + [(grad.at[t, :, lower, :], a) for t, a in enumerate(by_tiles(g_below, tiles) + [g_corner])]
+        + [(grad.at[t, :, upper, :], a) for t, a in enumerate(last_rows(g_own) + [g_right.at[:, last, :]])],
         sems,
     )
     start_all(stores)
     wait_all(stores)
 
 
-def corner_kernel(first, left, total, rim_buf, corner_buf, sems):
-    corner = left.at[:, pl.ds(left.shape[1] - PATCH, PATCH), :]
-    loads = copies_of([(first, rim_buf), (corner, corner_buf)], sems)
-    start_all(loads)
-    wait_all(loads)
-    rim_buf[...] += corner_buf[...]
-    store = pltpu.make_async_copy(rim_buf, total, sems.at[0])
-    store.start()
-    store.wait()
-
-
-def seam_kernel(grad_in, above_first, above_rest, left, grad, top_buf, left_buf, above_buf, beside_buf, sems):
+def seam_kernel(grad_in, above, left, corner, grad, top_buf, left_buf, above_buf, beside_buf, corner_buf, sems):
     rows, cols = grad.shape[1], grad.shape[2]
     rest = rows - PATCH
     top_rim = grad.at[:, pl.ds(0, PATCH), :]
     left_rim = grad.at[:, pl.ds(PATCH, rest), pl.ds(0, PATCH)]
     loads = copies_of(
-        [(top_rim, top_buf), (left_rim, left_buf), (left.at[:, pl.ds(0, rows), :], beside_buf),
-         (above_first, above_buf.at[:, :, pl.ds(0, PATCH)]),
-         (above_rest, above_buf.at[:, :, pl.ds(PATCH, cols - PATCH)])],
+        [(top_rim, top_buf), (left_rim, left_buf), (above, above_buf), (left, beside_buf), (corner, corner_buf)],
         sems,
     )
     start_all(loads)
     wait_all(loads)
     top_buf[:, :, PATCH:] += above_buf[:, :, PATCH:]
-    top_buf[:, :, :PATCH] += above_buf[:, :, :PATCH] + beside_buf[:, :PATCH, :]
+    top_buf[:, :, :PATCH] += above_buf[:, :, :PATCH] + (beside_buf[:, :PATCH, :] + corner_buf[...])
     left_buf[...] += beside_buf[:, PATCH:, :]
     stores = copies_of([(top_buf, top_rim), (left_buf, left_rim)], sems)
     start_all(stores)
@@ -365,7 +351,7 @@
             pltpu.SemaphoreType.DMA((slot_count,)),
         ]
 
-    own_shape, right_shape, probe_shape = shape(2, rows, cols), shape(2, rows + PATCH, PATCH), shape(*probe_modes.shape)
+    own_shape, right_shape, probe_shape = shape(2, rows, cols), shape(2, rows, PATCH), shape(*probe_modes.shape)
     g_own, g_right, probe_1 = pl.pallas_call(
         upper_kernel,
         out_shape=(own_shape, right_shape, probe_shape),
@@ -377,9 +363,9 @@
         name="upper_slots",
     )(pos, count, object_field, right, photon_rows, probe_modes, waves)
     rim_shape = shape(2, PATCH, PATCH)
-    g_own, g_right, g_first, g_rest, probe_2 = pl.pallas_call(
+    g_own, g_right, g_below, g_corner, probe_2 = pl.pallas_call(
         functools.partial(lower_kernel, scale),
-        out_shape=(own_shape, right_shape, rim_shape, shape(2, PATCH, cols - PATCH), probe_shape),
+        out_shape=(own_shape, right_shape, shape(2, PATCH, cols), rim_shape, probe_shape),
         in_specs=[smem] * 2 + [hbm] * 10,
         out_specs=(hbm,) * 5,
         scratch_shapes=scratch(2 * PATCH),
@@ -390,27 +376,14 @@
     )(pos, count, object_field, right, below, corner, photon_rows, probe_modes, waves, g_own, g_right, probe_1)
 
     plane, depth = lax.axis_size(PLANE), lax.axis_size(DEPTH)
-    left = lax.ppermute(g_right, COL, along)
-    above_rest = lax.ppermute(g_rest, ROW, down)
+    above = lax.ppermute(g_below, ROW, down)
     shares = lax.all_to_all(probe_2.reshape(plane, -1, PATCH), PLANE, 0, 0, tiled=True)
     share = jnp.sum(shares, axis=0)
-    g_first = pl.pallas_call(
-        corner_kernel,
-        out_shape=rim_shape,
-        in_specs=[hbm, hbm],
-        out_specs=hbm,
-        scratch_shapes=[
-            pltpu.VMEM((2, PATCH, PATCH), F32),
-            pltpu.VMEM((2, PATCH, PATCH), F32),
-            pltpu.SemaphoreType.DMA((2,)),
-        ],
-        compiler_params=small,
-        name="corner",
-    )(g_first, left)
-    share, g_first = lax.optimization_barrier((share, g_first))
-    above_first = lax.ppermute(g_first, ROW, down)
+    share, g_corner = lax.optimization_barrier((share, g_corner))
+    from_corner = lax.ppermute(g_corner, BOTH, diagonal)
     share = jnp.sum(everyone(share, DEPTH, depth), axis=0)
-    share, above_first, above_rest = lax.optimization_barrier((share, above_first, above_rest))
+    share, above, from_corner, g_right = lax.optimization_barrier((share, above, from_corner, g_right))
+    left = lax.ppermute(g_right, COL, along)
     parts = everyone(share, PLANE, plane)
 
     object_gradient = pl.pallas_call(
@@ -423,13 +396,14 @@
             pltpu.VMEM((2, rows - PATCH, PATCH), F32),
             pltpu.VMEM((2, PATCH, cols), F32),
             pltpu.VMEM((2, rows, PATCH), F32),
+            pltpu.VMEM((2, PATCH, PATCH), F32),
             pltpu.SemaphoreType.DMA((5,)),
         ],
         input_output_aliases={0: 0},
         compiler_params=small,
         cost_estimate=pl.CostEstimate(flops=10**9, bytes_accessed=2**20, transcendentals=0),
         name="seams",
-    )(g_own, above_first, above_rest, left)
+    )(g_own, above, left, from_corner)
     return (object_gradient, parts.reshape(probe_modes.shape))
 
 

time: 114 us -> 112 us (0.982)
  blocking collectives: 29.8 us -> 45.2 us
  starting transfers between devices: 28.5 us -> 19.3 us
  waiting for transfers between devices: 29.9 us -> 21.7 us
  Pallas kernels: 19.2 us -> 21.2 us
  local copies, waits for them, and re-layouts: 3.79 us -> 2.16 us
    all_to_all x1 -> x2, blocking collectives: 9.75 us -> 24.7 us  [everyone(): return lax.all_to_all(sent, axes, 0, 0, tiled=True)]
    all_to_all x1 -> x0, starting transfers between devices: 10.1 us -> none  [everyone(): return lax.all_to_all(sent, axes, 0, 0, tiled=True)]
    all_to_all x1 -> x0, waiting for transfers between devices: 6.76 us -> none  [everyone(): return lax.all_to_all(sent, axes, 0, 0, tiled=True)]
    pallas_call x1, Pallas kernels: 7.18 us -> 8.64 us  [body(): pl.pallas_call(upper_kernel, out_shape=(own_shape, right_shape, probe_sha...]
    ppermute x1, waiting for transfers between devices: 21.4 us -> 20 us  [body(): corner = lax.ppermute(corner, BOTH, diagonal_back)]
    unnamed x7 -> x5, local copies, waits for them, and re-layouts: 3.06 us -> 2.13 us
  transfers between devices with their start and end apart: 7 -> 6, of which waited for: 3 -> 2; matrix products, arithmetic and copies ran while one was open for 0% -> 0% of each run, Pallas kernels for 10% -> 9%
where the time goes in v4:
time: 112 us; the launch traced here: 111 us
  blocking collectives  45.2 us (40%)
  waiting for transfers between devices  21.7 us (19%)
  Pallas kernels  21.2 us (19%)
  starting transfers between devices  19.3 us (17%)
  local copies, waits for them, and re-layouts  2.16 us (2%)
  between operations  1.41 us (1%)
    all_to_all x2, blocking collectives, everyone(): return lax.all_to_all(sent, axes, 0, 0, tiled=True)  24.7 us
    all_to_all x1, blocking collectives, body(): lax.all_to_all(probe_2.reshape(plane, -1, PATCH), PLANE, 0, 0, tiled=True)  20.5 us
    ppermute x1, waiting for transfers between devices, body(): corner = lax.ppermute(corner, BOTH, diagonal_back)  20 us
    pallas_call x1, Pallas kernels, body(): pl.pallas_call(upper_kernel, out_shape=(own_shape, right_shape, probe_sha...  8.64 us
    pallas_call x1, Pallas kernels, body(): pl.pallas_call(functools.partial(lower_kernel, scale), out_shape=(own_sha...  6.6 us
    ppermute x1, starting transfers between devices, body(): above = lax.ppermute(g_below, ROW, down)  6.18 us
    ppermute x1, starting transfers between devices, body(): right = lax.ppermute(right, COL, back)  5.15 us
    ppermute x1, starting transfers between devices, body(): left = lax.ppermute(g_right, COL, along)  3.09 us
  transfers between devices with their start and end apart: 6, of which 2 were waited for; matrix products, arithmetic and copies ran while one was open for 0% of the time, Pallas kernels for 9%

profile of v4, /device:TPU:1, one launch (start us, length us, event | category | flops | bytes accessed | tf_op | source)
XLA Modules:
  0.0 111.0 jit_solution(13567686341509620077)
XLA Ops:
  0.6 1.8 %right_rim.1.after = f32[2,512,128]{2,1,0:T(8,128)} custom-call(f32[2,512,512]{2,1,0:T(8,128)} %own.7), custom_call_target="tpu_custom_call" | custom-call | tf_op jit(solution)/shard_map/right_rim/pallas_call | solution.py:317
  2.5 5.1 %collective-permute-start = (f32[2,512,128]{2,1,0:T(8,128)}, f32[2,512,128]{2,1,0:T(8,128)S(1)}, u32[]{:S(2)}, u32[]{:S(2)}) collective-permute-start(f32[2,512,128]{2,1,0:T(8,128)} %right_rim.1.after), channel_id=1, source_target_pairs={{1,0},{2,1},{3,2},{4,3},{5,4},{6,5},{7,6},{8,7},{9,8},{10,9},{11,1... | collective-permute-start | bytes 1572872 | tf_op jit(solution)/shard_map/ppermute | solution.py:336
  7.6 1.9 %below_rim.1 = (f32[2,128,512]{2,1,0:T(8,128)}, f32[2,128,128]{2,1,0:T(8,128)}) custom-call(f32[2,512,512]{2,1,0:T(8,128)} %own.7, f32[2,512,128]{2,1,0:T(8,128)} %right_rim.1.after), custom_call_target="tpu_custom_call" | custom-call | tf_op jit(solution)/shard_map/below_rim/pallas_call | solution.py:326
  9.5 1.3 %collective-permute-start.1 = (f32[2,128,512]{2,1,0:T(8,128)}, f32[2,128,512]{2,1,0:T(8,128)}, u32[]{:S(2)}, u32[]{:S(2)}) collective-permute-start(f32[2,128,512]{2,1,0:T(8,128)} %get-tuple-element.18), channel_id=1, source_target_pairs={{64,0},{128,64},{192,128},{65,1},{129,65},{193,129},{66,2},{130,66... | collective-permute-start | bytes 1572872 | tf_op jit(solution)/shard_map/ppermute | solution.py:335
  10.8 1.3 %collective-permute-start.2 = (f32[2,128,128]{2,1,0:T(8,128)}, f32[2,128,128]{2,1,0:T(8,128)S(1)}, u32[]{:S(2)}, u32[]{:S(2)}) collective-permute-start(f32[2,128,128]{2,1,0:T(8,128)} %get-tuple-element.19), channel_id=1, source_target_pairs={{65,0},{66,1},{67,2},{68,3},{69,4},{70,5},{71,6},{72,7},{73,8},{74... | collective-permute-start | bytes 393224 | tf_op jit(solution)/shard_map/ppermute | solution.py:337
  12.8 1.7 %collective-permute-done.right = f32[2,512,128]{2,1,0:T(8,128)S(1)} collective-permute-done((f32[2,512,128]{2,1,0:T(8,128)}, f32[2,512,128]{2,1,0:T(8,128)S(1)}, u32[]{:S(2)}, u32[]{:S(2)}) %collective-permute-start) | collective-permute-done | bytes 524320 | tf_op jit(solution)/shard_map/ppermute | solution.py:336
  14.5 0.0 copy-start
  14.5 0.8 copy-done
  15.3 8.6 %upper_slots.1 = (f32[2,512,512]{2,1,0:T(8,128)}, f32[2,512,128]{2,1,0:T(8,128)}, f32[2,2,128,128]{3,2,1,0:T(8,128)}) custom-call(s32[2,64]{1,0:T(2,128)} %bitcast.13, s32[1]{0:T(128)} %bitcast.7.count, f32[2,512,512]{2,1,0:T(8,128)} %own.7, f32[2,512,128]{2,1,0:T(8,128)} %copy-done, bf16[64,128,128]{2,1,0:T(8,128)(2,1)} %bitcast.9, ...), custom_call_target="tpu_custom_call" | custom-call | flops 1000000000 | bytes 1048576 | tf_op jit(solution)/shard_map/upper_slots/pallas_call | solution.py:355
  23.9 20.0 %collective-permute-done.2.corner = f32[2,128,128]{2,1,0:T(8,128)S(1)} collective-permute-done((f32[2,128,128]{2,1,0:T(8,128)}, f32[2,128,128]{2,1,0:T(8,128)S(1)}, u32[]{:S(2)}, u32[]{:S(2)}) %collective-permute-start.2) | collective-permute-done | bytes 131104 | tf_op jit(solution)/shard_map/ppermute | solution.py:337
  43.9 0.0 copy-start.1
  43.9 0.0 collective-permute-done.1.below
  43.9 0.6 copy-done.1
  44.5 6.6 %lower_slots.1 = (f32[2,512,512]{2,1,0:T(8,128)}, f32[2,512,128]{2,1,0:T(8,128)}, f32[2,128,512]{2,1,0:T(8,128)}, f32[2,128,128]{2,1,0:T(8,128)}, f32[2,2,128,128]{3,2,1,0:T(8,128)}) custom-call(s32[2,64]{1,0:T(2,128)} %bitcast.14, s32[1]{0:T(128)} %bitcast.8.count, f32[2,512,512]{2,1,0:T(8,128)} %own.7, ...), custom_call_target="tpu_custom_call", output_to_operand_aliasing={{0}: (9, {}), {1}: (10, {})} | custom-call | flops 1000000000 | bytes 1048576 | tf_op jit(solution)/shard_map/lower_slots/pallas_call | solution.py:366
  51.1 6.2 %collective-permute-start.3 = (f32[2,128,512]{2,1,0:T(8,128)}, f32[2,128,512]{2,1,0:T(8,128)S(1)}, u32[]{:S(2)}, u32[]{:S(2)}) collective-permute-start(f32[2,128,512]{2,1,0:T(8,128)} %get-tuple-element.27), channel_id=1, source_target_pairs={{0,64},{64,128},{128,192},{1,65},{65,129},{129,193},{2,66},{66,130... | collective-permute-start | bytes 1572872 | tf_op jit(solution)/shard_map/ppermute | solution.py:379
  57.3 20.5 %all_to_all.15 = f32[32,16,128]{2,1,0:T(8,128)S(1)} all-to-all(f32[32,16,128]{2,1,0:T(8,128)} %bitcast.12), channel_id=1, replica_groups=mesh['z_hi'=4,'x'=4,'y'=4,'z_lo'=2,'core'=2] {'x','y','core'}, dimensions={0} | all-to-all | bytes 524288 | tf_op jit(solution)/shard_map/all_to_all | solution.py:380
  77.9 2.3 %collective-permute-start.4 = (f32[2,128,128]{2,1,0:T(8,128)}, f32[2,128,128]{2,1,0:T(8,128)S(1)}, u32[]{:S(2)}, u32[]{:S(2)}) collective-permute-start(f32[2,128,128]{2,1,0:T(8,128)} %get-tuple-element.28), channel_id=1, source_target_pairs={{0,65},{1,66},{2,67},{3,68},{4,69},{5,70},{6,71},{7,72},{8,73},{9,... | collective-permute-start | bytes 393224 | tf_op jit(solution)/shard_map/ppermute | solution.py:383
  80.2 10.0 %all_to_all.16 = f32[8,16,128]{2,1,0:T(8,128)S(1)} all-to-all(f32[8,16,128]{2,1,0:T(8,128)S(1)} %broadcast_in_dim.4), channel_id=1, replica_groups=mesh['z_hi'=4,'x'=4,'y'=4,'z_lo'=2,'core'=2] {'z_hi','z_lo'}, dimensions={0} | all-to-all | bytes 131072 | tf_op jit(solution)/shard_map/all_to_all | solution.py:292
  90.2 0.0 collective-permute-done.4.corner
  90.2 0.0 collective-permute-done.3.above
  90.2 3.1 %collective-permute-start.5 = (f32[2,512,128]{2,1,0:T(8,128)}, f32[2,512,128]{2,1,0:T(8,128)S(1)}, u32[]{:S(2)}, u32[]{:S(2)}) collective-permute-start(f32[2,512,128]{2,1,0:T(8,128)} %get-tuple-element.31), channel_id=1, source_target_pairs={{0,1},{1,2},{2,3},{3,4},{4,5},{5,6},{6,7},{7,8},{8,9},{9,10},{10,1... | collective-permute-start | bytes 1572872 | tf_op jit(solution)/shard_map/ppermute | solution.py:386
  93.3 14.7 %all_to_all.17 = f32[32,16,128]{2,1,0:T(8,128)S(1)} all-to-all(f32[32,16,128]{2,1,0:T(8,128)S(1)} %broadcast_in_dim.5), channel_id=1, replica_groups=mesh['z_hi'=4,'x'=4,'y'=4,'z_lo'=2,'core'=2] {'x','y','core'}, dimensions={0} | all-to-all | bytes 524288 | tf_op jit(solution)/shard_map/all_to_all | solution.py:292
  108.0 0.0 collective-permute-done.5.left
  108.0 2.2 %seams.1 = f32[2,512,512]{2,1,0:T(8,128)} custom-call(f32[2,512,512]{2,1,0:T(8,128)} %get-tuple-element.23.grad_in, f32[2,128,512]{2,1,0:T(8,128)S(1)} %collective-permute-done.3.above, f32[2,512,128]{2,1,0:T(8,128)S(1)} %collective-permute-done.5.left, f32[2,128,128]{2,1,0:T(8,128)S(1)} %collective-permute-done.4.corner), custom_call_target="tpu_custom_call", output_to_operand_aliasing={{}: (0, {})} | custom-call | flops 1000000000 | bytes 1048576 | tf_op jit(solution)/shard_map/seams/pallas_call | solution.py:389
  110.3 0.7 copy.16
  (4 shorter events, 0.1 us)
Async XLA Ops:
  2.5 12.0 %collective-permute-start = (f32[2,512,128]{2,1,0:T(8,128)}, f32[2,512,128]{2,1,0:T(8,128)S(1)}, u32[]{:S(2)}, u32[]{:S(2)}) collective-permute-start(f32[2,512,128]{2,1,0:T(8,128)} %right_rim.1.after), channel_id=1, source_target_pairs={{1,0},{2,1},{3,2},{4,3},{5,4},{6,5},{7,6},{8,7},{9,8},{10,9},{11,1... | collective-permute-start | bytes 1572872 | tf_op jit(solution)/shard_map/ppermute | solution.py:336
  9.5 34.3 %collective-permute-start.1 = (f32[2,128,512]{2,1,0:T(8,128)}, f32[2,128,512]{2,1,0:T(8,128)}, u32[]{:S(2)}, u32[]{:S(2)}) collective-permute-start(f32[2,128,512]{2,1,0:T(8,128)} %get-tuple-element.18), channel_id=1, source_target_pairs={{64,0},{128,64},{192,128},{65,1},{129,65},{193,129},{66,2},{130,66... | collective-permute-start | bytes 1572872 | tf_op jit(solution)/shard_map/ppermute | solution.py:335
  10.8 33.0 %collective-permute-start.2 = (f32[2,128,128]{2,1,0:T(8,128)}, f32[2,128,128]{2,1,0:T(8,128)S(1)}, u32[]{:S(2)}, u32[]{:S(2)}) collective-permute-start(f32[2,128,128]{2,1,0:T(8,128)} %get-tuple-element.19), channel_id=1, source_target_pairs={{65,0},{66,1},{67,2},{68,3},{69,4},{70,5},{71,6},{72,7},{73,8},{74... | collective-permute-start | bytes 393224 | tf_op jit(solution)/shard_map/ppermute | solution.py:337
  14.5 0.8 copy-start
  43.9 0.6 copy-start.1
  51.1 39.1 %collective-permute-start.3 = (f32[2,128,512]{2,1,0:T(8,128)}, f32[2,128,512]{2,1,0:T(8,128)S(1)}, u32[]{:S(2)}, u32[]{:S(2)}) collective-permute-start(f32[2,128,512]{2,1,0:T(8,128)} %get-tuple-element.27), channel_id=1, source_target_pairs={{0,64},{64,128},{128,192},{1,65},{65,129},{129,193},{2,66},{66,130... | collective-permute-start | bytes 1572872 | tf_op jit(solution)/shard_map/ppermute | solution.py:379
  77.9 12.3 %collective-permute-start.4 = (f32[2,128,128]{2,1,0:T(8,128)}, f32[2,128,128]{2,1,0:T(8,128)S(1)}, u32[]{:S(2)}, u32[]{:S(2)}) collective-permute-start(f32[2,128,128]{2,1,0:T(8,128)} %get-tuple-element.28), channel_id=1, source_target_pairs={{0,65},{1,66},{2,67},{3,68},{4,69},{5,70},{6,71},{7,72},{8,73},{9,... | collective-permute-start | bytes 393224 | tf_op jit(solution)/shard_map/ppermute | solution.py:383
  90.2 17.8 %collective-permute-start.5 = (f32[2,512,128]{2,1,0:T(8,128)}, f32[2,512,128]{2,1,0:T(8,128)S(1)}, u32[]{:S(2)}, u32[]{:S(2)}) collective-permute-start(f32[2,512,128]{2,1,0:T(8,128)} %get-tuple-element.31), channel_id=1, source_target_pairs={{0,1},{1,2},{2,3},{3,4},{4,5},{5,6},{6,7},{7,8},{8,9},{9,10},{10,1... | collective-permute-start | bytes 1572872 | tf_op jit(solution)/shard_map/ppermute | solution.py:386

commit v5 on v4

--- a/solution.py
+++ b/solution.py
@@ -379,11 +379,10 @@
     above = lax.ppermute(g_below, ROW, down)
     shares = lax.all_to_all(probe_2.reshape(plane, -1, PATCH), PLANE, 0, 0, tiled=True)
     share = jnp.sum(shares, axis=0)
-    share, g_corner = lax.optimization_barrier((share, g_corner))
+    share = jnp.sum(everyone(share, DEPTH, depth), axis=0)
+    share, above, g_right, g_corner = lax.optimization_barrier((share, above, g_right, g_corner))
+    left = lax.ppermute(g_right, COL, along)
     from_corner = lax.ppermute(g_corner, BOTH, diagonal)
-    share = jnp.sum(everyone(share, DEPTH, depth), axis=0)
-    share, above, from_corner, g_right = lax.optimization_barrier((share, above, from_corner, g_right))
-    left = lax.ppermute(g_right, COL, along)
     parts = everyone(share, PLANE, plane)
 
     object_gradient = pl.pallas_call(

time: 112 us -> 108 us (0.964)
  blocking collectives: 45.2 us -> 25.8 us
  starting transfers between devices: 19.3 us -> 29.6 us
  Pallas kernels: 21.2 us -> 25.9 us
    all_to_all x2 -> x1, blocking collectives: 24.7 us -> 10.8 us  [everyone(): return lax.all_to_all(sent, axes, 0, 0, tiled=True)]
    all_to_all x1, blocking collectives: 20.5 us -> 15 us  [body(): lax.all_to_all(probe_2.reshape(plane, -1, PATCH), PLANE, 0, 0, tiled=True)]
    ppermute x1, waiting for transfers between devices: 20 us -> 15.2 us  [body(): corner = lax.ppermute(corner, BOTH, diagonal_back)]
    pallas_call x1, Pallas kernels: 8.64 us -> 13.4 us  [body(): pl.pallas_call(upper_kernel, out_shape=(own_shape, right_shape, probe_sha...]
    all_to_all x0 -> x1, waiting for transfers between devices: none -> 4.29 us  [everyone(): return lax.all_to_all(sent, axes, 0, 0, tiled=True)]
    all_to_all x0 -> x1, starting transfers between devices: none -> 3.66 us  [everyone(): return lax.all_to_all(sent, axes, 0, 0, tiled=True)]
    ppermute x1, starting transfers between devices: 6.18 us -> 9.51 us  [body(): above = lax.ppermute(g_below, ROW, down)]
    ppermute x1, starting transfers between devices: 2.28 us -> 4.98 us  [body(): from_corner = lax.ppermute(g_corner, BOTH, diagonal)]
  transfers between devices with their start and end apart: 6 -> 7, of which waited for: 2 -> 3; matrix products, arithmetic and copies ran while one was open for 0% -> 1% of each run, Pallas kernels for 9% -> 14%
where the time goes in v5:
time: 108 us; the launch traced here: 107 us
  starting transfers between devices  29.6 us (27%)
  Pallas kernels  25.9 us (24%)
  blocking collectives  25.8 us (24%)
  waiting for transfers between devices  21.2 us (20%)
  local copies, waits for them, and re-layouts  2.87 us (3%)
  between operations  1.4 us (1%)
    ppermute x1, waiting for transfers between devices, body(): corner = lax.ppermute(corner, BOTH, diagonal_back)  15.2 us
    all_to_all x1, blocking collectives, body(): lax.all_to_all(probe_2.reshape(plane, -1, PATCH), PLANE, 0, 0, tiled=True)  15 us
    pallas_call x1, Pallas kernels, body(): pl.pallas_call(upper_kernel, out_shape=(own_shape, right_shape, probe_sha...  13.4 us
    all_to_all x1, blocking collectives, everyone(): return lax.all_to_all(sent, axes, 0, 0, tiled=True)  10.8 us
    ppermute x1, starting transfers between devices, body(): above = lax.ppermute(g_below, ROW, down)  9.51 us
    pallas_call x1, Pallas kernels, body(): pl.pallas_call(functools.partial(lower_kernel, scale), out_shape=(own_sha...  6.61 us
    ppermute x1, starting transfers between devices, body(): right = lax.ppermute(right, COL, back)  5.15 us
    ppermute x1, starting transfers between devices, body(): from_corner = lax.ppermute(g_corner, BOTH, diagonal)  4.98 us
  transfers between devices with their start and end apart: 7, of which 3 were waited for; matrix products, arithmetic and copies ran while one was open for 1% of the time, Pallas kernels for 14%

profile of v5, /device:TPU:1, one launch (start us, length us, event | category | flops | bytes accessed | tf_op | source)
XLA Modules:
  0.0 106.9 jit_solution(13583690875889006324)
XLA Ops:
  0.6 1.8 %right_rim.1.after = f32[2,512,128]{2,1,0:T(8,128)} custom-call(f32[2,512,512]{2,1,0:T(8,128)} %own.7), custom_call_target="tpu_custom_call" | custom-call | tf_op jit(solution)/shard_map/right_rim/pallas_call | solution.py:317
  2.5 5.1 %collective-permute-start = (f32[2,512,128]{2,1,0:T(8,128)}, f32[2,512,128]{2,1,0:T(8,128)S(1)}, u32[]{:S(2)}, u32[]{:S(2)}) collective-permute-start(f32[2,512,128]{2,1,0:T(8,128)} %right_rim.1.after), channel_id=1, source_target_pairs={{1,0},{2,1},{3,2},{4,3},{5,4},{6,5},{7,6},{8,7},{9,8},{10,9},{11,1... | collective-permute-start | bytes 1572872 | tf_op jit(solution)/shard_map/ppermute | solution.py:336
  7.6 1.9 %below_rim.1 = (f32[2,128,512]{2,1,0:T(8,128)}, f32[2,128,128]{2,1,0:T(8,128)}) custom-call(f32[2,512,512]{2,1,0:T(8,128)} %own.7, f32[2,512,128]{2,1,0:T(8,128)} %right_rim.1.after), custom_call_target="tpu_custom_call" | custom-call | tf_op jit(solution)/shard_map/below_rim/pallas_call | solution.py:326
  9.6 1.3 %collective-permute-start.1 = (f32[2,128,512]{2,1,0:T(8,128)}, f32[2,128,512]{2,1,0:T(8,128)}, u32[]{:S(2)}, u32[]{:S(2)}) collective-permute-start(f32[2,128,512]{2,1,0:T(8,128)} %get-tuple-element.16), channel_id=1, source_target_pairs={{64,0},{128,64},{192,128},{65,1},{129,65},{193,129},{66,2},{130,66... | collective-permute-start | bytes 1572872 | tf_op jit(solution)/shard_map/ppermute | solution.py:335
  10.9 1.3 %collective-permute-start.2 = (f32[2,128,128]{2,1,0:T(8,128)}, f32[2,128,128]{2,1,0:T(8,128)S(1)}, u32[]{:S(2)}, u32[]{:S(2)}) collective-permute-start(f32[2,128,128]{2,1,0:T(8,128)} %get-tuple-element.17), channel_id=1, source_target_pairs={{65,0},{66,1},{67,2},{68,3},{69,4},{70,5},{71,6},{72,7},{73,8},{74... | collective-permute-start | bytes 393224 | tf_op jit(solution)/shard_map/ppermute | solution.py:337
  12.8 1.7 %collective-permute-done.right = f32[2,512,128]{2,1,0:T(8,128)S(1)} collective-permute-done((f32[2,512,128]{2,1,0:T(8,128)}, f32[2,512,128]{2,1,0:T(8,128)S(1)}, u32[]{:S(2)}, u32[]{:S(2)}) %collective-permute-start) | collective-permute-done | bytes 524320 | tf_op jit(solution)/shard_map/ppermute | solution.py:336
  14.5 0.0 copy-start
  14.5 0.8 copy-done
  15.3 13.4 %upper_slots.1 = (f32[2,512,512]{2,1,0:T(8,128)}, f32[2,512,128]{2,1,0:T(8,128)}, f32[2,2,128,128]{3,2,1,0:T(8,128)}) custom-call(s32[2,64]{1,0:T(2,128)} %bitcast.13, s32[1]{0:T(128)} %bitcast.7.count, f32[2,512,512]{2,1,0:T(8,128)} %own.7, f32[2,512,128]{2,1,0:T(8,128)} %copy-done, bf16[64,128,128]{2,1,0:T(8,128)(2,1)} %bitcast.9, ...), custom_call_target="tpu_custom_call" | custom-call | flops 1000000000 | bytes 1048576 | tf_op jit(solution)/shard_map/upper_slots/pallas_call | solution.py:355
  28.6 15.2 %collective-permute-done.2.corner = f32[2,128,128]{2,1,0:T(8,128)S(1)} collective-permute-done((f32[2,128,128]{2,1,0:T(8,128)}, f32[2,128,128]{2,1,0:T(8,128)S(1)}, u32[]{:S(2)}, u32[]{:S(2)}) %collective-permute-start.2) | collective-permute-done | bytes 131104 | tf_op jit(solution)/shard_map/ppermute | solution.py:337
  43.9 0.0 copy-start.1
  43.9 0.0 collective-permute-done.1.below
  43.9 0.6 copy-done.1
  44.5 6.6 %lower_slots.1 = (f32[2,512,512]{2,1,0:T(8,128)}, f32[2,512,128]{2,1,0:T(8,128)}, f32[2,128,512]{2,1,0:T(8,128)}, f32[2,128,128]{2,1,0:T(8,128)}, f32[2,2,128,128]{3,2,1,0:T(8,128)}) custom-call(s32[2,64]{1,0:T(2,128)} %bitcast.14, s32[1]{0:T(128)} %bitcast.8.count, f32[2,512,512]{2,1,0:T(8,128)} %own.7, ...), custom_call_target="tpu_custom_call", output_to_operand_aliasing={{0}: (9, {}), {1}: (10, {})} | custom-call | flops 1000000000 | bytes 1048576 | tf_op jit(solution)/shard_map/lower_slots/pallas_call | solution.py:366
  51.1 9.5 %collective-permute-start.3 = (f32[2,128,512]{2,1,0:T(8,128)}, f32[2,128,512]{2,1,0:T(8,128)S(1)}, u32[]{:S(2)}, u32[]{:S(2)}) collective-permute-start(f32[2,128,512]{2,1,0:T(8,128)} %get-tuple-element.23), channel_id=1, source_target_pairs={{0,64},{64,128},{128,192},{1,65},{65,129},{129,193},{2,66},{66,130... | collective-permute-start | bytes 1572872 | tf_op jit(solution)/shard_map/ppermute | solution.py:379
  60.7 15.0 %all_to_all.15 = f32[32,16,128]{2,1,0:T(8,128)S(1)} all-to-all(f32[32,16,128]{2,1,0:T(8,128)} %bitcast.12), channel_id=1, replica_groups=mesh['z_hi'=4,'x'=4,'y'=4,'z_lo'=2,'core'=2] {'x','y','core'}, dimensions={0} | all-to-all | bytes 524288 | tf_op jit(solution)/shard_map/all_to_all | solution.py:380
  75.7 10.8 %all_to_all.16 = f32[8,16,128]{2,1,0:T(8,128)S(1)} all-to-all(f32[8,16,128]{2,1,0:T(8,128)S(1)} %broadcast_in_dim.4), channel_id=1, replica_groups=mesh['z_hi'=4,'x'=4,'y'=4,'z_lo'=2,'core'=2] {'z_hi','z_lo'}, dimensions={0} | all-to-all | bytes 131072 | tf_op jit(solution)/shard_map/all_to_all | solution.py:292
  86.6 0.0 collective-permute-done.3.above
  86.6 3.7 %collective-permute-start.4 = (f32[2,512,128]{2,1,0:T(8,128)}, f32[2,512,128]{2,1,0:T(8,128)S(1)}, u32[]{:S(2)}, u32[]{:S(2)}) collective-permute-start(f32[2,512,128]{2,1,0:T(8,128)} %get-tuple-element.27), channel_id=1, source_target_pairs={{0,1},{1,2},{2,3},{3,4},{4,5},{5,6},{6,7},{7,8},{8,9},{9,10},{10,1... | collective-permute-start | bytes 1572872 | tf_op jit(solution)/shard_map/ppermute | solution.py:384
  90.3 0.7 broadcast_in_dim.5
  91.0 3.7 %all-to-all-start.2 = ((f32[32,16,128]{2,1,0:T(8,128)}), f32[32,16,128]{2,1,0:T(8,128)S(1)}, u32[]{:S(2)}, u32[]{:S(2)}) async-start(f32[32,16,128]{2,1,0:T(8,128)} %broadcast_in_dim.5), calls=%async_computation.2 | async-start | bytes 524288 | tf_op jit(solution)/shard_map/all_to_all | solution.py:292
  94.7 5.0 %collective-permute-start.5 = (f32[2,128,128]{2,1,0:T(8,128)}, f32[2,128,128]{2,1,0:T(8,128)S(1)}, u32[]{:S(2)}, u32[]{:S(2)}) collective-permute-start(f32[2,128,128]{2,1,0:T(8,128)} %get-tuple-element.28), channel_id=1, source_target_pairs={{0,65},{1,66},{2,67},{3,68},{4,69},{5,70},{6,71},{7,72},{8,73},{9,... | collective-permute-start | bytes 393224 | tf_op jit(solution)/shard_map/ppermute | solution.py:385
  99.7 4.3 %all-to-all-done.2 = f32[32,16,128]{2,1,0:T(8,128)S(1)} async-done(((f32[32,16,128]{2,1,0:T(8,128)}), f32[32,16,128]{2,1,0:T(8,128)S(1)}, u32[]{:S(2)}, u32[]{:S(2)}) %all-to-all-start.2) | async-done | bytes 262176 | tf_op jit(solution)/shard_map/all_to_all | solution.py:292
  104.0 0.0 collective-permute-done.5.corner
  104.0 0.0 collective-permute-done.4.left
  104.0 2.2 %seams.1 = f32[2,512,512]{2,1,0:T(8,128)} custom-call(f32[2,512,512]{2,1,0:T(8,128)} %get-tuple-element.21.grad_in, f32[2,128,512]{2,1,0:T(8,128)S(1)} %collective-permute-done.3.above, f32[2,512,128]{2,1,0:T(8,128)S(1)} %collective-permute-done.4.left, f32[2,128,128]{2,1,0:T(8,128)S(1)} %collective-permute-done.5.corner), custom_call_target="tpu_custom_call", output_to_operand_aliasing={{}: (0, {})} | custom-call | flops 1000000000 | bytes 1048576 | tf_op jit(solution)/shard_map/seams/pallas_call | solution.py:388
  106.2 0.7 copy.16
  (3 shorter events, 0.1 us)
Async XLA Ops:
  2.5 12.0 %collective-permute-start = (f32[2,512,128]{2,1,0:T(8,128)}, f32[2,512,128]{2,1,0:T(8,128)S(1)}, u32[]{:S(2)}, u32[]{:S(2)}) collective-permute-start(f32[2,512,128]{2,1,0:T(8,128)} %right_rim.1.after), channel_id=1, source_target_pairs={{1,0},{2,1},{3,2},{4,3},{5,4},{6,5},{7,6},{8,7},{9,8},{10,9},{11,1... | collective-permute-start | bytes 1572872 | tf_op jit(solution)/shard_map/ppermute | solution.py:336
  9.6 34.3 %collective-permute-start.1 = (f32[2,128,512]{2,1,0:T(8,128)}, f32[2,128,512]{2,1,0:T(8,128)}, u32[]{:S(2)}, u32[]{:S(2)}) collective-permute-start(f32[2,128,512]{2,1,0:T(8,128)} %get-tuple-element.16), channel_id=1, source_target_pairs={{64,0},{128,64},{192,128},{65,1},{129,65},{193,129},{66,2},{130,66... | collective-permute-start | bytes 1572872 | tf_op jit(solution)/shard_map/ppermute | solution.py:335
  10.9 33.0 %collective-permute-start.2 = (f32[2,128,128]{2,1,0:T(8,128)}, f32[2,128,128]{2,1,0:T(8,128)S(1)}, u32[]{:S(2)}, u32[]{:S(2)}) collective-permute-start(f32[2,128,128]{2,1,0:T(8,128)} %get-tuple-element.17), channel_id=1, source_target_pairs={{65,0},{66,1},{67,2},{68,3},{69,4},{70,5},{71,6},{72,7},{73,8},{74... | collective-permute-start | bytes 393224 | tf_op jit(solution)/shard_map/ppermute | solution.py:337
  14.5 0.8 copy-start
  43.9 0.7 copy-start.1
  51.1 35.4 %collective-permute-start.3 = (f32[2,128,512]{2,1,0:T(8,128)}, f32[2,128,512]{2,1,0:T(8,128)S(1)}, u32[]{:S(2)}, u32[]{:S(2)}) collective-permute-start(f32[2,128,512]{2,1,0:T(8,128)} %get-tuple-element.23), channel_id=1, source_target_pairs={{0,64},{64,128},{128,192},{1,65},{65,129},{129,193},{2,66},{66,130... | collective-permute-start | bytes 1572872 | tf_op jit(solution)/shard_map/ppermute | solution.py:379
  86.6 17.4 %collective-permute-start.4 = (f32[2,512,128]{2,1,0:T(8,128)}, f32[2,512,128]{2,1,0:T(8,128)S(1)}, u32[]{:S(2)}, u32[]{:S(2)}) collective-permute-start(f32[2,512,128]{2,1,0:T(8,128)} %get-tuple-element.27), channel_id=1, source_target_pairs={{0,1},{1,2},{2,3},{3,4},{4,5},{5,6},{6,7},{7,8},{8,9},{9,10},{10,1... | collective-permute-start | bytes 1572872 | tf_op jit(solution)/shard_map/ppermute | solution.py:384
  91.0 12.9 %all-to-all-start.2 = ((f32[32,16,128]{2,1,0:T(8,128)}), f32[32,16,128]{2,1,0:T(8,128)S(1)}, u32[]{:S(2)}, u32[]{:S(2)}) async-start(f32[32,16,128]{2,1,0:T(8,128)} %broadcast_in_dim.5), calls=%async_computation.2 | async-start | bytes 524288 | tf_op jit(solution)/shard_map/all_to_all | solution.py:292
  94.7 9.3 %collective-permute-start.5 = (f32[2,128,128]{2,1,0:T(8,128)}, f32[2,128,128]{2,1,0:T(8,128)S(1)}, u32[]{:S(2)}, u32[]{:S(2)}) collective-permute-start(f32[2,128,128]{2,1,0:T(8,128)} %get-tuple-element.28), channel_id=1, source_target_pairs={{0,65},{1,66},{2,67},{3,68},{4,69},{5,70},{6,71},{7,72},{8,73},{9,... | collective-permute-start | bytes 393224 | tf_op jit(solution)/shard_map/ppermute | solution.py:385

commit v6 on v5

--- a/solution.py
+++ b/solution.py
@@ -197,7 +197,7 @@
     wait_all(stores)
 
 
-def upper_kernel(pos, count, own, right, photons, probe_in, waves_in, g_own, g_right, probe_out,
+def upper_kernel(pos, count, own, right, photons, probe_in, waves_in, g_own, g_top, g_bottom, probe_out,
                  field, grad, photon_buf, probe, waves, plus_ref, minus_ref, probe_sum, listed, sems, photon_sems):
     rows, cols = own.shape[1], own.shape[2]
     tiles = cols // PATCH
@@ -219,15 +219,16 @@
     stores = copies_of(
         [(probe_sum, probe_out)]
         + [(grad.at[t], a) for t, a in enumerate(by_tiles(g_own, tiles))]
-        + [(grad.at[tiles], g_right)],
+        + [(grad.at[tiles, :, pl.ds(0, rows - PATCH), :], g_top),
+           (grad.at[tiles, :, pl.ds(rows - PATCH, PATCH), :], g_bottom)],
         sems,
     )
     start_all(stores)
     wait_all(stores)
 
 
-def lower_kernel(scale, pos, count, own, right, below, corner, photons, probe_in, waves_in, own_in, right_in, sum_in,
-                 g_own, g_right, g_below, g_corner, probe_out,
+def lower_kernel(scale, pos, count, own, right, below, corner, photons, probe_in, waves_in, own_in, bottom_in, sum_in,
+                 g_own, g_bottom, g_below, g_corner, probe_out,
                  field, grad, photon_buf, probe, waves, plus_ref, minus_ref, probe_sum, listed, sems, photon_sems):
     rows, cols = own.shape[1], own.shape[2]
     tiles = cols // PATCH
@@ -241,7 +242,7 @@
         [(waves_in, waves), (probe_in, probe), (sum_in, probe_sum)]
         + [(a, field.at[t, :, upper, :]) for t, a in enumerate(last_rows(own) + [right.at[:, last, :]])]
         + [(a, field.at[t, :, lower, :]) for t, a in enumerate(by_tiles(below, tiles) + [corner])]
-        + [(a, grad.at[t, :, upper, :]) for t, a in enumerate(last_rows(own_in) + [right_in.at[:, last, :]])],
+        + [(a, grad.at[t, :, upper, :]) for t, a in enumerate(last_rows(own_in) + [bottom_in])],
         sems,
     )
     start_all(loads)
@@ -257,30 +258,36 @@
     stores = copies_of(
         [(probe_sum, probe_out)]
         + [(grad.at[t, :, lower, :], a) for t, a in enumerate(by_tiles(g_below, tiles) + [g_corner])]
-        + [(grad.at[t, :, upper, :], a) for t, a in enumerate(last_rows(g_own) + [g_right.at[:, last, :]])],
+        + [(grad.at[t, :, upper, :], a) for t, a in enumerate(last_rows(g_own) + [g_bottom])],
         sems,
     )
     start_all(stores)
     wait_all(stores)
 
 
-def seam_kernel(grad_in, above, left, corner, grad, top_buf, left_buf, above_buf, beside_buf, corner_buf, sems):
+def seam_kernel(grad_in, above, left_top, left_bottom, corner, parts, grad, probe,
+                top_buf, left_buf, above_buf, beside_buf, corner_buf, probe_buf, sems):
     rows, cols = grad.shape[1], grad.shape[2]
     rest = rows - PATCH
     top_rim = grad.at[:, pl.ds(0, PATCH), :]
     left_rim = grad.at[:, pl.ds(PATCH, rest), pl.ds(0, PATCH)]
     loads = copies_of(
-        [(top_rim, top_buf), (left_rim, left_buf), (above, above_buf), (left, beside_buf), (corner, corner_buf)],
+        [(top_rim, top_buf), (left_rim, left_buf), (above, above_buf), (corner, corner_buf),
+         (left_top, beside_buf.at[:, pl.ds(0, rest), :]), (left_bottom, beside_buf.at[:, pl.ds(rest, PATCH), :]),
+         (parts, probe_buf)],
         sems,
     )
     start_all(loads)
     wait_all(loads)
+    join = pltpu.make_async_copy(probe_buf, probe, sems.at[2])
+    join.start()
     top_buf[:, :, PATCH:] += above_buf[:, :, PATCH:]
     top_buf[:, :, :PATCH] += above_buf[:, :, :PATCH] + (beside_buf[:, :PATCH, :] + corner_buf[...])
     left_buf[...] += beside_buf[:, PATCH:, :]
     stores = copies_of([(top_buf, top_rim), (left_buf, left_rim)], sems)
     start_all(stores)
     wait_all(stores)
+    join.wait()
 
 
 def shape(*dims):
@@ -351,59 +358,61 @@
             pltpu.SemaphoreType.DMA((slot_count,)),
         ]
 
-    own_shape, right_shape, probe_shape = shape(2, rows, cols), shape(2, rows, PATCH), shape(*probe_modes.shape)
-    g_own, g_right, probe_1 = pl.pallas_call(
+    own_shape, probe_shape, rim_shape = shape(2, rows, cols), shape(*probe_modes.shape), shape(2, PATCH, PATCH)
+    g_own, g_top, g_bottom, probe_1 = pl.pallas_call(
         upper_kernel,
-        out_shape=(own_shape, right_shape, probe_shape),
+        out_shape=(own_shape, shape(2, rows - PATCH, PATCH), rim_shape, probe_shape),
         in_specs=[smem, smem] + [hbm] * 5,
-        out_specs=(hbm,) * 3,
+        out_specs=(hbm,) * 4,
         scratch_shapes=scratch(rows),
         compiler_params=params,
         cost_estimate=pl.CostEstimate(flops=10**9, bytes_accessed=2**20, transcendentals=0),
         name="upper_slots",
     )(pos, count, object_field, right, photon_rows, probe_modes, waves)
-    rim_shape = shape(2, PATCH, PATCH)
-    g_own, g_right, g_below, g_corner, probe_2 = pl.pallas_call(
+    left_top = lax.ppermute(g_top, COL, along)
+    g_own, g_bottom, g_below, g_corner, probe_2 = pl.pallas_call(
         functools.partial(lower_kernel, scale),
-        out_shape=(own_shape, right_shape, shape(2, PATCH, cols), rim_shape, probe_shape),
+        out_shape=(own_shape, rim_shape, shape(2, PATCH, cols), rim_shape, probe_shape),
         in_specs=[smem] * 2 + [hbm] * 10,
         out_specs=(hbm,) * 5,
         scratch_shapes=scratch(2 * PATCH),
         input_output_aliases={9: 0, 10: 1},
         compiler_params=params,
-        cost_estimate=pl.CostEstimate(flops=10**9, bytes_accessed=2**20, transcendentals=0),
+        cost_estimate=pl.CostEstimate(flops=2 * 10**10, bytes_accessed=2**20, transcendentals=0),
         name="lower_slots",
-    )(pos, count, object_field, right, below, corner, photon_rows, probe_modes, waves, g_own, g_right, probe_1)
+    )(pos, count, object_field, right, below, corner, photon_rows, probe_modes, waves, g_own, g_bottom, probe_1)
 
     plane, depth = lax.axis_size(PLANE), lax.axis_size(DEPTH)
     above = lax.ppermute(g_below, ROW, down)
+    probe_2, left_top = lax.optimization_barrier((probe_2, left_top))
     shares = lax.all_to_all(probe_2.reshape(plane, -1, PATCH), PLANE, 0, 0, tiled=True)
     share = jnp.sum(shares, axis=0)
     share = jnp.sum(everyone(share, DEPTH, depth), axis=0)
-    share, above, g_right, g_corner = lax.optimization_barrier((share, above, g_right, g_corner))
-    left = lax.ppermute(g_right, COL, along)
+    share, above, g_bottom, g_corner = lax.optimization_barrier((share, above, g_bottom, g_corner))
+    left_bottom = lax.ppermute(g_bottom, COL, along)
     from_corner = lax.ppermute(g_corner, BOTH, diagonal)
     parts = everyone(share, PLANE, plane)
 
-    object_gradient = pl.pallas_call(
+    object_gradient, probe_gradient = pl.pallas_call(
         seam_kernel,
-        out_shape=own_shape,
-        in_specs=[hbm] * 4,
-        out_specs=hbm,
+        out_shape=(own_shape, shape(*parts.shape)),
+        in_specs=[hbm] * 6,
+        out_specs=(hbm, hbm),
         scratch_shapes=[
             pltpu.VMEM((2, PATCH, cols), F32),
             pltpu.VMEM((2, rows - PATCH, PATCH), F32),
             pltpu.VMEM((2, PATCH, cols), F32),
             pltpu.VMEM((2, rows, PATCH), F32),
             pltpu.VMEM((2, PATCH, PATCH), F32),
-            pltpu.SemaphoreType.DMA((5,)),
+            pltpu.VMEM(parts.shape, F32),
+            pltpu.SemaphoreType.DMA((8,)),
         ],
         input_output_aliases={0: 0},
         compiler_params=small,
         cost_estimate=pl.CostEstimate(flops=10**9, bytes_accessed=2**20, transcendentals=0),
         name="seams",
-    )(g_own, above, left, from_corner)
-    return (object_gradient, parts.reshape(probe_modes.shape))
+    )(g_own, above, left_top, left_bottom, from_corner, parts)
+    return (object_gradient, probe_gradient.reshape(probe_modes.shape))
 
 
 def solution(mesh):

time: 108 us -> 108 us (level)
  the two profiles are of different devices: /device:TPU:1 before, /device:TPU:70 now
where the time goes in v6:
time: 108 us; the launch traced here: 106 us
  starting transfers between devices  32.3 us (30%)
  blocking collectives  28.8 us (27%)
  Pallas kernels  28.4 us (26%)
  waiting for transfers between devices  13.8 us (13%)
  local copies, waits for them, and re-layouts  1.53 us (1%)
  between operations  1.41 us (1%)
    all_to_all x1, blocking collectives, body(): lax.all_to_all(probe_2.reshape(plane, -1, PATCH), PLANE, 0, 0, tiled=True)  17.6 us
    pallas_call x1, Pallas kernels, body(): pl.pallas_call(upper_kernel, out_shape=(own_shape, shape(2, rows - PATCH,...  15.7 us
    all_to_all x1, blocking collectives, everyone(): return lax.all_to_all(sent, axes, 0, 0, tiled=True)  11.2 us
    ppermute x1, starting transfers between devices, body(): above = lax.ppermute(g_below, ROW, down)  6.75 us
    pallas_call x1, Pallas kernels, body(): pl.pallas_call(functools.partial(lower_kernel, scale), out_shape=(own_sha...  6.66 us
    ppermute x1, waiting for transfers between devices, body(): from_corner = lax.ppermute(g_corner, BOTH, diagonal)  6.66 us
    ppermute x1, starting transfers between devices, body(): right = lax.ppermute(right, COL, back)  5.98 us
    ppermute x1, starting transfers between devices, body(): from_corner = lax.ppermute(g_corner, BOTH, diagonal)  5.86 us
  transfers between devices with their start and end apart: 8, of which 5 were waited for; matrix products, arithmetic and copies ran while one was open for 0% of the time, Pallas kernels for 23%

profile of v6, /device:TPU:70, one launch (start us, length us, event | category | flops | bytes accessed | tf_op | source)
XLA Modules:
  0.0 106.3 jit_solution(467039038239396760)
XLA Ops:
  0.6 1.8 %right_rim.1.after = f32[2,512,128]{2,1,0:T(8,128)} custom-call(f32[2,512,512]{2,1,0:T(8,128)} %own.7), custom_call_target="tpu_custom_call" | custom-call | tf_op jit(solution)/shard_map/right_rim/pallas_call | solution.py:324
  2.5 6.0 %collective-permute-start = (f32[2,512,128]{2,1,0:T(8,128)}, f32[2,512,128]{2,1,0:T(8,128)S(1)}, u32[]{:S(2)}, u32[]{:S(2)}) collective-permute-start(f32[2,512,128]{2,1,0:T(8,128)} %right_rim.1.after), channel_id=1, source_target_pairs={{1,0},{2,1},{3,2},{4,3},{5,4},{6,5},{7,6},{8,7},{9,8},{10,9},{11,1... | collective-permute-start | bytes 1572872 | tf_op jit(solution)/shard_map/ppermute | solution.py:343
  8.5 1.9 %below_rim.1 = (f32[2,128,512]{2,1,0:T(8,128)}, f32[2,128,128]{2,1,0:T(8,128)}) custom-call(f32[2,512,512]{2,1,0:T(8,128)} %own.7, f32[2,512,128]{2,1,0:T(8,128)} %right_rim.1.after), custom_call_target="tpu_custom_call" | custom-call | tf_op jit(solution)/shard_map/below_rim/pallas_call | solution.py:333
  10.4 1.9 %collective-permute-start.1 = (f32[2,128,512]{2,1,0:T(8,128)}, f32[2,128,512]{2,1,0:T(8,128)}, u32[]{:S(2)}, u32[]{:S(2)}) collective-permute-start(f32[2,128,512]{2,1,0:T(8,128)} %get-tuple-element.21), channel_id=1, source_target_pairs={{64,0},{128,64},{192,128},{65,1},{129,65},{193,129},{66,2},{130,66... | collective-permute-start | bytes 1572872 | tf_op jit(solution)/shard_map/ppermute | solution.py:342
  12.3 1.9 %collective-permute-start.2 = (f32[2,128,128]{2,1,0:T(8,128)}, f32[2,128,128]{2,1,0:T(8,128)}, u32[]{:S(2)}, u32[]{:S(2)}) collective-permute-start(f32[2,128,128]{2,1,0:T(8,128)} %get-tuple-element.22), channel_id=1, source_target_pairs={{65,0},{66,1},{67,2},{68,3},{69,4},{70,5},{71,6},{72,7},{73,8},{74... | collective-permute-start | bytes 393224 | tf_op jit(solution)/shard_map/ppermute | solution.py:344
  14.9 0.6 collective-permute-done.right
  15.5 0.0 copy-start
  15.5 0.8 copy-done
  16.3 15.7 %upper_slots.1 = (f32[2,512,512]{2,1,0:T(8,128)}, f32[2,384,128]{2,1,0:T(8,128)}, f32[2,128,128]{2,1,0:T(8,128)}, f32[2,2,128,128]{3,2,1,0:T(8,128)}) custom-call(s32[2,64]{1,0:T(2,128)} %bitcast.12, s32[1]{0:T(128)} %bitcast.7.count, f32[2,512,512]{2,1,0:T(8,128)} %own.7, f32[2,512,128]{2,1,0:T(8,128)} %copy-done, bf16[64,128,128]{2,1,0:T(8,128)(2,1)} %bitcast.9, ...), custom_call_target="tpu_custom_call" | custom-call | flops 1000000000 | bytes 1048576 | tf_op jit(solution)/shard_map/upper_slots/pallas_call | solution.py:362
  32.0 1.9 %collective-permute-start.3 = (f32[2,384,128]{2,1,0:T(8,128)}, f32[2,384,128]{2,1,0:T(8,128)S(1)}, u32[]{:S(2)}, u32[]{:S(2)}) collective-permute-start(f32[2,384,128]{2,1,0:T(8,128)} %get-tuple-element.28), channel_id=1, source_target_pairs={{0,1},{1,2},{2,3},{3,4},{4,5},{5,6},{6,7},{7,8},{8,9},{9,10},{10,1... | collective-permute-start | bytes 1179656 | tf_op jit(solution)/shard_map/ppermute | solution.py:372
  33.9 3.5 %collective-permute-done.2.corner = f32[2,128,128]{2,1,0:T(8,128)} collective-permute-done((f32[2,128,128]{2,1,0:T(8,128)}, f32[2,128,128]{2,1,0:T(8,128)}, u32[]{:S(2)}, u32[]{:S(2)}) %collective-permute-start.2) | collective-permute-done | bytes 131104 | tf_op jit(solution)/shard_map/ppermute | solution.py:344
  37.4 1.6 %collective-permute-done.1.below = f32[2,128,512]{2,1,0:T(8,128)} collective-permute-done((f32[2,128,512]{2,1,0:T(8,128)}, f32[2,128,512]{2,1,0:T(8,128)}, u32[]{:S(2)}, u32[]{:S(2)}) %collective-permute-start.1) | collective-permute-done | bytes 524320 | tf_op jit(solution)/shard_map/ppermute | solution.py:342
  38.9 6.7 %lower_slots.1 = (f32[2,512,512]{2,1,0:T(8,128)}, f32[2,128,128]{2,1,0:T(8,128)}, f32[2,128,512]{2,1,0:T(8,128)}, f32[2,128,128]{2,1,0:T(8,128)}, f32[2,2,128,128]{3,2,1,0:T(8,128)}) custom-call(s32[2,64]{1,0:T(2,128)} %bitcast.13, s32[1]{0:T(128)} %bitcast.8.count, f32[2,512,512]{2,1,0:T(8,128)} %own.7, ...), custom_call_target="tpu_custom_call", output_to_operand_aliasing={{0}: (9, {}), {1}: (10, {})} | custom-call | flops 20000000000 | bytes 1048576 | tf_op jit(solution)/shard_map/lower_slots/pallas_call | solution.py:373
  45.6 6.8 %collective-permute-start.4 = (f32[2,128,512]{2,1,0:T(8,128)}, f32[2,128,512]{2,1,0:T(8,128)S(1)}, u32[]{:S(2)}, u32[]{:S(2)}) collective-permute-start(f32[2,128,512]{2,1,0:T(8,128)} %get-tuple-element.30), channel_id=1, source_target_pairs={{0,64},{64,128},{128,192},{1,65},{65,129},{129,193},{2,66},{66,130... | collective-permute-start | bytes 1572872 | tf_op jit(solution)/shard_map/ppermute | solution.py:386
  52.4 0.0 collective-permute-done.3.left_top
  52.4 17.6 %all_to_all.15 = f32[32,16,128]{2,1,0:T(8,128)S(1)} all-to-all(f32[32,16,128]{2,1,0:T(8,128)} %bitcast.11), channel_id=1, replica_groups=mesh['z_hi'=4,'x'=4,'y'=4,'z_lo'=2,'core'=2] {'x','y','core'}, dimensions={0} | all-to-all | bytes 524288 | tf_op jit(solution)/shard_map/all_to_all | solution.py:388
  70.1 11.2 %all_to_all.16 = f32[8,16,128]{2,1,0:T(8,128)S(1)} all-to-all(f32[8,16,128]{2,1,0:T(8,128)S(1)} %broadcast_in_dim.4), channel_id=1, replica_groups=mesh['z_hi'=4,'x'=4,'y'=4,'z_lo'=2,'core'=2] {'z_hi','z_lo'}, dimensions={0} | all-to-all | bytes 131072 | tf_op jit(solution)/shard_map/all_to_all | solution.py:299
  81.3 0.0 collective-permute-done.4.above
  81.3 0.7 broadcast_in_dim.5
  82.0 5.8 %all-to-all-start.2 = ((f32[32,16,128]{2,1,0:T(8,128)}), f32[32,16,128]{2,1,0:T(8,128)S(1)}, u32[]{:S(2)}, u32[]{:S(2)}) async-start(f32[32,16,128]{2,1,0:T(8,128)} %broadcast_in_dim.5), calls=%async_computation.2 | async-start | bytes 524288 | tf_op jit(solution)/shard_map/all_to_all | solution.py:299
  87.9 2.1 %collective-permute-start.5 = (f32[2,128,128]{2,1,0:T(8,128)}, f32[2,128,128]{2,1,0:T(8,128)S(1)}, u32[]{:S(2)}, u32[]{:S(2)}) collective-permute-start(f32[2,128,128]{2,1,0:T(8,128)} %get-tuple-element.35), channel_id=1, source_target_pairs={{0,1},{1,2},{2,3},{3,4},{4,5},{5,6},{6,7},{7,8},{8,9},{9,10},{10,1... | collective-permute-start | bytes 393224 | tf_op jit(solution)/shard_map/ppermute | solution.py:392
  89.9 5.9 %collective-permute-start.6 = (f32[2,128,128]{2,1,0:T(8,128)}, f32[2,128,128]{2,1,0:T(8,128)S(1)}, u32[]{:S(2)}, u32[]{:S(2)}) collective-permute-start(f32[2,128,128]{2,1,0:T(8,128)} %get-tuple-element.36), channel_id=1, source_target_pairs={{0,65},{1,66},{2,67},{3,68},{4,69},{5,70},{6,71},{7,72},{8,73},{9,... | collective-permute-start | bytes 393224 | tf_op jit(solution)/shard_map/ppermute | solution.py:393
  95.8 1.6 %collective-permute-done.5.left_bottom = f32[2,128,128]{2,1,0:T(8,128)S(1)} collective-permute-done((f32[2,128,128]{2,1,0:T(8,128)}, f32[2,128,128]{2,1,0:T(8,128)S(1)}, u32[]{:S(2)}, u32[]{:S(2)}) %collective-permute-start.5) | collective-permute-done | bytes 131104 | tf_op jit(solution)/shard_map/ppermute | solution.py:392
  97.4 6.7 %collective-permute-done.6.corner = f32[2,128,128]{2,1,0:T(8,128)S(1)} collective-permute-done((f32[2,128,128]{2,1,0:T(8,128)}, f32[2,128,128]{2,1,0:T(8,128)S(1)}, u32[]{:S(2)}, u32[]{:S(2)}) %collective-permute-start.6) | collective-permute-done | bytes 131104 | tf_op jit(solution)/shard_map/ppermute | solution.py:393
  104.0 0.0 all-to-all-done.2.parts
  104.0 2.2 %seams.1 = (f32[2,512,512]{2,1,0:T(8,128)}, f32[32,16,128]{2,1,0:T(8,128)}) custom-call(f32[2,512,512]{2,1,0:T(8,128)} %get-tuple-element.26.grad_in, f32[2,128,512]{2,1,0:T(8,128)S(1)} %collective-permute-done.4.above, f32[2,384,128]{2,1,0:T(8,128)S(1)} %collective-permute-done.3.left_top, ...), custom_call_target="tpu_custom_call", output_to_operand_aliasing={{0}: (0, {})} | custom-call | flops 1000000000 | bytes 1048576 | tf_op jit(solution)/shard_map/seams/pallas_call | solution.py:396
  (3 shorter events, 0.1 us)
Async XLA Ops:
  2.5 13.0 %collective-permute-start = (f32[2,512,128]{2,1,0:T(8,128)}, f32[2,512,128]{2,1,0:T(8,128)S(1)}, u32[]{:S(2)}, u32[]{:S(2)}) collective-permute-start(f32[2,512,128]{2,1,0:T(8,128)} %right_rim.1.after), channel_id=1, source_target_pairs={{1,0},{2,1},{3,2},{4,3},{5,4},{6,5},{7,6},{8,7},{9,8},{10,9},{11,1... | collective-permute-start | bytes 1572872 | tf_op jit(solution)/shard_map/ppermute | solution.py:343
  10.4 28.6 %collective-permute-start.1 = (f32[2,128,512]{2,1,0:T(8,128)}, f32[2,128,512]{2,1,0:T(8,128)}, u32[]{:S(2)}, u32[]{:S(2)}) collective-permute-start(f32[2,128,512]{2,1,0:T(8,128)} %get-tuple-element.21), channel_id=1, source_target_pairs={{64,0},{128,64},{192,128},{65,1},{129,65},{193,129},{66,2},{130,66... | collective-permute-start | bytes 1572872 | tf_op jit(solution)/shard_map/ppermute | solution.py:342
  12.3 25.0 %collective-permute-start.2 = (f32[2,128,128]{2,1,0:T(8,128)}, f32[2,128,128]{2,1,0:T(8,128)}, u32[]{:S(2)}, u32[]{:S(2)}) collective-permute-start(f32[2,128,128]{2,1,0:T(8,128)} %get-tuple-element.22), channel_id=1, source_target_pairs={{65,0},{66,1},{67,2},{68,3},{69,4},{70,5},{71,6},{72,7},{73,8},{74... | collective-permute-start | bytes 393224 | tf_op jit(solution)/shard_map/ppermute | solution.py:344
  15.5 0.8 copy-start
  32.0 20.4 %collective-permute-start.3 = (f32[2,384,128]{2,1,0:T(8,128)}, f32[2,384,128]{2,1,0:T(8,128)S(1)}, u32[]{:S(2)}, u32[]{:S(2)}) collective-permute-start(f32[2,384,128]{2,1,0:T(8,128)} %get-tuple-element.28), channel_id=1, source_target_pairs={{0,1},{1,2},{2,3},{3,4},{4,5},{5,6},{6,7},{7,8},{8,9},{9,10},{10,1... | collective-permute-start | bytes 1179656 | tf_op jit(solution)/shard_map/ppermute | solution.py:372
  45.6 35.7 %collective-permute-start.4 = (f32[2,128,512]{2,1,0:T(8,128)}, f32[2,128,512]{2,1,0:T(8,128)S(1)}, u32[]{:S(2)}, u32[]{:S(2)}) collective-permute-start(f32[2,128,512]{2,1,0:T(8,128)} %get-tuple-element.30), channel_id=1, source_target_pairs={{0,64},{64,128},{128,192},{1,65},{65,129},{129,193},{2,66},{66,130... | collective-permute-start | bytes 1572872 | tf_op jit(solution)/shard_map/ppermute | solution.py:386
  82.0 22.0 %all-to-all-start.2 = ((f32[32,16,128]{2,1,0:T(8,128)}), f32[32,16,128]{2,1,0:T(8,128)S(1)}, u32[]{:S(2)}, u32[]{:S(2)}) async-start(f32[32,16,128]{2,1,0:T(8,128)} %broadcast_in_dim.5), calls=%async_computation.2 | async-start | bytes 524288 | tf_op jit(solution)/shard_map/all_to_all | solution.py:299
  87.9 9.5 %collective-permute-start.5 = (f32[2,128,128]{2,1,0:T(8,128)}, f32[2,128,128]{2,1,0:T(8,128)S(1)}, u32[]{:S(2)}, u32[]{:S(2)}) collective-permute-start(f32[2,128,128]{2,1,0:T(8,128)} %get-tuple-element.35), channel_id=1, source_target_pairs={{0,1},{1,2},{2,3},{3,4},{4,5},{5,6},{6,7},{7,8},{8,9},{9,10},{10,1... | collective-permute-start | bytes 393224 | tf_op jit(solution)/shard_map/ppermute | solution.py:392
  89.9 14.1 %collective-permute-start.6 = (f32[2,128,128]{2,1,0:T(8,128)}, f32[2,128,128]{2,1,0:T(8,128)S(1)}, u32[]{:S(2)}, u32[]{:S(2)}) collective-permute-start(f32[2,128,128]{2,1,0:T(8,128)} %get-tuple-element.36), channel_id=1, source_target_pairs={{0,65},{1,66},{2,67},{3,68},{4,69},{5,70},{6,71},{7,72},{8,73},{9,... | collective-permute-start | bytes 393224 | tf_op jit(solution)/shard_map/ppermute | solution.py:393

commit v7 on v6

--- a/solution.py
+++ b/solution.py
@@ -387,9 +387,10 @@
     probe_2, left_top = lax.optimization_barrier((probe_2, left_top))
     shares = lax.all_to_all(probe_2.reshape(plane, -1, PATCH), PLANE, 0, 0, tiled=True)
     share = jnp.sum(shares, axis=0)
+    left_bottom = lax.ppermute(g_bottom, COL, along)
+    share, left_bottom = lax.optimization_barrier((share, left_bottom))
     share = jnp.sum(everyone(share, DEPTH, depth), axis=0)
-    share, above, g_bottom, g_corner = lax.optimization_barrier((share, above, g_bottom, g_corner))
-    left_bottom = lax.ppermute(g_bottom, COL, along)
+    share, above, g_corner = lax.optimization_barrier((share, above, g_corner))
     from_corner = lax.ppermute(g_corner, BOTH, diagonal)
     parts = everyone(share, PLANE, plane)
 

time: 108 us -> 114 us (1.056)
  the two profiles are of different devices: /device:TPU:70 before, /device:TPU:1 now
where the time goes in v7:
time: 114 us; the launch traced here: 113 us
  starting transfers between devices  39.9 us (35%)
  waiting for transfers between devices  31.7 us (28%)
  Pallas kernels  23.7 us (21%)
  blocking collectives  14.6 us (13%)
  local copies, waits for them, and re-layouts  1.52 us (1%)
  between operations  1.42 us (1%)
    ppermute x1, waiting for transfers between devices, body(): corner = lax.ppermute(corner, BOTH, diagonal_back)  17.6 us
    all_to_all x1, blocking collectives, everyone(): return lax.all_to_all(sent, axes, 0, 0, tiled=True)  14.6 us
    pallas_call x1, Pallas kernels, body(): pl.pallas_call(upper_kernel, out_shape=(own_shape, shape(2, rows - PATCH,...  11 us
    all_to_all x1, starting transfers between devices, everyone(): return lax.all_to_all(sent, axes, 0, 0, tiled=True)  9.71 us
    ppermute x1, starting transfers between devices, body(): above = lax.ppermute(g_below, ROW, down)  7.27 us
    all_to_all x1, starting transfers between devices, body(): lax.all_to_all(probe_2.reshape(plane, -1, PATCH), PLANE, 0, 0, tiled=True)  7.25 us
    pallas_call x1, Pallas kernels, body(): pl.pallas_call(functools.partial(lower_kernel, scale), out_shape=(own_sha...  6.65 us
    all_to_all x1, waiting for transfers between devices, body(): lax.all_to_all(probe_2.reshape(plane, -1, PATCH), PLANE, 0, 0, tiled=True)  5.57 us
  transfers between devices with their start and end apart: 9, of which 5 were waited for; matrix products, arithmetic and copies ran while one was open for 0% of the time, Pallas kernels for 17%

profile of v7, /device:TPU:1, one launch (start us, length us, event | category | flops | bytes accessed | tf_op | source)
XLA Modules:
  0.0 112.8 jit_solution(2291608264904901321)
XLA Ops:
  0.6 1.8 %right_rim.1.after = f32[2,512,128]{2,1,0:T(8,128)} custom-call(f32[2,512,512]{2,1,0:T(8,128)} %own.7), custom_call_target="tpu_custom_call" | custom-call | tf_op jit(solution)/shard_map/right_rim/pallas_call | solution.py:324
  2.5 5.1 %collective-permute-start = (f32[2,512,128]{2,1,0:T(8,128)}, f32[2,512,128]{2,1,0:T(8,128)S(1)}, u32[]{:S(2)}, u32[]{:S(2)}) collective-permute-start(f32[2,512,128]{2,1,0:T(8,128)} %right_rim.1.after), channel_id=1, source_target_pairs={{1,0},{2,1},{3,2},{4,3},{5,4},{6,5},{7,6},{8,7},{9,8},{10,9},{11,1... | collective-permute-start | bytes 1572872 | tf_op jit(solution)/shard_map/ppermute | solution.py:343
  7.6 1.9 %below_rim.1 = (f32[2,128,512]{2,1,0:T(8,128)}, f32[2,128,128]{2,1,0:T(8,128)}) custom-call(f32[2,512,512]{2,1,0:T(8,128)} %own.7, f32[2,512,128]{2,1,0:T(8,128)} %right_rim.1.after), custom_call_target="tpu_custom_call" | custom-call | tf_op jit(solution)/shard_map/below_rim/pallas_call | solution.py:333
  9.6 1.3 %collective-permute-start.1 = (f32[2,128,512]{2,1,0:T(8,128)}, f32[2,128,512]{2,1,0:T(8,128)}, u32[]{:S(2)}, u32[]{:S(2)}) collective-permute-start(f32[2,128,512]{2,1,0:T(8,128)} %get-tuple-element.22), channel_id=1, source_target_pairs={{64,0},{128,64},{192,128},{65,1},{129,65},{193,129},{66,2},{130,66... | collective-permute-start | bytes 1572872 | tf_op jit(solution)/shard_map/ppermute | solution.py:342
  10.9 1.3 %collective-permute-start.2 = (f32[2,128,128]{2,1,0:T(8,128)}, f32[2,128,128]{2,1,0:T(8,128)}, u32[]{:S(2)}, u32[]{:S(2)}) collective-permute-start(f32[2,128,128]{2,1,0:T(8,128)} %get-tuple-element.23), channel_id=1, source_target_pairs={{65,0},{66,1},{67,2},{68,3},{69,4},{70,5},{71,6},{72,7},{73,8},{74... | collective-permute-start | bytes 393224 | tf_op jit(solution)/shard_map/ppermute | solution.py:344
  12.8 1.7 %collective-permute-done.right = f32[2,512,128]{2,1,0:T(8,128)S(1)} collective-permute-done((f32[2,512,128]{2,1,0:T(8,128)}, f32[2,512,128]{2,1,0:T(8,128)S(1)}, u32[]{:S(2)}, u32[]{:S(2)}) %collective-permute-start) | collective-permute-done | bytes 524320 | tf_op jit(solution)/shard_map/ppermute | solution.py:343
  14.5 0.0 copy-start
  14.5 0.8 copy-done
  15.3 11.0 %upper_slots.1 = (f32[2,512,512]{2,1,0:T(8,128)}, f32[2,384,128]{2,1,0:T(8,128)}, f32[2,128,128]{2,1,0:T(8,128)}, f32[2,2,128,128]{3,2,1,0:T(8,128)}) custom-call(s32[2,64]{1,0:T(2,128)} %bitcast.12, s32[1]{0:T(128)} %bitcast.7.count, f32[2,512,512]{2,1,0:T(8,128)} %own.7, f32[2,512,128]{2,1,0:T(8,128)} %copy-done, bf16[64,128,128]{2,1,0:T(8,128)(2,1)} %bitcast.9, ...), custom_call_target="tpu_custom_call" | custom-call | flops 1000000000 | bytes 1048576 | tf_op jit(solution)/shard_map/upper_slots/pallas_call | solution.py:362
  26.3 1.9 %collective-permute-start.3 = (f32[2,384,128]{2,1,0:T(8,128)}, f32[2,384,128]{2,1,0:T(8,128)S(1)}, u32[]{:S(2)}, u32[]{:S(2)}) collective-permute-start(f32[2,384,128]{2,1,0:T(8,128)} %get-tuple-element.29), channel_id=1, source_target_pairs={{0,1},{1,2},{2,3},{3,4},{4,5},{5,6},{6,7},{7,8},{8,9},{9,10},{10,1... | collective-permute-start | bytes 1179656 | tf_op jit(solution)/shard_map/ppermute | solution.py:372
  28.2 17.6 %collective-permute-done.2.corner = f32[2,128,128]{2,1,0:T(8,128)} collective-permute-done((f32[2,128,128]{2,1,0:T(8,128)}, f32[2,128,128]{2,1,0:T(8,128)}, u32[]{:S(2)}, u32[]{:S(2)}) %collective-permute-start.2) | collective-permute-done | bytes 131104 | tf_op jit(solution)/shard_map/ppermute | solution.py:344
  45.9 0.0 collective-permute-done.1.below
  45.9 6.6 %lower_slots.1 = (f32[2,512,512]{2,1,0:T(8,128)}, f32[2,128,128]{2,1,0:T(8,128)}, f32[2,128,512]{2,1,0:T(8,128)}, f32[2,128,128]{2,1,0:T(8,128)}, f32[2,2,128,128]{3,2,1,0:T(8,128)}) custom-call(s32[2,64]{1,0:T(2,128)} %bitcast.13, s32[1]{0:T(128)} %bitcast.8.count, f32[2,512,512]{2,1,0:T(8,128)} %own.7, ...), custom_call_target="tpu_custom_call", output_to_operand_aliasing={{0}: (9, {}), {1}: (10, {})} | custom-call | flops 20000000000 | bytes 1048576 | tf_op jit(solution)/shard_map/lower_slots/pallas_call | solution.py:373
  52.5 7.3 %collective-permute-start.5 = (f32[2,128,512]{2,1,0:T(8,128)}, f32[2,128,512]{2,1,0:T(8,128)S(1)}, u32[]{:S(2)}, u32[]{:S(2)}) collective-permute-start(f32[2,128,512]{2,1,0:T(8,128)} %get-tuple-element.33), channel_id=1, source_target_pairs={{0,64},{64,128},{128,192},{1,65},{65,129},{129,193},{2,66},{66,130... | collective-permute-start | bytes 1572872 | tf_op jit(solution)/shard_map/ppermute | solution.py:386
  59.8 0.0 collective-permute-done.3.left_top
  59.8 7.3 %all-to-all-start = ((f32[32,16,128]{2,1,0:T(8,128)}), f32[32,16,128]{2,1,0:T(8,128)S(1)}, u32[]{:S(2)}, u32[]{:S(2)}) async-start(f32[32,16,128]{2,1,0:T(8,128)} %bitcast.11), calls=%async_computation | async-start | bytes 524288 | tf_op jit(solution)/shard_map/all_to_all | solution.py:388
  67.1 3.9 %collective-permute-start.4 = (f32[2,128,128]{2,1,0:T(8,128)}, f32[2,128,128]{2,1,0:T(8,128)S(1)}, u32[]{:S(2)}, u32[]{:S(2)}) collective-permute-start(f32[2,128,128]{2,1,0:T(8,128)} %get-tuple-element.31), channel_id=1, source_target_pairs={{0,1},{1,2},{2,3},{3,4},{4,5},{5,6},{6,7},{7,8},{8,9},{9,10},{10,1... | collective-permute-start | bytes 393224 | tf_op jit(solution)/shard_map/ppermute | solution.py:390
  70.9 5.6 %all-to-all-done = f32[32,16,128]{2,1,0:T(8,128)S(1)} async-done(((f32[32,16,128]{2,1,0:T(8,128)}), f32[32,16,128]{2,1,0:T(8,128)S(1)}, u32[]{:S(2)}, u32[]{:S(2)}) %all-to-all-start) | async-done | bytes 262176 | tf_op jit(solution)/shard_map/all_to_all | solution.py:388
  76.5 0.0 collective-permute-done.4.left_bottom
  76.5 14.6 %all_to_all.15 = f32[8,16,128]{2,1,0:T(8,128)S(1)} all-to-all(f32[8,16,128]{2,1,0:T(8,128)S(1)} %broadcast_in_dim.4), channel_id=1, replica_groups=mesh['z_hi'=4,'x'=4,'y'=4,'z_lo'=2,'core'=2] {'z_hi','z_lo'}, dimensions={0} | all-to-all | bytes 131072 | tf_op jit(solution)/shard_map/all_to_all | solution.py:299
  91.1 0.0 collective-permute-done.5.above
  91.1 0.7 broadcast_in_dim.5
  91.9 9.7 %all-to-all-start.2 = ((f32[32,16,128]{2,1,0:T(8,128)}), f32[32,16,128]{2,1,0:T(8,128)S(1)}, u32[]{:S(2)}, u32[]{:S(2)}) async-start(f32[32,16,128]{2,1,0:T(8,128)} %broadcast_in_dim.5), calls=%async_computation.2 | async-start | bytes 524288 | tf_op jit(solution)/shard_map/all_to_all | solution.py:299
  101.6 2.2 %collective-permute-start.6 = (f32[2,128,128]{2,1,0:T(8,128)}, f32[2,128,128]{2,1,0:T(8,128)S(1)}, u32[]{:S(2)}, u32[]{:S(2)}) collective-permute-start(f32[2,128,128]{2,1,0:T(8,128)} %get-tuple-element.38), channel_id=1, source_target_pairs={{0,65},{1,66},{2,67},{3,68},{4,69},{5,70},{6,71},{7,72},{8,73},{9,... | collective-permute-start | bytes 393224 | tf_op jit(solution)/shard_map/ppermute | solution.py:394
  103.8 3.3 %collective-permute-done.6.corner = f32[2,128,128]{2,1,0:T(8,128)S(1)} collective-permute-done((f32[2,128,128]{2,1,0:T(8,128)}, f32[2,128,128]{2,1,0:T(8,128)S(1)}, u32[]{:S(2)}, u32[]{:S(2)}) %collective-permute-start.6) | collective-permute-done | bytes 131104 | tf_op jit(solution)/shard_map/ppermute | solution.py:394
  107.0 3.6 %all-to-all-done.2.parts = f32[32,16,128]{2,1,0:T(8,128)S(1)} async-done(((f32[32,16,128]{2,1,0:T(8,128)}), f32[32,16,128]{2,1,0:T(8,128)S(1)}, u32[]{:S(2)}, u32[]{:S(2)}) %all-to-all-start.2) | async-done | bytes 262176 | tf_op jit(solution)/shard_map/all_to_all | solution.py:299
  110.6 2.2 %seams.1 = (f32[2,512,512]{2,1,0:T(8,128)}, f32[32,16,128]{2,1,0:T(8,128)}) custom-call(f32[2,512,512]{2,1,0:T(8,128)} %get-tuple-element.27.grad_in, f32[2,128,512]{2,1,0:T(8,128)S(1)} %collective-permute-done.5.above, f32[2,384,128]{2,1,0:T(8,128)S(1)} %collective-permute-done.3.left_top, ...), custom_call_target="tpu_custom_call", output_to_operand_aliasing={{0}: (0, {})} | custom-call | flops 1000000000 | bytes 1048576 | tf_op jit(solution)/shard_map/seams/pallas_call | solution.py:397
  (3 shorter events, 0.1 us)
Async XLA Ops:
  2.5 12.0 %collective-permute-start = (f32[2,512,128]{2,1,0:T(8,128)}, f32[2,512,128]{2,1,0:T(8,128)S(1)}, u32[]{:S(2)}, u32[]{:S(2)}) collective-permute-start(f32[2,512,128]{2,1,0:T(8,128)} %right_rim.1.after), channel_id=1, source_target_pairs={{1,0},{2,1},{3,2},{4,3},{5,4},{6,5},{7,6},{8,7},{9,8},{10,9},{11,1... | collective-permute-start | bytes 1572872 | tf_op jit(solution)/shard_map/ppermute | solution.py:343
  9.6 36.3 %collective-permute-start.1 = (f32[2,128,512]{2,1,0:T(8,128)}, f32[2,128,512]{2,1,0:T(8,128)}, u32[]{:S(2)}, u32[]{:S(2)}) collective-permute-start(f32[2,128,512]{2,1,0:T(8,128)} %get-tuple-element.22), channel_id=1, source_target_pairs={{64,0},{128,64},{192,128},{65,1},{129,65},{193,129},{66,2},{130,66... | collective-permute-start | bytes 1572872 | tf_op jit(solution)/shard_map/ppermute | solution.py:342
  10.9 35.0 %collective-permute-start.2 = (f32[2,128,128]{2,1,0:T(8,128)}, f32[2,128,128]{2,1,0:T(8,128)}, u32[]{:S(2)}, u32[]{:S(2)}) collective-permute-start(f32[2,128,128]{2,1,0:T(8,128)} %get-tuple-element.23), channel_id=1, source_target_pairs={{65,0},{66,1},{67,2},{68,3},{69,4},{70,5},{71,6},{72,7},{73,8},{74... | collective-permute-start | bytes 393224 | tf_op jit(solution)/shard_map/ppermute | solution.py:344
  14.5 0.8 copy-start
  26.3 33.5 %collective-permute-start.3 = (f32[2,384,128]{2,1,0:T(8,128)}, f32[2,384,128]{2,1,0:T(8,128)S(1)}, u32[]{:S(2)}, u32[]{:S(2)}) collective-permute-start(f32[2,384,128]{2,1,0:T(8,128)} %get-tuple-element.29), channel_id=1, source_target_pairs={{0,1},{1,2},{2,3},{3,4},{4,5},{5,6},{6,7},{7,8},{8,9},{9,10},{10,1... | collective-permute-start | bytes 1179656 | tf_op jit(solution)/shard_map/ppermute | solution.py:372
  52.5 38.6 %collective-permute-start.5 = (f32[2,128,512]{2,1,0:T(8,128)}, f32[2,128,512]{2,1,0:T(8,128)S(1)}, u32[]{:S(2)}, u32[]{:S(2)}) collective-permute-start(f32[2,128,512]{2,1,0:T(8,128)} %get-tuple-element.33), channel_id=1, source_target_pairs={{0,64},{64,128},{128,192},{1,65},{65,129},{129,193},{2,66},{66,130... | collective-permute-start | bytes 1572872 | tf_op jit(solution)/shard_map/ppermute | solution.py:386
  59.8 16.7 %all-to-all-start = ((f32[32,16,128]{2,1,0:T(8,128)}), f32[32,16,128]{2,1,0:T(8,128)S(1)}, u32[]{:S(2)}, u32[]{:S(2)}) async-start(f32[32,16,128]{2,1,0:T(8,128)} %bitcast.11), calls=%async_computation | async-start | bytes 524288 | tf_op jit(solution)/shard_map/all_to_all | solution.py:388
  67.1 9.5 %collective-permute-start.4 = (f32[2,128,128]{2,1,0:T(8,128)}, f32[2,128,128]{2,1,0:T(8,128)S(1)}, u32[]{:S(2)}, u32[]{:S(2)}) collective-permute-start(f32[2,128,128]{2,1,0:T(8,128)} %get-tuple-element.31), channel_id=1, source_target_pairs={{0,1},{1,2},{2,3},{3,4},{4,5},{5,6},{6,7},{7,8},{8,9},{9,10},{10,1... | collective-permute-start | bytes 393224 | tf_op jit(solution)/shard_map/ppermute | solution.py:390
  91.9 18.7 %all-to-all-start.2 = ((f32[32,16,128]{2,1,0:T(8,128)}), f32[32,16,128]{2,1,0:T(8,128)S(1)}, u32[]{:S(2)}, u32[]{:S(2)}) async-start(f32[32,16,128]{2,1,0:T(8,128)} %broadcast_in_dim.5), calls=%async_computation.2 | async-start | bytes 524288 | tf_op jit(solution)/shard_map/all_to_all | solution.py:299
  101.6 5.4 %collective-permute-start.6 = (f32[2,128,128]{2,1,0:T(8,128)}, f32[2,128,128]{2,1,0:T(8,128)S(1)}, u32[]{:S(2)}, u32[]{:S(2)}) collective-permute-start(f32[2,128,128]{2,1,0:T(8,128)} %get-tuple-element.38), channel_id=1, source_target_pairs={{0,65},{1,66},{2,67},{3,68},{4,69},{5,70},{6,71},{7,72},{8,73},{9,... | collective-permute-start | bytes 393224 | tf_op jit(solution)/shard_map/ppermute | solution.py:394

commit v8 on v6

--- a/solution.py
+++ b/solution.py
@@ -389,8 +389,8 @@
     share = jnp.sum(shares, axis=0)
     share = jnp.sum(everyone(share, DEPTH, depth), axis=0)
     share, above, g_bottom, g_corner = lax.optimization_barrier((share, above, g_bottom, g_corner))
+    from_corner = lax.ppermute(g_corner, BOTH, diagonal)
     left_bottom = lax.ppermute(g_bottom, COL, along)
-    from_corner = lax.ppermute(g_corner, BOTH, diagonal)
     parts = everyone(share, PLANE, plane)
 
     object_gradient, probe_gradient = pl.pallas_call(

time: 108 us -> 107 us (level)
  blocking collectives: 28.8 us -> 26.4 us
  waiting for transfers between devices: 13.8 us -> 15.9 us
    pallas_call x1, Pallas kernels: 6.66 us -> 9.01 us  [body(): pl.pallas_call(functools.partial(lower_kernel, scale), out_shape=(own_sha...]
    all_to_all x1, blocking collectives: 17.6 us -> 15.3 us  [body(): lax.all_to_all(probe_2.reshape(plane, -1, PATCH), PLANE, 0, 0, tiled=True)]
    pallas_call x1, Pallas kernels: 15.7 us -> 14.4 us  [body(): pl.pallas_call(upper_kernel, out_shape=(own_shape, shape(2, rows - PATCH,...]
    ppermute x1, waiting for transfers between devices: 3.46 us -> 4.78 us  [body(): corner = lax.ppermute(corner, BOTH, diagonal_back)]
  transfers between devices with their start and end apart: 8 -> 8, of which waited for: 5 -> 5; matrix products, arithmetic and copies ran while one was open for 0% -> 0% of each run, Pallas kernels for 23% -> 24%
where the time goes in v8:
time: 107 us; the launch traced here: 106 us
  starting transfers between devices  31.5 us (29%)
  Pallas kernels  29.4 us (27%)
  blocking collectives  26.4 us (25%)
  waiting for transfers between devices  15.9 us (15%)
  local copies, waits for them, and re-layouts  1.53 us (1%)
  between operations  1.41 us (1%)
    all_to_all x1, blocking collectives, body(): lax.all_to_all(probe_2.reshape(plane, -1, PATCH), PLANE, 0, 0, tiled=True)  15.3 us
    pallas_call x1, Pallas kernels, body(): pl.pallas_call(upper_kernel, out_shape=(own_shape, shape(2, rows - PATCH,...  14.4 us
    all_to_all x1, blocking collectives, everyone(): return lax.all_to_all(sent, axes, 0, 0, tiled=True)  11.1 us
    pallas_call x1, Pallas kernels, body(): pl.pallas_call(functools.partial(lower_kernel, scale), out_shape=(own_sha...  9.01 us
    ppermute x1, starting transfers between devices, body(): above = lax.ppermute(g_below, ROW, down)  6.78 us
    ppermute x1, waiting for transfers between devices, body(): from_corner = lax.ppermute(g_corner, BOTH, diagonal)  6.62 us
    ppermute x1, starting transfers between devices, body(): right = lax.ppermute(right, COL, back)  5.98 us
    all_to_all x1, starting transfers between devices, everyone(): return lax.all_to_all(sent, axes, 0, 0, tiled=True)  5.85 us
  transfers between devices with their start and end apart: 8, of which 5 were waited for; matrix products, arithmetic and copies ran while one was open for 0% of the time, Pallas kernels for 24%

profile of v8, /device:TPU:70, one launch (start us, length us, event | category | flops | bytes accessed | tf_op | source)
XLA Modules:
  0.0 106.2 jit_solution(467039038239396760)
XLA Ops:
  0.6 1.8 %right_rim.1.after = f32[2,512,128]{2,1,0:T(8,128)} custom-call(f32[2,512,512]{2,1,0:T(8,128)} %own.7), custom_call_target="tpu_custom_call" | custom-call | tf_op jit(solution)/shard_map/right_rim/pallas_call | solution.py:324
  2.5 6.0 %collective-permute-start = (f32[2,512,128]{2,1,0:T(8,128)}, f32[2,512,128]{2,1,0:T(8,128)S(1)}, u32[]{:S(2)}, u32[]{:S(2)}) collective-permute-start(f32[2,512,128]{2,1,0:T(8,128)} %right_rim.1.after), channel_id=1, source_target_pairs={{1,0},{2,1},{3,2},{4,3},{5,4},{6,5},{7,6},{8,7},{9,8},{10,9},{11,1... | collective-permute-start | bytes 1572872 | tf_op jit(solution)/shard_map/ppermute | solution.py:343
  8.5 1.9 %below_rim.1 = (f32[2,128,512]{2,1,0:T(8,128)}, f32[2,128,128]{2,1,0:T(8,128)}) custom-call(f32[2,512,512]{2,1,0:T(8,128)} %own.7, f32[2,512,128]{2,1,0:T(8,128)} %right_rim.1.after), custom_call_target="tpu_custom_call" | custom-call | tf_op jit(solution)/shard_map/below_rim/pallas_call | solution.py:333
  10.4 1.9 %collective-permute-start.1 = (f32[2,128,512]{2,1,0:T(8,128)}, f32[2,128,512]{2,1,0:T(8,128)}, u32[]{:S(2)}, u32[]{:S(2)}) collective-permute-start(f32[2,128,512]{2,1,0:T(8,128)} %get-tuple-element.21), channel_id=1, source_target_pairs={{64,0},{128,64},{192,128},{65,1},{129,65},{193,129},{66,2},{130,66... | collective-permute-start | bytes 1572872 | tf_op jit(solution)/shard_map/ppermute | solution.py:342
  12.3 1.9 %collective-permute-start.2 = (f32[2,128,128]{2,1,0:T(8,128)}, f32[2,128,128]{2,1,0:T(8,128)}, u32[]{:S(2)}, u32[]{:S(2)}) collective-permute-start(f32[2,128,128]{2,1,0:T(8,128)} %get-tuple-element.22), channel_id=1, source_target_pairs={{65,0},{66,1},{67,2},{68,3},{69,4},{70,5},{71,6},{72,7},{73,8},{74... | collective-permute-start | bytes 393224 | tf_op jit(solution)/shard_map/ppermute | solution.py:344
  14.9 0.6 collective-permute-done.right
  15.5 0.0 copy-start
  15.5 0.8 copy-done
  16.3 14.4 %upper_slots.1 = (f32[2,512,512]{2,1,0:T(8,128)}, f32[2,384,128]{2,1,0:T(8,128)}, f32[2,128,128]{2,1,0:T(8,128)}, f32[2,2,128,128]{3,2,1,0:T(8,128)}) custom-call(s32[2,64]{1,0:T(2,128)} %bitcast.12, s32[1]{0:T(128)} %bitcast.7.count, f32[2,512,512]{2,1,0:T(8,128)} %own.7, f32[2,512,128]{2,1,0:T(8,128)} %copy-done, bf16[64,128,128]{2,1,0:T(8,128)(2,1)} %bitcast.9, ...), custom_call_target="tpu_custom_call" | custom-call | flops 1000000000 | bytes 1048576 | tf_op jit(solution)/shard_map/upper_slots/pallas_call | solution.py:362
  30.7 1.9 %collective-permute-start.3 = (f32[2,384,128]{2,1,0:T(8,128)}, f32[2,384,128]{2,1,0:T(8,128)S(1)}, u32[]{:S(2)}, u32[]{:S(2)}) collective-permute-start(f32[2,384,128]{2,1,0:T(8,128)} %get-tuple-element.28), channel_id=1, source_target_pairs={{0,1},{1,2},{2,3},{3,4},{4,5},{5,6},{6,7},{7,8},{8,9},{9,10},{10,1... | collective-permute-start | bytes 1179656 | tf_op jit(solution)/shard_map/ppermute | solution.py:372
  32.6 4.8 %collective-permute-done.2.corner = f32[2,128,128]{2,1,0:T(8,128)} collective-permute-done((f32[2,128,128]{2,1,0:T(8,128)}, f32[2,128,128]{2,1,0:T(8,128)}, u32[]{:S(2)}, u32[]{:S(2)}) %collective-permute-start.2) | collective-permute-done | bytes 131104 | tf_op jit(solution)/shard_map/ppermute | solution.py:344
  37.4 1.6 %collective-permute-done.1.below = f32[2,128,512]{2,1,0:T(8,128)} collective-permute-done((f32[2,128,512]{2,1,0:T(8,128)}, f32[2,128,512]{2,1,0:T(8,128)}, u32[]{:S(2)}, u32[]{:S(2)}) %collective-permute-start.1) | collective-permute-done | bytes 524320 | tf_op jit(solution)/shard_map/ppermute | solution.py:342
  38.9 9.0 %lower_slots.1 = (f32[2,512,512]{2,1,0:T(8,128)}, f32[2,128,128]{2,1,0:T(8,128)}, f32[2,128,512]{2,1,0:T(8,128)}, f32[2,128,128]{2,1,0:T(8,128)}, f32[2,2,128,128]{3,2,1,0:T(8,128)}) custom-call(s32[2,64]{1,0:T(2,128)} %bitcast.13, s32[1]{0:T(128)} %bitcast.8.count, f32[2,512,512]{2,1,0:T(8,128)} %own.7, ...), custom_call_target="tpu_custom_call", output_to_operand_aliasing={{0}: (9, {}), {1}: (10, {})} | custom-call | flops 20000000000 | bytes 1048576 | tf_op jit(solution)/shard_map/lower_slots/pallas_call | solution.py:373
  48.0 6.8 %collective-permute-start.4 = (f32[2,128,512]{2,1,0:T(8,128)}, f32[2,128,512]{2,1,0:T(8,128)S(1)}, u32[]{:S(2)}, u32[]{:S(2)}) collective-permute-start(f32[2,128,512]{2,1,0:T(8,128)} %get-tuple-element.30), channel_id=1, source_target_pairs={{0,64},{64,128},{128,192},{1,65},{65,129},{129,193},{2,66},{66,130... | collective-permute-start | bytes 1572872 | tf_op jit(solution)/shard_map/ppermute | solution.py:386
  54.8 0.0 collective-permute-done.3.left_top
  54.8 15.3 %all_to_all.15 = f32[32,16,128]{2,1,0:T(8,128)S(1)} all-to-all(f32[32,16,128]{2,1,0:T(8,128)} %bitcast.11), channel_id=1, replica_groups=mesh['z_hi'=4,'x'=4,'y'=4,'z_lo'=2,'core'=2] {'x','y','core'}, dimensions={0} | all-to-all | bytes 524288 | tf_op jit(solution)/shard_map/all_to_all | solution.py:388
  70.1 11.1 %all_to_all.16 = f32[8,16,128]{2,1,0:T(8,128)S(1)} all-to-all(f32[8,16,128]{2,1,0:T(8,128)S(1)} %broadcast_in_dim.4), channel_id=1, replica_groups=mesh['z_hi'=4,'x'=4,'y'=4,'z_lo'=2,'core'=2] {'z_hi','z_lo'}, dimensions={0} | all-to-all | bytes 131072 | tf_op jit(solution)/shard_map/all_to_all | solution.py:299
  81.2 0.0 collective-permute-done.4.above
  81.3 0.7 broadcast_in_dim.5
  82.0 5.8 %all-to-all-start.2 = ((f32[32,16,128]{2,1,0:T(8,128)}), f32[32,16,128]{2,1,0:T(8,128)S(1)}, u32[]{:S(2)}, u32[]{:S(2)}) async-start(f32[32,16,128]{2,1,0:T(8,128)} %broadcast_in_dim.5), calls=%async_computation.2 | async-start | bytes 524288 | tf_op jit(solution)/shard_map/all_to_all | solution.py:299
  87.8 2.1 %collective-permute-start.5 = (f32[2,128,128]{2,1,0:T(8,128)}, f32[2,128,128]{2,1,0:T(8,128)S(1)}, u32[]{:S(2)}, u32[]{:S(2)}) collective-permute-start(f32[2,128,128]{2,1,0:T(8,128)} %get-tuple-element.35), channel_id=1, source_target_pairs={{0,1},{1,2},{2,3},{3,4},{4,5},{5,6},{6,7},{7,8},{8,9},{9,10},{10,1... | collective-permute-start | bytes 393224 | tf_op jit(solution)/shard_map/ppermute | solution.py:393
  89.9 5.1 %collective-permute-start.6 = (f32[2,128,128]{2,1,0:T(8,128)}, f32[2,128,128]{2,1,0:T(8,128)S(1)}, u32[]{:S(2)}, u32[]{:S(2)}) collective-permute-start(f32[2,128,128]{2,1,0:T(8,128)} %get-tuple-element.36), channel_id=1, source_target_pairs={{0,65},{1,66},{2,67},{3,68},{4,69},{5,70},{6,71},{7,72},{8,73},{9,... | collective-permute-start | bytes 393224 | tf_op jit(solution)/shard_map/ppermute | solution.py:392
  95.0 2.3 %collective-permute-done.5.left_bottom = f32[2,128,128]{2,1,0:T(8,128)S(1)} collective-permute-done((f32[2,128,128]{2,1,0:T(8,128)}, f32[2,128,128]{2,1,0:T(8,128)S(1)}, u32[]{:S(2)}, u32[]{:S(2)}) %collective-permute-start.5) | collective-permute-done | bytes 131104 | tf_op jit(solution)/shard_map/ppermute | solution.py:393
  97.3 6.6 %collective-permute-done.6.corner = f32[2,128,128]{2,1,0:T(8,128)S(1)} collective-permute-done((f32[2,128,128]{2,1,0:T(8,128)}, f32[2,128,128]{2,1,0:T(8,128)S(1)}, u32[]{:S(2)}, u32[]{:S(2)}) %collective-permute-start.6) | collective-permute-done | bytes 131104 | tf_op jit(solution)/shard_map/ppermute | solution.py:392
  104.0 0.0 all-to-all-done.2.parts
  104.0 2.2 %seams.1 = (f32[2,512,512]{2,1,0:T(8,128)}, f32[32,16,128]{2,1,0:T(8,128)}) custom-call(f32[2,512,512]{2,1,0:T(8,128)} %get-tuple-element.26.grad_in, f32[2,128,512]{2,1,0:T(8,128)S(1)} %collective-permute-done.4.above, f32[2,384,128]{2,1,0:T(8,128)S(1)} %collective-permute-done.3.left_top, ...), custom_call_target="tpu_custom_call", output_to_operand_aliasing={{0}: (0, {})} | custom-call | flops 1000000000 | bytes 1048576 | tf_op jit(solution)/shard_map/seams/pallas_call | solution.py:396
  (3 shorter events, 0.1 us)
Async XLA Ops:
  2.5 13.0 %collective-permute-start = (f32[2,512,128]{2,1,0:T(8,128)}, f32[2,512,128]{2,1,0:T(8,128)S(1)}, u32[]{:S(2)}, u32[]{:S(2)}) collective-permute-start(f32[2,512,128]{2,1,0:T(8,128)} %right_rim.1.after), channel_id=1, source_target_pairs={{1,0},{2,1},{3,2},{4,3},{5,4},{6,5},{7,6},{8,7},{9,8},{10,9},{11,1... | collective-permute-start | bytes 1572872 | tf_op jit(solution)/shard_map/ppermute | solution.py:343
  10.4 28.6 %collective-permute-start.1 = (f32[2,128,512]{2,1,0:T(8,128)}, f32[2,128,512]{2,1,0:T(8,128)}, u32[]{:S(2)}, u32[]{:S(2)}) collective-permute-start(f32[2,128,512]{2,1,0:T(8,128)} %get-tuple-element.21), channel_id=1, source_target_pairs={{64,0},{128,64},{192,128},{65,1},{129,65},{193,129},{66,2},{130,66... | collective-permute-start | bytes 1572872 | tf_op jit(solution)/shard_map/ppermute | solution.py:342
  12.3 25.0 %collective-permute-start.2 = (f32[2,128,128]{2,1,0:T(8,128)}, f32[2,128,128]{2,1,0:T(8,128)}, u32[]{:S(2)}, u32[]{:S(2)}) collective-permute-start(f32[2,128,128]{2,1,0:T(8,128)} %get-tuple-element.22), channel_id=1, source_target_pairs={{65,0},{66,1},{67,2},{68,3},{69,4},{70,5},{71,6},{72,7},{73,8},{74... | collective-permute-start | bytes 393224 | tf_op jit(solution)/shard_map/ppermute | solution.py:344
  15.5 0.8 copy-start
  30.7 24.1 %collective-permute-start.3 = (f32[2,384,128]{2,1,0:T(8,128)}, f32[2,384,128]{2,1,0:T(8,128)S(1)}, u32[]{:S(2)}, u32[]{:S(2)}) collective-permute-start(f32[2,384,128]{2,1,0:T(8,128)} %get-tuple-element.28), channel_id=1, source_target_pairs={{0,1},{1,2},{2,3},{3,4},{4,5},{5,6},{6,7},{7,8},{8,9},{9,10},{10,1... | collective-permute-start | bytes 1179656 | tf_op jit(solution)/shard_map/ppermute | solution.py:372
  48.0 33.3 %collective-permute-start.4 = (f32[2,128,512]{2,1,0:T(8,128)}, f32[2,128,512]{2,1,0:T(8,128)S(1)}, u32[]{:S(2)}, u32[]{:S(2)}) collective-permute-start(f32[2,128,512]{2,1,0:T(8,128)} %get-tuple-element.30), channel_id=1, source_target_pairs={{0,64},{64,128},{128,192},{1,65},{65,129},{129,193},{2,66},{66,130... | collective-permute-start | bytes 1572872 | tf_op jit(solution)/shard_map/ppermute | solution.py:386
  82.0 22.0 %all-to-all-start.2 = ((f32[32,16,128]{2,1,0:T(8,128)}), f32[32,16,128]{2,1,0:T(8,128)S(1)}, u32[]{:S(2)}, u32[]{:S(2)}) async-start(f32[32,16,128]{2,1,0:T(8,128)} %broadcast_in_dim.5), calls=%async_computation.2 | async-start | bytes 524288 | tf_op jit(solution)/shard_map/all_to_all | solution.py:299
  87.8 9.5 %collective-permute-start.5 = (f32[2,128,128]{2,1,0:T(8,128)}, f32[2,128,128]{2,1,0:T(8,128)S(1)}, u32[]{:S(2)}, u32[]{:S(2)}) collective-permute-start(f32[2,128,128]{2,1,0:T(8,128)} %get-tuple-element.35), channel_id=1, source_target_pairs={{0,1},{1,2},{2,3},{3,4},{4,5},{5,6},{6,7},{7,8},{8,9},{9,10},{10,1... | collective-permute-start | bytes 393224 | tf_op jit(solution)/shard_map/ppermute | solution.py:393
  89.9 14.1 %collective-permute-start.6 = (f32[2,128,128]{2,1,0:T(8,128)}, f32[2,128,128]{2,1,0:T(8,128)S(1)}, u32[]{:S(2)}, u32[]{:S(2)}) collective-permute-start(f32[2,128,128]{2,1,0:T(8,128)} %get-tuple-element.36), channel_id=1, source_target_pairs={{0,65},{1,66},{2,67},{3,68},{4,69},{5,70},{6,71},{7,72},{8,73},{9,... | collective-permute-start | bytes 393224 | tf_op jit(solution)/shard_map/ppermute | solution.py:392
